TPU v7x, 32 devices: a whole 2x2x4 slice. The times are simulated.
32 devices in a mesh: rows: 32 (over z, y, x, core).
Axes of the slice: x: 2, y: 2, z: 4, core: 2. Of those that a mesh axis runs over, the one named last changes fastest.
Arguments:
- signal: bfloat16 [32768, 256], P('rows'), may hold values from -6 to 6
- leaves: bfloat16 [32768, 512], P('rows'), may hold values from -0.25 to 0.25
- bases: bfloat16 [4, 32768, 128], P(None, 'rows'), may hold values from -6 to 6
- couplings: bfloat16 [15, 128, 128], replicated, may hold values from -0.5 to 0.5
- weights: float32 [32768], P('rows'), may hold values from 0.25 to 4
Outputs:
- result: bfloat16 [32768, 256], P('rows')
All inputs are finite; a program needn't handle non-finite values.
Results may differ from a plain program's by a relative error of at most 0.007.
Values sent between devices are 32-bit elements; how exact they have to be, the bound alone decides.
No kernel may reach another device: no remote copies, remote signals or barrier semaphores. Data moves between devices by JAX's collectives and lax.ppermute only.
A program may use at most 64 MiB of HBM per device.

v0:
```python
import math

import jax
import jax.numpy as jnp
from jax import lax
from jax.sharding import PartitionSpec as P

LEAF = 512


def partner(value, axis, apart):
    mask = 2**apart
    pairs = [(source, source ^ mask) for source in range(lax.axis_size(axis))]
    return lax.ppermute(value, axis, pairs)


def on_device(signal, leaves, bases, couplings, weights):
    count = lax.axis_size("rows")
    bits = count.bit_length() - 1
    myself = lax.axis_index("rows")
    rows_dev = signal.shape[0]
    width = signal.shape[1]
    rank = bases.shape[2]
    levels = bases.shape[0]

    def sums_doubling(proj):
        totals = proj
        siblings = [None] * levels
        for step in range(bits):
            active = min(levels, bits - step)
            keeping = min(levels, bits - step - 1)
            got = partner(totals, "rows", step)
            if active > keeping:
                siblings[active - 1] = got[active - 1]
            totals = totals[:keeping] + got[:keeping]
        return siblings

    def apply_kernel(vec):
        nleaf = rows_dev // LEAF
        result = jnp.einsum(
            "lab,lbc->lac",
            leaves.reshape(nleaf, LEAF, LEAF),
            vec.reshape(nleaf, LEAF, width),
            preferred_element_type=jnp.float32,
        ).reshape(rows_dev, width)
        proj = jnp.einsum("lrk,rc->lkc", bases, vec, preferred_element_type=jnp.float32)
        siblings = sums_doubling(proj)
        for level in range(levels):
            level_bit = bits - level - 1
            side = myself >> level_bit & 1
            pair_idx = myself >> level_bit + 1
            size = rows_dev * (count >> level + 1)
            factor = 1.0 / math.sqrt(size * rank)
            quotient = (siblings[level] * factor).astype(jnp.bfloat16)
            coupling = lax.dynamic_index_in_dim(
                couplings, (1 << level) - 1 + pair_idx, 0, keepdims=False
            )
            oriented = jnp.where(side == 0, coupling, coupling.T)
            coeffs = jnp.dot(oriented, quotient, preferred_element_type=jnp.float32).astype(
                jnp.bfloat16
            )
            result = result + jnp.dot(bases[level], coeffs, preferred_element_type=jnp.float32)
        return result

    first = apply_kernel(signal)
    scaled = (weights[:, None] * first).astype(jnp.bfloat16)
    return apply_kernel(scaled).astype(jnp.bfloat16)


def solution(mesh):
    in_specs = (P("rows", None), P("rows", None), P(None, "rows", None), P(), P("rows"))
    out_specs = P("rows", None)
    return jax.shard_map(
        on_device, mesh=mesh, in_specs=in_specs, out_specs=out_specs, check_vma=False
    )
```

profile of v0, /device:TPU:0, one launch (start us, length us, event | category | flops | bytes accessed | tf_op | source)
XLA Modules:
  0.0 99.7 jit_solution(8566120922418657427)
XLA Ops:
  0.0 1.9 %fusion.14 = f32[4,128,256]{2,1,0:T(8,128)S(1)} fusion(bf16[4,1024,128]{2,1,0:T(8,128)(2,1)} %param.7, bf16[1024,256]{1,0:T(8,128)(2,1)} %param.5), kind=kOutput, calls=%fused_computation.32 | convolution fusion | flops 268435456 | bytes 2097152 | tf_op jit(solution)/shard_map/lrk,rc->lkc/dot_general | solution.py:46
  4.1 2.9 %collective-permute-start.1 = (f32[4,128,256]{2,1,0:T(8,128)S(1)}, f32[4,128,256]{2,1,0:T(8,128)S(1)}, u32[]{:S(2)}, u32[]{:S(2)}) collective-permute-start(f32[4,128,256]{2,1,0:T(8,128)S(1)} %add.84), channel_id=1, source_target_pairs={{0,2},{1,3},{2,0},{3,1},{4,6},{5,7},{6,4},{7,5},{8,10},{9,11},{10,... | collective-permute-start | bytes 1572872 | tf_op jit(solution)/shard_map/ppermute | solution.py:14
  7.0 12.2 %collective-permute-done.1 = f32[4,128,256]{2,1,0:T(8,128)S(1)} collective-permute-done((f32[4,128,256]{2,1,0:T(8,128)S(1)}, f32[4,128,256]{2,1,0:T(8,128)S(1)}, u32[]{:S(2)}, u32[]{:S(2)}) %collective-permute-start.1) | collective-permute-done | bytes 524320 | tf_op jit(solution)/shard_map/ppermute | solution.py:14
  20.0 1.8 %collective-permute-start.2 = (f32[3,128,256]{2,1,0:T(8,128)S(1)}, f32[3,128,256]{2,1,0:T(8,128)}, u32[]{:S(2)}, u32[]{:S(2)}) collective-permute-start(f32[3,128,256]{2,1,0:T(8,128)S(1)} %slice_add_fusion.1), channel_id=1, source_target_pairs={{0,4},{1,5},{2,6},{3,7},{4,0},{5,1},{6,2},{7,3},{8,12},{9,13},{10,... | collective-permute-start | bytes 1179656 | tf_op jit(solution)/shard_map/ppermute | solution.py:14
  27.3 2.4 %convolution_bitcast_fusion.4 = f32[1024,256]{0,1:T(8,128)} fusion(bf16[4,1024,128]{2,1,0:T(8,128)(2,1)S(1)} %copy-done.1, f32[4,128,256]{2,1,0:T(8,128)} %copy-done.14, bf16[128,128]{1,0:T(8,128)(2,1)} %copy-done.13, bf16[128,128]{0,1:T(8,128)(2,1)} %copy.20, pred[]{:T(512)S(6)} %eq.19), kind=kOutput, calls=%fused_computation.4 | convolution fusion | flops 75612160 | bytes 1507329 | tf_op jit(solution)/shard_map/dot_general | solution.py:62
  31.7 1.6 %collective-permute-start.3 = (f32[2,128,256]{2,1,0:T(8,128)S(1)}, f32[2,128,256]{2,1,0:T(8,128)S(1)}, u32[]{:S(2)}, u32[]{:S(2)}) collective-permute-start(f32[2,128,256]{2,1,0:T(8,128)S(1)} %slice_add_fusion.3), channel_id=1, source_target_pairs={{0,8},{1,9},{2,10},{3,11},{4,12},{5,13},{6,14},{7,15},{8,0},{9,1},... | collective-permute-start | bytes 786440 | tf_op jit(solution)/shard_map/ppermute | solution.py:14
  33.3 2.4 %convolution_bitcast_fusion.5 = f32[1024,256]{0,1:T(8,128)} fusion(bf16[4,1024,128]{2,1,0:T(8,128)(2,1)S(1)} %copy-done.1, f32[3,128,256]{2,1,0:T(8,128)} %collective-permute-done.2, bf16[128,128]{1,0:T(8,128)(2,1)S(1)} %copy-done.11, bf16[128,128]{0,1:T(8,128)(2,1)S(1)} %copy-done.20, pred[]{:T(512)S(6)} %eq.18), kind=kOutput, calls=%fused_computation.5 | convolution fusion | flops 75612160 | bytes 1507329 | tf_op jit(solution)/shard_map/dot_general | solution.py:62
  35.7 3.1 %collective-permute-done.3 = f32[2,128,256]{2,1,0:T(8,128)S(1)} collective-permute-done((f32[2,128,256]{2,1,0:T(8,128)S(1)}, f32[2,128,256]{2,1,0:T(8,128)S(1)}, u32[]{:S(2)}, u32[]{:S(2)}) %collective-permute-start.3) | collective-permute-done | bytes 262176 | tf_op jit(solution)/shard_map/ppermute | solution.py:14
  38.8 2.2 %collective-permute-start.4 = (f32[1,128,256]{2,1,0:T(8,128)S(1)}, f32[1,128,256]{2,1,0:T(8,128)S(1)}, u32[]{:S(2)}, u32[]{:S(2)}) collective-permute-start(f32[1,128,256]{2,1,0:T(8,128)S(1)} %slice_add_fusion.5), channel_id=1, source_target_pairs={{0,16},{1,17},{2,18},{3,19},{4,20},{5,21},{6,22},{7,23},{8,24},{9,... | collective-permute-start | bytes 393224 | tf_op jit(solution)/shard_map/ppermute | solution.py:14
  42.5 3.6 %collective-permute-done.4 = f32[1,128,256]{2,1,0:T(8,128)S(1)} collective-permute-done((f32[1,128,256]{2,1,0:T(8,128)S(1)}, f32[1,128,256]{2,1,0:T(8,128)S(1)}, u32[]{:S(2)}, u32[]{:S(2)}) %collective-permute-start.4) | collective-permute-done | bytes 131104 | tf_op jit(solution)/shard_map/ppermute | solution.py:14
  46.2 2.7 %fusion.10 = bf16[1024,256]{0,1:T(8,128)(2,1)S(1)} fusion(f32[1024,256]{0,1:T(8,128)} %convolution_bitcast_fusion.4, f32[1024,256]{0,1:T(8,128)} %convolution_bitcast_fusion.5, f32[1024,256]{0,1:T(8,128)} %convolution_bitcast_fusion.6, f32[1024,256]{0,1:T(8,128)} %copy.17, f32[1024]{0:T(1024)S(1)} %copy-done.22, bf16[4,1024,128]{2,1,0:T(8,128)(2,1)S(1)} %copy-done.1, ...), kind=kOutput, calls=%fused_computation.19 | convolution fusion | flops 77185024 | bytes 5181441 | tf_op jit(solution)/shard_map/dot_general | solution.py:62
  49.5 1.9 %collective-permute-done.5 = f32[4,128,256]{2,1,0:T(8,128)S(1)} collective-permute-done((f32[4,128,256]{2,1,0:T(8,128)S(1)}, f32[4,128,256]{2,1,0:T(8,128)S(1)}, u32[]{:S(2)}, u32[]{:S(2)}) %collective-permute-start.5) | collective-permute-done | bytes 524320 | tf_op jit(solution)/shard_map/ppermute | solution.py:14
  52.6 12.9 %collective-permute-done.6 = f32[4,128,256]{2,1,0:T(8,128)S(1)} collective-permute-done((f32[4,128,256]{2,1,0:T(8,128)S(1)}, f32[4,128,256]{2,1,0:T(8,128)S(1)}, u32[]{:S(2)}, u32[]{:S(2)}) %collective-permute-start.6) | collective-permute-done | bytes 524320 | tf_op jit(solution)/shard_map/ppermute | solution.py:14
  68.8 1.6 %copy.22 = f32[2,512,256]{2,1,0:T(8,128)S(1)} copy(f32[2,512,256]{1,2,0:T(8,128)} %convolution_bitcast_fusion.8) | data formatting | bytes 2097152 | tf_op jit(solution)/shard_map/lab,lbc->lac/dot_general | solution.py:40
  71.7 2.4 %convolution_bitcast_fusion = f32[1024,256]{0,1:T(8,128)} fusion(bf16[4,1024,128]{2,1,0:T(8,128)(2,1)S(1)} %copy-done.1, f32[4,128,256]{2,1,0:T(8,128)} %copy-done.15, bf16[128,128]{1,0:T(8,128)(2,1)} %copy-done.13, bf16[128,128]{0,1:T(8,128)(2,1)} %copy.20, pred[]{:T(512)S(6)} %eq.19), kind=kOutput, calls=%fused_computation | convolution fusion | flops 75612160 | bytes 1507329 | tf_op jit(solution)/shard_map/dot_general | solution.py:62
  74.1 2.6 %collective-permute-done.7 = f32[3,128,256]{2,1,0:T(8,128)} collective-permute-done((f32[3,128,256]{2,1,0:T(8,128)S(1)}, f32[3,128,256]{2,1,0:T(8,128)}, u32[]{:S(2)}, u32[]{:S(2)}) %collective-permute-start.7) | collective-permute-done | bytes 393248 | tf_op jit(solution)/shard_map/ppermute | solution.py:14
  76.7 1.7 %slice_add_fusion.2 = f32[2,128,256]{2,1,0:T(8,128)} fusion(f32[3,128,256]{2,1,0:T(8,128)} %collective-permute-done.7, f32[3,128,256]{2,1,0:T(8,128)S(1)} %slice_add_fusion), kind=kLoop, calls=%fused_computation.36 | loop fusion | flops 65536 | bytes 786432 | tf_op jit(solution)/shard_map/add | solution.py:35
  78.7 2.4 %convolution_bitcast_fusion.1 = f32[1024,256]{0,1:T(8,128)} fusion(bf16[4,1024,128]{2,1,0:T(8,128)(2,1)S(1)} %copy-done.1, f32[3,128,256]{2,1,0:T(8,128)} %collective-permute-done.7, bf16[128,128]{1,0:T(8,128)(2,1)S(1)} %copy-done.12, bf16[128,128]{0,1:T(8,128)(2,1)S(1)} %copy-done.21, pred[]{:T(512)S(6)} %eq.18), kind=kOutput, calls=%fused_computation.1 | convolution fusion | flops 75612160 | bytes 1507329 | tf_op jit(solution)/shard_map/dot_general | solution.py:62
  81.1 4.2 %collective-permute-done.8 = f32[2,128,256]{2,1,0:T(8,128)S(1)} collective-permute-done((f32[2,128,256]{2,1,0:T(8,128)}, f32[2,128,256]{2,1,0:T(8,128)S(1)}, u32[]{:S(2)}, u32[]{:S(2)}) %collective-permute-start.8) | collective-permute-done | bytes 262176 | tf_op jit(solution)/shard_map/ppermute | solution.py:14
  85.2 1.6 %slice_add_fusion.4 = f32[1,128,256]{2,1,0:T(8,128)} fusion(f32[2,128,256]{2,1,0:T(8,128)S(1)} %collective-permute-done.8, f32[2,128,256]{2,1,0:T(8,128)} %slice_add_fusion.2), kind=kLoop, calls=%fused_computation.60 | loop fusion | flops 32768 | bytes 393216 | tf_op jit(solution)/shard_map/add | solution.py:35
  86.8 1.9 %collective-permute-start.9 = (f32[1,128,256]{2,1,0:T(8,128)}, f32[1,128,256]{2,1,0:T(8,128)}, u32[]{:S(2)}, u32[]{:S(2)}) collective-permute-start(f32[1,128,256]{2,1,0:T(8,128)} %slice_add_fusion.4), channel_id=1, source_target_pairs={{0,16},{1,17},{2,18},{3,19},{4,20},{5,21},{6,22},{7,23},{8,24},{9,... | collective-permute-start | bytes 393224 | tf_op jit(solution)/shard_map/ppermute | solution.py:14
  90.1 4.2 %collective-permute-done.9 = f32[1,128,256]{2,1,0:T(8,128)} collective-permute-done((f32[1,128,256]{2,1,0:T(8,128)}, f32[1,128,256]{2,1,0:T(8,128)}, u32[]{:S(2)}, u32[]{:S(2)}) %collective-permute-start.9) | collective-permute-done | bytes 131104 | tf_op jit(solution)/shard_map/ppermute | solution.py:14
  94.4 3.2 %fusion.9 = bf16[1024,256]{0,1:T(8,128)(2,1)} fusion(f32[1024,256]{0,1:T(8,128)} %convolution_bitcast_fusion, f32[1024,256]{0,1:T(8,128)} %convolution_bitcast_fusion.1, f32[1024,256]{0,1:T(8,128)} %convolution_bitcast_fusion.2, f32[1024,256]{0,1:T(8,128)S(1)} %copy-done.2, bf16[4,1024,128]{2,1,0:T(8,128)(2,1)S(1)} %copy-done.1, ...), kind=kOutput, calls=%fused_computation.18 | convolution fusion | flops 76922880 | bytes 5177345 | tf_op jit(solution)/shard_map/dot_general | solution.py:62
  97.6 2.0 %copy.25 = bf16[1024,256]{1,0:T(8,128)(2,1)} copy(bf16[1024,256]{0,1:T(8,128)(2,1)} %fusion.9) | data formatting | bytes 1048576 | tf_op jit(solution)/shard_map/convert_element_type | solution.py:67
  (71 shorter events, 20.1 us)
Async XLA Ops:
  0.0 21.8 %copy-start = (bf16[1024,512]{1,0:T(8,128)(2,1)S(1)}, bf16[1024,512]{1,0:T(8,128)(2,1)}, u32[]{:S(2)}) copy-start(bf16[1024,512]{1,0:T(8,128)(2,1)} %param.6) | copy-start | bytes 3145732
  1.9 2.1 %collective-permute-start = (f32[4,128,256]{2,1,0:T(8,128)S(1)}, f32[4,128,256]{2,1,0:T(8,128)S(1)}, u32[]{:S(2)}, u32[]{:S(2)}) collective-permute-start(f32[4,128,256]{2,1,0:T(8,128)S(1)} %fusion.14), channel_id=1, source_target_pairs={{0,1},{1,0},{2,3},{3,2},{4,5},{5,4},{6,7},{7,6},{8,9},{9,8},{10,11... | collective-permute-start | bytes 1572872 | tf_op jit(solution)/shard_map/ppermute | solution.py:14
  4.1 17.7 %copy-start.3 = (bf16[1024,256]{1,0:T(8,128)(2,1)S(1)}, bf16[1024,256]{1,0:T(8,128)(2,1)}, u32[]{:S(2)}) copy-start(bf16[1024,256]{1,0:T(8,128)(2,1)} %param.5) | copy-start | bytes 1572868
  4.1 15.2 %collective-permute-start.1 = (f32[4,128,256]{2,1,0:T(8,128)S(1)}, f32[4,128,256]{2,1,0:T(8,128)S(1)}, u32[]{:S(2)}, u32[]{:S(2)}) collective-permute-start(f32[4,128,256]{2,1,0:T(8,128)S(1)} %add.84), channel_id=1, source_target_pairs={{0,2},{1,3},{2,0},{3,1},{4,6},{5,7},{6,4},{7,5},{8,10},{9,11},{10,... | collective-permute-start | bytes 1572872 | tf_op jit(solution)/shard_map/ppermute | solution.py:14
  20.0 10.8 %collective-permute-start.2 = (f32[3,128,256]{2,1,0:T(8,128)S(1)}, f32[3,128,256]{2,1,0:T(8,128)}, u32[]{:S(2)}, u32[]{:S(2)}) collective-permute-start(f32[3,128,256]{2,1,0:T(8,128)S(1)} %slice_add_fusion.1), channel_id=1, source_target_pairs={{0,4},{1,5},{2,6},{3,7},{4,0},{5,1},{6,2},{7,3},{8,12},{9,13},{10,... | collective-permute-start | bytes 1179656 | tf_op jit(solution)/shard_map/ppermute | solution.py:14
  31.7 7.0 %collective-permute-start.3 = (f32[2,128,256]{2,1,0:T(8,128)S(1)}, f32[2,128,256]{2,1,0:T(8,128)S(1)}, u32[]{:S(2)}, u32[]{:S(2)}) collective-permute-start(f32[2,128,256]{2,1,0:T(8,128)S(1)} %slice_add_fusion.3), channel_id=1, source_target_pairs={{0,8},{1,9},{2,10},{3,11},{4,12},{5,13},{6,14},{7,15},{8,0},{9,1},... | collective-permute-start | bytes 786440 | tf_op jit(solution)/shard_map/ppermute | solution.py:14
  35.7 5.4 %copy-start.8 = (bf16[128,128]{1,0:T(8,128)(2,1)S(1)}, bf16[128,128]{1,0:T(8,128)(2,1)}, u32[]{:S(2)}) copy-start(bf16[128,128]{1,0:T(8,128)(2,1)} %copy-done.7) | copy-start | bytes 98308
  35.7 5.4 %copy-start.18 = (bf16[128,128]{0,1:T(8,128)(2,1)S(1)}, bf16[128,128]{0,1:T(8,128)(2,1)}, u32[]{:S(2)}) copy-start(bf16[128,128]{0,1:T(8,128)(2,1)} %copy.18) | copy-start | bytes 98308
  38.8 7.4 %copy-start.5 = (bf16[128,128]{1,0:T(8,128)(2,1)S(1)}, bf16[128,128]{1,0:T(8,128)(2,1)}, u32[]{:S(2)}) copy-start(bf16[128,128]{1,0:T(8,128)(2,1)} %copy-done.4) | copy-start | bytes 98308
  38.8 7.4 %copy-start.16 = (bf16[128,128]{0,1:T(8,128)(2,1)S(1)}, bf16[128,128]{0,1:T(8,128)(2,1)}, u32[]{:S(2)}) copy-start(bf16[128,128]{0,1:T(8,128)(2,1)} %copy.15) | copy-start | bytes 98308
  38.8 7.4 %copy-start.22 = (f32[1024]{0:T(1024)S(1)}, f32[1024]{0:T(1024)}, u32[]{:S(2)}) copy-start(f32[1024]{0:T(1024)} %param.9) | copy-start | bytes 12292
  38.8 7.3 %collective-permute-start.4 = (f32[1,128,256]{2,1,0:T(8,128)S(1)}, f32[1,128,256]{2,1,0:T(8,128)S(1)}, u32[]{:S(2)}, u32[]{:S(2)}) collective-permute-start(f32[1,128,256]{2,1,0:T(8,128)S(1)} %slice_add_fusion.5), channel_id=1, source_target_pairs={{0,16},{1,17},{2,18},{3,19},{4,20},{5,21},{6,22},{7,23},{8,24},{9,... | collective-permute-start | bytes 393224 | tf_op jit(solution)/shard_map/ppermute | solution.py:14
  49.4 2.0 %collective-permute-start.5 = (f32[4,128,256]{2,1,0:T(8,128)S(1)}, f32[4,128,256]{2,1,0:T(8,128)S(1)}, u32[]{:S(2)}, u32[]{:S(2)}) collective-permute-start(f32[4,128,256]{2,1,0:T(8,128)S(1)} %convolution_bitcast_fusion.9), channel_id=1, source_target_pairs={{0,1},{1,0},{2,3},{3,2},{4,5},{5,4},{6,7},{7,6},{8,9},{9,8},{10,11... | collective-permute-start | bytes 1572872 | tf_op jit(solution)/shard_map/ppermute | solution.py:14
  51.5 14.0 %collective-permute-start.6 = (f32[4,128,256]{2,1,0:T(8,128)S(1)}, f32[4,128,256]{2,1,0:T(8,128)S(1)}, u32[]{:S(2)}, u32[]{:S(2)}) collective-permute-start(f32[4,128,256]{2,1,0:T(8,128)S(1)} %add.98), channel_id=1, source_target_pairs={{0,2},{1,3},{2,0},{3,1},{4,6},{5,7},{6,4},{7,5},{8,10},{9,11},{10,... | collective-permute-start | bytes 1572872 | tf_op jit(solution)/shard_map/ppermute | solution.py:14
  66.3 10.4 %collective-permute-start.7 = (f32[3,128,256]{2,1,0:T(8,128)S(1)}, f32[3,128,256]{2,1,0:T(8,128)}, u32[]{:S(2)}, u32[]{:S(2)}) collective-permute-start(f32[3,128,256]{2,1,0:T(8,128)S(1)} %slice_add_fusion), channel_id=1, source_target_pairs={{0,4},{1,5},{2,6},{3,7},{4,0},{5,1},{6,2},{7,3},{8,12},{9,13},{10,... | collective-permute-start | bytes 1179656 | tf_op jit(solution)/shard_map/ppermute | solution.py:14
  74.1 4.6 %copy-start.12 = (bf16[128,128]{1,0:T(8,128)(2,1)S(1)}, bf16[128,128]{1,0:T(8,128)(2,1)}, u32[]{:S(2)}) copy-start(bf16[128,128]{1,0:T(8,128)(2,1)} %copy-done.10) | copy-start | bytes 98308
  74.1 4.6 %copy-start.21 = (bf16[128,128]{0,1:T(8,128)(2,1)S(1)}, bf16[128,128]{0,1:T(8,128)(2,1)}, u32[]{:S(2)}) copy-start(bf16[128,128]{0,1:T(8,128)(2,1)} %copy.19) | copy-start | bytes 98308
  78.4 6.8 %collective-permute-start.8 = (f32[2,128,256]{2,1,0:T(8,128)}, f32[2,128,256]{2,1,0:T(8,128)S(1)}, u32[]{:S(2)}, u32[]{:S(2)}) collective-permute-start(f32[2,128,256]{2,1,0:T(8,128)} %slice_add_fusion.2), channel_id=1, source_target_pairs={{0,8},{1,9},{2,10},{3,11},{4,12},{5,13},{6,14},{7,15},{8,0},{9,1},... | collective-permute-start | bytes 786440 | tf_op jit(solution)/shard_map/ppermute | solution.py:14
  78.7 10.0 %copy-start.9 = (bf16[128,128]{1,0:T(8,128)(2,1)S(1)}, bf16[128,128]{1,0:T(8,128)(2,1)}, u32[]{:S(2)}) copy-start(bf16[128,128]{1,0:T(8,128)(2,1)} %copy-done.7) | copy-start | bytes 98308
  78.7 10.0 %copy-start.19 = (bf16[128,128]{0,1:T(8,128)(2,1)S(1)}, bf16[128,128]{0,1:T(8,128)(2,1)}, u32[]{:S(2)}) copy-start(bf16[128,128]{0,1:T(8,128)(2,1)} %copy.18) | copy-start | bytes 98308
  81.1 13.3 %copy-start.2 = (f32[1024,256]{0,1:T(8,128)S(1)}, f32[1024,256]{0,1:T(8,128)}, u32[]{:S(2)}) copy-start(f32[1024,256]{0,1:T(8,128)} %copy.24) | copy-start | bytes 3145732
  86.8 7.6 %copy-start.6 = (bf16[128,128]{1,0:T(8,128)(2,1)S(1)}, bf16[128,128]{1,0:T(8,128)(2,1)}, u32[]{:S(2)}) copy-start(bf16[128,128]{1,0:T(8,128)(2,1)} %copy-done.4) | copy-start | bytes 98308
  86.8 7.6 %copy-start.17 = (bf16[128,128]{0,1:T(8,128)(2,1)S(1)}, bf16[128,128]{0,1:T(8,128)(2,1)}, u32[]{:S(2)}) copy-start(bf16[128,128]{0,1:T(8,128)(2,1)} %copy.15) | copy-start | bytes 98308
  86.8 7.6 %collective-permute-start.9 = (f32[1,128,256]{2,1,0:T(8,128)}, f32[1,128,256]{2,1,0:T(8,128)}, u32[]{:S(2)}, u32[]{:S(2)}) collective-permute-start(f32[1,128,256]{2,1,0:T(8,128)} %slice_add_fusion.4), channel_id=1, source_target_pairs={{0,16},{1,17},{2,18},{3,19},{4,20},{5,21},{6,22},{7,23},{8,24},{9,... | collective-permute-start | bytes 393224 | tf_op jit(solution)/shard_map/ppermute | solution.py:14
  (9 other events, 15.3 us)
where the time goes:
time: 100 us; the launch traced here: 99.7 us
  waiting for transfers between devices  47.3 us (47%)
  matrix products  22.7 us (23%)
  starting transfers between devices  13.5 us (14%)
  local copies, waits for them, and re-layouts  11.4 us (11%)
  other arithmetic  4.5 us (4%)
    ppermute x10, waiting for transfers between devices, partner(): return lax.ppermute(value, axis, pairs)  47.3 us
    dot_general x8, matrix products, apply_kernel(): jnp.dot(bases[level], coeffs, preferred_element_type=jnp.float32)  18.4 us
    ppermute x10, starting transfers between devices, partner(): return lax.ppermute(value, axis, pairs)  13.5 us
    add x8, other arithmetic, sums_doubling(): totals = totals[:keeping] + got[:keeping]  4.5 us
    squeeze x5, local copies, waits for them, and re-layouts, apply_kernel(): lax.dynamic_index_in_dim(couplings, (1 << level) - 1 + pair_idx, 0, keepd...  3.66 us
    reshape x2, local copies, waits for them, and re-layouts, apply_kernel(): result = jnp.einsum('lab,lbc->lac', leaves.reshape(nleaf, LEAF, LEAF), ve...  2.63 us
    dot_general x2, matrix products, apply_kernel(): jnp.einsum('lrk,rc->lkc', bases, vec, preferred_element_type=jnp.float32)  2.45 us
    convert_element_type x1, local copies, waits for them, and re-layouts, on_device(): return apply_kernel(scaled).astype(jnp.bfloat16)  2.04 us
  transfers between devices with their start and end apart: 10, of which 10 were waited for; matrix products, arithmetic and copies ran while one was open for 22% of the time, Pallas kernels for 0%

commit v1 on v0

v1 whole, which is shorter than its diff:
```python
import functools
import math

import jax
import jax.numpy as jnp
from jax import lax
from jax.experimental import pallas as pl
from jax.experimental.pallas import tpu as pltpu
from jax.sharding import PartitionSpec as P

LEAF = 512
F32 = jnp.float32
BF16 = jnp.bfloat16


def in_vmem(count):
    return [pl.BlockSpec(memory_space=pltpu.VMEM)] * count


def call(kernel, outs, scalars, arrays, flops):
    moved = sum(math.prod(a.shape) * a.dtype.itemsize for a in (*arrays, *outs))
    return pl.pallas_call(
        kernel,
        out_shape=outs,
        in_specs=[pl.BlockSpec(memory_space=pltpu.SMEM)] + in_vmem(len(arrays)),
        out_specs=in_vmem(len(outs)),
        compiler_params=pltpu.CompilerParams(vmem_limit_bytes=24 * 2**20),
        cost_estimate=pl.CostEstimate(flops=flops, bytes_accessed=moved, transcendentals=0),
    )(scalars, *arrays)


def side_by_side(bases_ref, first, second):
    return jnp.concatenate([bases_ref[first], bases_ref[second]], axis=1)


def projections(bases_ref, parity, vec, out_ref):
    both = side_by_side(bases_ref, parity, parity + 2)
    proj = lax.dot_general(both, vec, (((0,), (0,)), ((), ())), preferred_element_type=F32)
    rank = bases_ref.shape[2]
    out_ref[0] = proj[:rank]
    out_ref[1] = proj[rank:]


def project_kernel(flip, ids_ref, bases_ref, vec_ref, out_ref):
    parity = ids_ref[0]
    projections(bases_ref, 1 - parity if flip else parity, vec_ref[...], out_ref)


def coefficients(ids_ref, couplings_ref, level, sums, factors):
    quotient = (sums * factors[level]).astype(BF16)
    coupling = couplings_ref[ids_ref[1 + level]]
    oriented = jnp.where(ids_ref[5 + level] == 0, coupling.astype(F32), coupling.astype(F32).T)
    return jnp.dot(oriented.astype(BF16), quotient, preferred_element_type=F32).astype(BF16)


def both_coefficients(ids_ref, couplings_ref, slot, own, other, factors):
    odd = ids_ref[0] == 1
    lower = coefficients(ids_ref, couplings_ref, 2 * slot, jnp.where(odd, own, other), factors)
    upper = coefficients(ids_ref, couplings_ref, 2 * slot + 1, jnp.where(odd, other, own), factors)
    return jnp.concatenate([lower, upper], axis=0)


def local_kernel(factors, ids_ref, couplings_ref, own_ref, other_ref, bases_ref, leaves_ref, vec_ref, part_ref):
    coeffs = both_coefficients(ids_ref, couplings_ref, 1, own_ref[...], other_ref[...], factors)
    for leaf in range(vec_ref.shape[0] // LEAF):
        rows = pl.ds(leaf * LEAF, LEAF)
        near = jnp.dot(leaves_ref[rows, :], vec_ref[rows, :], preferred_element_type=F32)
        basis = jnp.concatenate([bases_ref[2, rows, :], bases_ref[3, rows, :]], axis=1)
        part_ref[rows, :] = near + jnp.dot(basis, coeffs, preferred_element_type=F32)


def far(ids_ref, couplings_ref, own_ref, other_ref, bases_ref, part_ref, factors):
    coeffs = both_coefficients(ids_ref, couplings_ref, 0, own_ref[...], other_ref[...], factors)
    return part_ref[...] + jnp.dot(side_by_side(bases_ref, 0, 1), coeffs, preferred_element_type=F32)


def scale_kernel(
    factors, ids_ref, couplings_ref, own_ref, other_ref, bases_ref, part_ref, weights_ref, scaled_ref, send_ref
):
    first = far(ids_ref, couplings_ref, own_ref, other_ref, bases_ref, part_ref, factors)
    columns = weights_ref[...].T
    span = weights_ref.shape[1]
    for block in range(weights_ref.shape[0]):
        rows = slice(block * span, (block + 1) * span)
        scaled_ref[rows, :] = (columns[:, block : block + 1] * first[rows]).astype(BF16)
    projections(bases_ref, ids_ref[0], scaled_ref[...], send_ref)


def result_kernel(factors, ids_ref, couplings_ref, own_ref, other_ref, bases_ref, part_ref, result_ref):
    total = far(ids_ref, couplings_ref, own_ref, other_ref, bases_ref, part_ref, factors)
    result_ref[...] = total.astype(BF16)


def on_device(signal, leaves, bases, couplings, weights):
    count = lax.axis_size("rows")
    bits = count.bit_length() - 1
    myself = lax.axis_index("rows")
    rows_dev, width = signal.shape
    levels, _, rank = bases.shape
    odd = myself % 2 == 1
    far1, far2, far3, far4 = (1 << (bits - level - 1) for level in range(levels))
    factors = [1.0 / math.sqrt(rows_dev * (count >> level + 1) * rank) for level in range(levels)]
    ids = jnp.stack(
        [myself % 2]
        + [(1 << level) - 1 + (myself >> bits - level) for level in range(levels)]
        + [myself >> bits - level - 1 & 1 for level in range(levels)]
    ).astype(jnp.int32)
    span = 128
    weight_rows = weights.reshape(rows_dev // span, span)
    mults = rows_dev * width * rank * 2

    def swap(value, odd_mask, even_mask):
        pairs = [(source, source ^ (odd_mask if source % 2 else even_mask)) for source in range(count)]
        return lax.ppermute(value, "rows", pairs)

    def project(vec, flip):
        (out,) = call(
            functools.partial(project_kernel, flip),
            [jax.ShapeDtypeStruct((2, rank, width), F32)],
            ids,
            [bases, vec],
            2 * mults,
        )
        return out

    def siblings(send, keep):
        sums = keep + swap(send, 1, 1)
        for bit in range(1, bits - levels):
            sums = sums + swap(sums, 1 << bit, 1 << bit)
        high, low = sums[0], sums[1]
        high = high + swap(high, far4, far3)
        low = swap(low, far3, far4)
        high = high + swap(high, far3, far4)
        low = jnp.where(odd, low + swap(low, far4, 0), low)
        got = swap(high, far2, far2)
        high = jnp.where(odd, high + got, got)
        high = swap(high, far1, 0)
        return (high, swap(high, 1, 1)), (low, swap(low, 1, 1))

    def local(vec, low):
        (part,) = call(
            functools.partial(local_kernel, factors),
            [jax.ShapeDtypeStruct((rows_dev, width), F32)],
            ids,
            [couplings, *low, bases, leaves, vec],
            (2 + LEAF // rank) * mults,
        )
        return part

    high, low = siblings(project(signal, False), project(signal, True))
    scaled, send = call(
        functools.partial(scale_kernel, factors),
        [jax.ShapeDtypeStruct((rows_dev, width), BF16), jax.ShapeDtypeStruct((2, rank, width), F32)],
        ids,
        [couplings, *high, bases, local(signal, low), weight_rows],
        4 * mults,
    )
    high, low = siblings(send, project(scaled, True))
    (result,) = call(
        functools.partial(result_kernel, factors),
        [jax.ShapeDtypeStruct((rows_dev, width), BF16)],
        ids,
        [couplings, *high, bases, local(scaled, low)],
        2 * mults,
    )
    return result


def solution(mesh):
    in_specs = (P("rows", None), P("rows", None), P(None, "rows", None), P(), P("rows"))
    out_specs = P("rows", None)
    return jax.shard_map(
        on_device, mesh=mesh, in_specs=in_specs, out_specs=out_specs, check_vma=False
    )
```

time: 100 us -> 56.2 us (0.56)
  waiting for transfers between devices: 47.3 us -> 18.8 us
  matrix products: 22.7 us -> 0 us
  starting transfers between devices: 13.5 us -> 25.1 us
  Pallas kernels: 0 us -> 8.61 us
  local copies, waits for them, and re-layouts: 11.4 us -> 3.07 us
  other arithmetic: 4.5 us -> 0.21 us
    ppermute x10 -> x18, waiting for transfers between devices: 47.3 us -> 18.8 us  [swap(): return lax.ppermute(value, 'rows', pairs)]
    dot_general x12 -> x0, matrix products: 22.7 us -> none  [the longest x8 18.4 us: apply_kernel(): jnp.dot(bases[level], coeffs, preferred_element_type=jnp.float32)]
    ppermute x10 -> x18, starting transfers between devices: 13.5 us -> 25.1 us  [swap(): return lax.ppermute(value, 'rows', pairs)]
    pallas_call x0 -> x7, Pallas kernels: none -> 8.61 us  [call(): pl.pallas_call(kernel, out_shape=outs, in_specs=[pl.BlockSpec(memory_spac...]
    add x8 -> x6, other arithmetic: 4.5 us -> 0.14 us  [the longest x2 0.07 us: siblings(): sums = keep + swap(send, 1, 1)]
    squeeze x5 -> x2, local copies, waits for them, and re-layouts: 3.66 us -> 0.69 us  [siblings(): high, low = (sums[0], sums[1])]
    reshape x2 -> x0, local copies, waits for them, and re-layouts: 2.63 us -> none  [apply_kernel(): result = jnp.einsum('lab,lbc->lac', leaves.reshape(nleaf, LEAF, LEAF), ve...]
    convert_element_type x1 -> x0, local copies, waits for them, and re-layouts: 2.04 us -> none  [on_device(): return apply_kernel(scaled).astype(jnp.bfloat16)]
  transfers between devices with their start and end apart: 10 -> 18, of which waited for: 10 -> 9; matrix products, arithmetic and copies ran while one was open for 22% -> 0% of each run, Pallas kernels for 0% -> 8%
where the time goes in v1:
time: 56.2 us; the launch traced here: 56 us
  starting transfers between devices  25.1 us (45%)
  waiting for transfers between devices  18.8 us (33%)
  Pallas kernels  8.61 us (15%)
  local copies, waits for them, and re-layouts  3.07 us (5%)
    ppermute x18, starting transfers between devices, swap(): return lax.ppermute(value, 'rows', pairs)  25.1 us
    ppermute x18, waiting for transfers between devices, swap(): return lax.ppermute(value, 'rows', pairs)  18.8 us
    pallas_call x7, Pallas kernels, call(): pl.pallas_call(kernel, out_shape=outs, in_specs=[pl.BlockSpec(memory_spac...  8.61 us
    unnamed x14, local copies, waits for them, and re-layouts  2.29 us
  transfers between devices with their start and end apart: 18, of which 9 were waited for; matrix products, arithmetic and copies ran while one was open for 0% of the time, Pallas kernels for 8%

profile of v1, /device:TPU:0, one launch (start us, length us, event | category | flops | bytes accessed | tf_op | source)
XLA Modules:
  0.0 56.0 jit_solution(3414028846435348931)
XLA Ops:
  0.1 1.2 %copy-done = bf16[4,1024,128]{2,1,0:T(8,128)(2,1)S(1)} copy-done((bf16[4,1024,128]{2,1,0:T(8,128)(2,1)S(1)}, bf16[4,1024,128]{2,1,0:T(8,128)(2,1)}, u32[]{:S(2)}) %copy-start) | copy-done | bytes 1048600
  1.3 1.0 %copy-done.3 = bf16[1024,256]{1,0:T(8,128)(2,1)S(1)} copy-done((bf16[1024,256]{1,0:T(8,128)(2,1)S(1)}, bf16[1024,256]{1,0:T(8,128)(2,1)}, u32[]{:S(2)}) %copy-start.3) | copy-done | bytes 524312
  2.4 0.9 %shard_map.56 = f32[2,128,256]{2,1,0:T(8,128)S(1)} custom-call(s32[9]{0:T(128)S(1)} %stack.39.ids_ref, bf16[4,1024,128]{2,1,0:T(8,128)(2,1)S(1)} %copy-done, bf16[1024,256]{1,0:T(8,128)(2,1)S(1)} %copy-done.3), custom_call_target="tpu_custom_call" | custom-call | flops 134217728 | bytes 1835008 | tf_op jit(solution)/shard_map/pallas_call | solution.py:22
  3.8 0.9 %shard_map.55 = f32[2,128,256]{2,1,0:T(8,128)S(1)} custom-call(s32[9]{0:T(128)S(1)} %stack.39.ids_ref, bf16[4,1024,128]{2,1,0:T(8,128)(2,1)S(1)} %copy-done, bf16[1024,256]{1,0:T(8,128)(2,1)S(1)} %copy-done.3), custom_call_target="tpu_custom_call" | custom-call | flops 134217728 | bytes 1835008 | tf_op jit(solution)/shard_map/pallas_call | solution.py:22
  5.7 2.9 %collective-permute-start.1 = (f32[128,256]{1,0:T(8,128)S(1)}, f32[128,256]{1,0:T(8,128)S(1)}, u32[]{:S(2)}, u32[]{:S(2)}) collective-permute-start(f32[128,256]{1,0:T(8,128)S(1)} %get-tuple-element.12), channel_id=1, source_target_pairs={{0,4},{1,3},{2,6},{3,1},{4,0},{5,7},{6,2},{7,5},{8,12},{9,11},{10,... | collective-permute-start | bytes 393224 | tf_op jit(solution)/shard_map/ppermute | solution.py:114
  8.5 2.9 %collective-permute-done.1 = f32[128,256]{1,0:T(8,128)S(1)} collective-permute-done((f32[128,256]{1,0:T(8,128)S(1)}, f32[128,256]{1,0:T(8,128)S(1)}, u32[]{:S(2)}, u32[]{:S(2)}) %collective-permute-start.1) | collective-permute-done | bytes 131104 | tf_op jit(solution)/shard_map/ppermute | solution.py:114
  11.5 2.1 %collective-permute-start.2 = (f32[128,256]{1,0:T(8,128)S(1)}, f32[128,256]{1,0:T(8,128)S(1)}, u32[]{:S(2)}, u32[]{:S(2)}) collective-permute-start(f32[128,256]{1,0:T(8,128)S(1)} %fusion), channel_id=1, source_target_pairs={{0,2},{1,5},{2,0},{3,7},{4,6},{5,1},{6,4},{7,3},{8,10},{9,13},{10,... | collective-permute-start | bytes 393224 | tf_op jit(solution)/shard_map/ppermute | solution.py:114
  13.7 2.9 %collective-permute-done.2 = f32[128,256]{1,0:T(8,128)S(1)} collective-permute-done((f32[128,256]{1,0:T(8,128)S(1)}, f32[128,256]{1,0:T(8,128)S(1)}, u32[]{:S(2)}, u32[]{:S(2)}) %collective-permute-start.2) | collective-permute-done | bytes 131104 | tf_op jit(solution)/shard_map/ppermute | solution.py:114
  16.6 2.1 %collective-permute-start.3 = (f32[128,256]{1,0:T(8,128)S(1)}, f32[128,256]{1,0:T(8,128)S(1)}, u32[]{:S(2)}, u32[]{:S(2)}) collective-permute-start(f32[128,256]{1,0:T(8,128)S(1)} %add.46), channel_id=1, source_target_pairs={{0,8},{1,9},{2,10},{3,11},{4,12},{5,13},{6,14},{7,15},{8,0},{9,1},... | collective-permute-start | bytes 393224 | tf_op jit(solution)/shard_map/ppermute | solution.py:114
  19.4 2.3 %collective-permute-done.3 = f32[128,256]{1,0:T(8,128)S(1)} collective-permute-done((f32[128,256]{1,0:T(8,128)S(1)}, f32[128,256]{1,0:T(8,128)S(1)}, u32[]{:S(2)}, u32[]{:S(2)}) %collective-permute-start.3) | collective-permute-done | bytes 131104 | tf_op jit(solution)/shard_map/ppermute | solution.py:114
  22.4 2.0 %collective-permute-start.8 = (f32[128,256]{1,0:T(8,128)S(1)}, f32[128,256]{1,0:T(8,128)S(1)}, u32[]{:S(2)}, u32[]{:S(2)}) collective-permute-start(f32[128,256]{1,0:T(8,128)S(1)} %add_select_fusion.2.own_ref), channel_id=1, source_target_pairs={{0,1},{1,0},{2,3},{3,2},{4,5},{5,4},{6,7},{7,6},{8,9},{9,8},{10,11... | collective-permute-start | bytes 393224 | tf_op jit(solution)/shard_map/ppermute | solution.py:114
  24.4 3.7 %collective-permute-start.5 = (f32[128,256]{1,0:T(8,128)S(1)}, f32[128,256]{1,0:T(8,128)S(1)}, u32[]{:S(2)}, u32[]{:S(2)}) collective-permute-start(f32[128,256]{1,0:T(8,128)S(1)} %collective-permute-done.4.own_ref), channel_id=1, source_target_pairs={{0,1},{1,0},{2,3},{3,2},{4,5},{5,4},{6,7},{7,6},{8,9},{9,8},{10,11... | collective-permute-start | bytes 393224 | tf_op jit(solution)/shard_map/ppermute | solution.py:114
  28.1 1.3 %shard_map.57.part_ref = f32[1024,256]{1,0:T(8,128)S(1)} custom-call(s32[9]{0:T(128)S(1)} %stack.39.ids_ref, bf16[15,128,128]{2,1,0:T(8,128)(2,1)S(1)} %copy-done.2, f32[128,256]{1,0:T(8,128)S(1)} %add_select_fusion.2.own_ref, f32[128,256]{1,0:T(8,128)S(1)} %collective-permute-done.8.other_ref, bf16[4,1024,128]{2,1,0:T(8,128)(2,1)S(1)} %copy-done.1, ...), custom_call_target="tpu_custom_call" | custom-call | flops 402653184 | bytes 4423680 | tf_op jit(solution)/shard_map/pallas_call | solution.py:22
  29.5 1.4 %shard_map.58 = (bf16[1024,256]{1,0:T(8,128)(2,1)S(1)}, f32[2,128,256]{2,1,0:T(8,128)S(1)}) custom-call(s32[9]{0:T(128)S(1)} %stack.39.ids_ref, bf16[15,128,128]{2,1,0:T(8,128)(2,1)S(1)} %copy-done.2, f32[128,256]{1,0:T(8,128)S(1)} %collective-permute-done.4.own_ref, f32[128,256]{1,0:T(8,128)S(1)} %collective-permute-done.5.other_ref, ...), custom_call_target="tpu_custom_call" | custom-call | flops 268435456 | bytes 3641344 | tf_op jit(solution)/shard_map/pallas_call | solution.py:22
  31.0 0.9 %shard_map.59 = f32[2,128,256]{2,1,0:T(8,128)S(1)} custom-call(s32[9]{0:T(128)S(1)} %stack.39.ids_ref, bf16[4,1024,128]{2,1,0:T(8,128)(2,1)S(1)} %copy-done.1, bf16[1024,256]{1,0:T(8,128)(2,1)S(1)} %get-tuple-element.7.vec_ref), custom_call_target="tpu_custom_call" | custom-call | flops 134217728 | bytes 1835008 | tf_op jit(solution)/shard_map/pallas_call | solution.py:22
  32.6 1.5 %collective-permute-start.10 = (f32[128,256]{1,0:T(8,128)S(1)}, f32[128,256]{1,0:T(8,128)S(1)}, u32[]{:S(2)}, u32[]{:S(2)}) collective-permute-start(f32[128,256]{1,0:T(8,128)S(1)} %get-tuple-element.10), channel_id=1, source_target_pairs={{0,4},{1,3},{2,6},{3,1},{4,0},{5,7},{6,2},{7,5},{8,12},{9,11},{10,... | collective-permute-start | bytes 393224 | tf_op jit(solution)/shard_map/ppermute | solution.py:114
  34.1 3.5 %collective-permute-done.10 = f32[128,256]{1,0:T(8,128)S(1)} collective-permute-done((f32[128,256]{1,0:T(8,128)S(1)}, f32[128,256]{1,0:T(8,128)S(1)}, u32[]{:S(2)}, u32[]{:S(2)}) %collective-permute-start.10) | collective-permute-done | bytes 131104 | tf_op jit(solution)/shard_map/ppermute | solution.py:114
  38.2 1.5 %collective-permute-start.15 = (f32[128,256]{1,0:T(8,128)S(1)}, f32[128,256]{1,0:T(8,128)S(1)}, u32[]{:S(2)}, u32[]{:S(2)}) collective-permute-start(f32[128,256]{1,0:T(8,128)S(1)} %get-tuple-element.9), channel_id=1, source_target_pairs={{0,2},{1,5},{2,0},{3,7},{4,6},{5,1},{6,4},{7,3},{8,10},{9,13},{10,... | collective-permute-start | bytes 393224 | tf_op jit(solution)/shard_map/ppermute | solution.py:114
  39.7 2.9 %collective-permute-done.11 = f32[128,256]{1,0:T(8,128)S(1)} collective-permute-done((f32[128,256]{1,0:T(8,128)S(1)}, f32[128,256]{1,0:T(8,128)S(1)}, u32[]{:S(2)}, u32[]{:S(2)}) %collective-permute-start.11) | collective-permute-done | bytes 131104 | tf_op jit(solution)/shard_map/ppermute | solution.py:114
  42.7 1.0 %collective-permute-start.12 = (f32[128,256]{1,0:T(8,128)S(1)}, f32[128,256]{1,0:T(8,128)S(1)}, u32[]{:S(2)}, u32[]{:S(2)}) collective-permute-start(f32[128,256]{1,0:T(8,128)S(1)} %add.51), channel_id=1, source_target_pairs={{0,8},{1,9},{2,10},{3,11},{4,12},{5,13},{6,14},{7,15},{8,0},{9,1},... | collective-permute-start | bytes 393224 | tf_op jit(solution)/shard_map/ppermute | solution.py:114
  44.7 3.0 %collective-permute-done.12 = f32[128,256]{1,0:T(8,128)S(1)} collective-permute-done((f32[128,256]{1,0:T(8,128)S(1)}, f32[128,256]{1,0:T(8,128)S(1)}, u32[]{:S(2)}, u32[]{:S(2)}) %collective-permute-start.12) | collective-permute-done | bytes 131104 | tf_op jit(solution)/shard_map/ppermute | solution.py:114
  48.8 4.0 %collective-permute-start.14 = (f32[128,256]{1,0:T(8,128)S(1)}, f32[128,256]{1,0:T(8,128)S(1)}, u32[]{:S(2)}, u32[]{:S(2)}) collective-permute-start(f32[128,256]{1,0:T(8,128)S(1)} %collective-permute-done.13.own_ref), channel_id=1, source_target_pairs={{0,1},{1,0},{2,3},{3,2},{4,5},{5,4},{6,7},{7,6},{8,9},{9,8},{10,11... | collective-permute-start | bytes 393224 | tf_op jit(solution)/shard_map/ppermute | solution.py:114
  52.7 1.3 %shard_map.60.part_ref = f32[1024,256]{1,0:T(8,128)S(1)} custom-call(s32[9]{0:T(128)S(1)} %stack.39.ids_ref, bf16[15,128,128]{2,1,0:T(8,128)(2,1)S(1)} %copy-done.2, f32[128,256]{1,0:T(8,128)S(1)} %add_select_fusion.own_ref, f32[128,256]{1,0:T(8,128)S(1)} %collective-permute-done.17.other_ref, bf16[4,1024,128]{2,1,0:T(8,128)(2,1)S(1)} %copy-done.1, ...), custom_call_target="tpu_custom_call" | custom-call | flops 402653184 | bytes 4423680 | tf_op jit(solution)/shard_map/pallas_call | solution.py:22
  54.1 1.9 %shard_map.61 = bf16[1024,256]{1,0:T(8,128)(2,1)} custom-call(s32[9]{0:T(128)S(1)} %stack.39.ids_ref, bf16[15,128,128]{2,1,0:T(8,128)(2,1)S(1)} %copy-done.2, f32[128,256]{1,0:T(8,128)S(1)} %collective-permute-done.13.own_ref, f32[128,256]{1,0:T(8,128)S(1)} %collective-permute-done.14.other_ref, bf16[4,1024,128]{2,1,0:T(8,128)(2,1)S(1)} %copy-done.1, ...), custom_call_target="tpu_custom_call" | custom-call | flops 134217728 | bytes 3375104 | tf_op jit(solution)/shard_map/pallas_call | solution.py:22
  (46 shorter events, 6.5 us)
Async XLA Ops:
  0.1 1.2 %copy-start = (bf16[4,1024,128]{2,1,0:T(8,128)(2,1)S(1)}, bf16[4,1024,128]{2,1,0:T(8,128)(2,1)}, u32[]{:S(2)}) copy-start(bf16[4,1024,128]{2,1,0:T(8,128)(2,1)} %bases_ref.13) | copy-start | bytes 3145732
  3.3 1.7 %collective-permute-start = (f32[2,128,256]{2,1,0:T(8,128)S(1)}, f32[2,128,256]{2,1,0:T(8,128)S(1)}, u32[]{:S(2)}, u32[]{:S(2)}) collective-permute-start(f32[2,128,256]{2,1,0:T(8,128)S(1)} %shard_map.56), channel_id=1, source_target_pairs={{0,1},{1,0},{2,3},{3,2},{4,5},{5,4},{6,7},{7,6},{8,9},{9,8},{10,11... | collective-permute-start | bytes 786440 | tf_op jit(solution)/shard_map/ppermute | solution.py:114
  3.8 24.3 %copy-start.5 = (bf16[1024,512]{1,0:T(8,128)(2,1)S(1)}, bf16[1024,512]{1,0:T(8,128)(2,1)}, u32[]{:S(2)}) copy-start(bf16[1024,512]{1,0:T(8,128)(2,1)} %leaves_ref.3) | copy-start | bytes 3145732
  5.0 23.1 %copy-start.1 = (bf16[4,1024,128]{2,1,0:T(8,128)(2,1)S(1)}, bf16[4,1024,128]{2,1,0:T(8,128)(2,1)}, u32[]{:S(2)}) copy-start(bf16[4,1024,128]{2,1,0:T(8,128)(2,1)} %bases_ref.13) | copy-start | bytes 3145732
  5.7 5.8 %collective-permute-start.1 = (f32[128,256]{1,0:T(8,128)S(1)}, f32[128,256]{1,0:T(8,128)S(1)}, u32[]{:S(2)}, u32[]{:S(2)}) collective-permute-start(f32[128,256]{1,0:T(8,128)S(1)} %get-tuple-element.12), channel_id=1, source_target_pairs={{0,4},{1,3},{2,6},{3,1},{4,0},{5,7},{6,2},{7,5},{8,12},{9,11},{10,... | collective-permute-start | bytes 393224 | tf_op jit(solution)/shard_map/ppermute | solution.py:114
  11.5 5.0 %collective-permute-start.2 = (f32[128,256]{1,0:T(8,128)S(1)}, f32[128,256]{1,0:T(8,128)S(1)}, u32[]{:S(2)}, u32[]{:S(2)}) collective-permute-start(f32[128,256]{1,0:T(8,128)S(1)} %fusion), channel_id=1, source_target_pairs={{0,2},{1,5},{2,0},{3,7},{4,6},{5,1},{6,4},{7,3},{8,10},{9,13},{10,... | collective-permute-start | bytes 393224 | tf_op jit(solution)/shard_map/ppermute | solution.py:114
  13.6 14.5 %copy-start.4 = (bf16[1024,256]{1,0:T(8,128)(2,1)S(1)}, bf16[1024,256]{1,0:T(8,128)(2,1)}, u32[]{:S(2)}) copy-start(bf16[1024,256]{1,0:T(8,128)(2,1)} %vec_ref.5) | copy-start | bytes 1572868
  13.6 5.2 %collective-permute-start.6 = (f32[128,256]{1,0:T(8,128)}, f32[128,256]{1,0:T(8,128)S(1)}, u32[]{:S(2)}, u32[]{:S(2)}) collective-permute-start(f32[128,256]{1,0:T(8,128)} %get-tuple-element.11), channel_id=1, source_target_pairs={{0,2},{1,5},{2,0},{3,7},{4,6},{5,1},{6,4},{7,3},{8,10},{9,13},{10,... | collective-permute-start | bytes 393224 | tf_op jit(solution)/shard_map/ppermute | solution.py:114
  16.6 11.6 %copy-start.2 = (bf16[15,128,128]{2,1,0:T(8,128)(2,1)S(1)}, bf16[15,128,128]{2,1,0:T(8,128)(2,1)}, u32[]{:S(2)}) copy-start(bf16[15,128,128]{2,1,0:T(8,128)(2,1)} %couplings_ref.7) | copy-start | bytes 1474564
  16.6 5.1 %collective-permute-start.3 = (f32[128,256]{1,0:T(8,128)S(1)}, f32[128,256]{1,0:T(8,128)S(1)}, u32[]{:S(2)}, u32[]{:S(2)}) collective-permute-start(f32[128,256]{1,0:T(8,128)S(1)} %add.46), channel_id=1, source_target_pairs={{0,8},{1,9},{2,10},{3,11},{4,12},{5,13},{6,14},{7,15},{8,0},{9,1},... | collective-permute-start | bytes 393224 | tf_op jit(solution)/shard_map/ppermute | solution.py:114
  18.8 3.6 %collective-permute-start.7 = (f32[128,256]{1,0:T(8,128)S(1)}, f32[128,256]{1,0:T(8,128)S(1)}, u32[]{:S(2)}, u32[]{:S(2)}) collective-permute-start(f32[128,256]{1,0:T(8,128)S(1)} %collective-permute-done.6), channel_id=1, source_target_pairs={{0,0},{1,3},{2,2},{3,1},{4,4},{5,7},{6,6},{7,5},{8,8},{9,11},{10,1... | collective-permute-start | bytes 393224 | tf_op jit(solution)/shard_map/ppermute | solution.py:114
  21.7 2.7 %collective-permute-start.4 = (f32[128,256]{1,0:T(8,128)S(1)}, f32[128,256]{1,0:T(8,128)S(1)}, u32[]{:S(2)}, u32[]{:S(2)}) collective-permute-start(f32[128,256]{1,0:T(8,128)S(1)} %add_select_fusion.3), channel_id=1, source_target_pairs={{0,0},{1,17},{2,2},{3,19},{4,4},{5,21},{6,6},{7,23},{8,8},{9,25},{... | collective-permute-start | bytes 393224 | tf_op jit(solution)/shard_map/ppermute | solution.py:114
  22.4 5.7 %collective-permute-start.8 = (f32[128,256]{1,0:T(8,128)S(1)}, f32[128,256]{1,0:T(8,128)S(1)}, u32[]{:S(2)}, u32[]{:S(2)}) collective-permute-start(f32[128,256]{1,0:T(8,128)S(1)} %add_select_fusion.2.own_ref), channel_id=1, source_target_pairs={{0,1},{1,0},{2,3},{3,2},{4,5},{5,4},{6,7},{7,6},{8,9},{9,8},{10,11... | collective-permute-start | bytes 393224 | tf_op jit(solution)/shard_map/ppermute | solution.py:114
  24.4 5.1 %collective-permute-start.5 = (f32[128,256]{1,0:T(8,128)S(1)}, f32[128,256]{1,0:T(8,128)S(1)}, u32[]{:S(2)}, u32[]{:S(2)}) collective-permute-start(f32[128,256]{1,0:T(8,128)S(1)} %collective-permute-done.4.own_ref), channel_id=1, source_target_pairs={{0,1},{1,0},{2,3},{3,2},{4,5},{5,4},{6,7},{7,6},{8,9},{9,8},{10,11... | collective-permute-start | bytes 393224 | tf_op jit(solution)/shard_map/ppermute | solution.py:114
  28.1 1.4 %copy-start.6 = (f32[1024]{0:T(1024)S(1)}, f32[1024]{0:T(1024)}, u32[]{:S(2)}) copy-start(f32[1024]{0:T(1024)} %param.9) | copy-start | bytes 12292
  30.9 1.6 %collective-permute-start.9 = (f32[2,128,256]{2,1,0:T(8,128)S(1)}, f32[2,128,256]{2,1,0:T(8,128)S(1)}, u32[]{:S(2)}, u32[]{:S(2)}) collective-permute-start(f32[2,128,256]{2,1,0:T(8,128)S(1)} %get-tuple-element.8), channel_id=1, source_target_pairs={{0,1},{1,0},{2,3},{3,2},{4,5},{5,4},{6,7},{7,6},{8,9},{9,8},{10,11... | collective-permute-start | bytes 786440 | tf_op jit(solution)/shard_map/ppermute | solution.py:114
  32.6 5.0 %collective-permute-start.10 = (f32[128,256]{1,0:T(8,128)S(1)}, f32[128,256]{1,0:T(8,128)S(1)}, u32[]{:S(2)}, u32[]{:S(2)}) collective-permute-start(f32[128,256]{1,0:T(8,128)S(1)} %get-tuple-element.10), channel_id=1, source_target_pairs={{0,4},{1,3},{2,6},{3,1},{4,0},{5,7},{6,2},{7,5},{8,12},{9,11},{10,... | collective-permute-start | bytes 393224 | tf_op jit(solution)/shard_map/ppermute | solution.py:114
  37.6 5.0 %collective-permute-start.11 = (f32[128,256]{1,0:T(8,128)S(1)}, f32[128,256]{1,0:T(8,128)S(1)}, u32[]{:S(2)}, u32[]{:S(2)}) collective-permute-start(f32[128,256]{1,0:T(8,128)S(1)} %fusion.1), channel_id=1, source_target_pairs={{0,2},{1,5},{2,0},{3,7},{4,6},{5,1},{6,4},{7,3},{8,10},{9,13},{10,... | collective-permute-start | bytes 393224 | tf_op jit(solution)/shard_map/ppermute | solution.py:114
  38.2 5.8 %collective-permute-start.15 = (f32[128,256]{1,0:T(8,128)S(1)}, f32[128,256]{1,0:T(8,128)S(1)}, u32[]{:S(2)}, u32[]{:S(2)}) collective-permute-start(f32[128,256]{1,0:T(8,128)S(1)} %get-tuple-element.9), channel_id=1, source_target_pairs={{0,2},{1,5},{2,0},{3,7},{4,6},{5,1},{6,4},{7,3},{8,10},{9,13},{10,... | collective-permute-start | bytes 393224 | tf_op jit(solution)/shard_map/ppermute | solution.py:114
  42.7 5.0 %collective-permute-start.12 = (f32[128,256]{1,0:T(8,128)S(1)}, f32[128,256]{1,0:T(8,128)S(1)}, u32[]{:S(2)}, u32[]{:S(2)}) collective-permute-start(f32[128,256]{1,0:T(8,128)S(1)} %add.51), channel_id=1, source_target_pairs={{0,8},{1,9},{2,10},{3,11},{4,12},{5,13},{6,14},{7,15},{8,0},{9,1},... | collective-permute-start | bytes 393224 | tf_op jit(solution)/shard_map/ppermute | solution.py:114
  44.1 4.3 %collective-permute-start.16 = (f32[128,256]{1,0:T(8,128)S(1)}, f32[128,256]{1,0:T(8,128)S(1)}, u32[]{:S(2)}, u32[]{:S(2)}) collective-permute-start(f32[128,256]{1,0:T(8,128)S(1)} %collective-permute-done.15), channel_id=1, source_target_pairs={{0,0},{1,3},{2,2},{3,1},{4,4},{5,7},{6,6},{7,5},{8,8},{9,11},{10,1... | collective-permute-start | bytes 393224 | tf_op jit(solution)/shard_map/ppermute | solution.py:114
  47.7 1.0 %collective-permute-start.13 = (f32[128,256]{1,0:T(8,128)S(1)}, f32[128,256]{1,0:T(8,128)S(1)}, u32[]{:S(2)}, u32[]{:S(2)}) collective-permute-start(f32[128,256]{1,0:T(8,128)S(1)} %add_select_fusion.1), channel_id=1, source_target_pairs={{0,0},{1,17},{2,2},{3,19},{4,4},{5,21},{6,6},{7,23},{8,8},{9,25},{... | collective-permute-start | bytes 393224 | tf_op jit(solution)/shard_map/ppermute | solution.py:114
  48.5 4.3 %collective-permute-start.17 = (f32[128,256]{1,0:T(8,128)S(1)}, f32[128,256]{1,0:T(8,128)S(1)}, u32[]{:S(2)}, u32[]{:S(2)}) collective-permute-start(f32[128,256]{1,0:T(8,128)S(1)} %add_select_fusion.own_ref), channel_id=1, source_target_pairs={{0,1},{1,0},{2,3},{3,2},{4,5},{5,4},{6,7},{7,6},{8,9},{9,8},{10,11... | collective-permute-start | bytes 393224 | tf_op jit(solution)/shard_map/ppermute | solution.py:114
  48.8 5.3 %collective-permute-start.14 = (f32[128,256]{1,0:T(8,128)S(1)}, f32[128,256]{1,0:T(8,128)S(1)}, u32[]{:S(2)}, u32[]{:S(2)}) collective-permute-start(f32[128,256]{1,0:T(8,128)S(1)} %collective-permute-done.13.own_ref), channel_id=1, source_target_pairs={{0,1},{1,0},{2,3},{3,2},{4,5},{5,4},{6,7},{7,6},{8,9},{9,8},{10,11... | collective-permute-start | bytes 393224 | tf_op jit(solution)/shard_map/ppermute | solution.py:114
  (1 other events, 1.0 us)

commit v2 on v1

v2 whole, which is shorter than its diff:
```python
import functools
import math

import jax
import jax.numpy as jnp
from jax import lax
from jax.experimental import pallas as pl
from jax.experimental.pallas import tpu as pltpu
from jax.sharding import PartitionSpec as P

LEAF = 512
CHUNK = 256
SPAN = 128
F32 = jnp.float32
BF16 = jnp.bfloat16


VMEM = pl.BlockSpec(memory_space=pltpu.VMEM)
SMEM = pl.BlockSpec(memory_space=pltpu.SMEM)
HBM = pl.BlockSpec(memory_space=pltpu.HBM)


def call(kernel, outs, scalars, arrays, flops, arrays_in=VMEM, outs_in=VMEM, scratch=()):
    moved = sum(math.prod(a.shape) * a.dtype.itemsize for a in (*arrays, *outs))
    return pl.pallas_call(
        kernel,
        out_shape=outs,
        in_specs=[SMEM] + [arrays_in] * len(arrays),
        out_specs=[outs_in] * len(outs),
        scratch_shapes=scratch,
        compiler_params=pltpu.CompilerParams(vmem_limit_bytes=24 * 2**20),
        cost_estimate=pl.CostEstimate(flops=flops, bytes_accessed=moved, transcendentals=0),
    )(scalars, *arrays)


def transposed_dot(basis, vec):
    return lax.dot_general(basis, vec, (((0,), (0,)), ((), ())), preferred_element_type=F32)


def first_kernel(ids_ref, bases_ref, vec_ref, out_ref, bases_buf, vec_buf, sems):
    parity = ids_ref[0]
    rank = bases_ref.shape[2]
    copies = []
    for chunk in range(vec_ref.shape[0] // CHUNK):
        rows = pl.ds(chunk * CHUNK, CHUNK)
        own = [pltpu.make_async_copy(vec_ref.at[rows, :], vec_buf.at[rows, :], sems.at[chunk, 0])]
        for slot in range(2):
            source = bases_ref.at[parity + 2 * slot, rows, :]
            target = bases_buf.at[rows, pl.ds(slot * rank, rank)]
            own.append(pltpu.make_async_copy(source, target, sems.at[chunk, 1 + slot]))
        for copy in own:
            copy.start()
        copies.append(own)
    total = None
    for chunk, own in enumerate(copies):
        for copy in own:
            copy.wait()
        rows = slice(chunk * CHUNK, (chunk + 1) * CHUNK)
        term = transposed_dot(bases_buf[rows, :], vec_buf[rows, :])
        total = term if total is None else total + term
    out_ref[0] = total[:rank]
    out_ref[1] = total[rank:]


def kept_kernel(ids_ref, bases_ref, vec_ref, high_ref, low_ref):
    other = 1 - ids_ref[0]
    rank = bases_ref.shape[2]
    both = jnp.concatenate([bases_ref[other], bases_ref[other + 2]], axis=1)
    proj = transposed_dot(both, vec_ref[...])
    high_ref[...] = proj[:rank]
    low_ref[...] = proj[rank:]


def prepare_kernel(ids_ref, couplings_ref, bases_ref, oriented_ref, turned_ref):
    for level in range(bases_ref.shape[0]):
        coupling = couplings_ref[ids_ref[1 + level]].astype(F32)
        oriented_ref[level] = jnp.where(ids_ref[5 + level] == 0, coupling, coupling.T).astype(BF16)
        turned_ref[level] = bases_ref[level].T


def coefficients(ids_ref, oriented_ref, level, own, other, factors):
    odd = ids_ref[0] == 1
    pieces = []
    for step, sums in enumerate((jnp.where(odd, own, other), jnp.where(odd, other, own))):
        quotient = (sums * factors[level + step]).astype(BF16)
        coeffs = jnp.dot(oriented_ref[level + step], quotient, preferred_element_type=F32)
        pieces.append(coeffs.astype(BF16))
    return jnp.concatenate(pieces, axis=0)


def expanded(bases_ref, level, rows, coeffs):
    basis = jnp.concatenate([bases_ref[level, rows, :], bases_ref[level + 1, rows, :]], axis=1)
    return jnp.dot(basis, coeffs, preferred_element_type=F32)


def local_kernel(factors, ids_ref, oriented_ref, own_ref, other_ref, bases_ref, leaves_ref, vec_ref, part_ref):
    coeffs = coefficients(ids_ref, oriented_ref, 2, own_ref[...], other_ref[...], factors)
    for leaf in range(vec_ref.shape[0] // LEAF):
        rows = pl.ds(leaf * LEAF, LEAF)
        near = jnp.dot(leaves_ref[rows, :], vec_ref[rows, :], preferred_element_type=F32)
        part_ref[rows, :] = near + expanded(bases_ref, 2, rows, coeffs)


def scale_kernel(
    factors, ids_ref, oriented_ref, own_ref, other_ref, bases_ref, part_ref, turned_ref, weights_ref, scaled_ref, send_ref
):
    coeffs = coefficients(ids_ref, oriented_ref, 0, own_ref[...], other_ref[...], factors)
    columns = weights_ref[...].T
    parity = ids_ref[0]
    rank = bases_ref.shape[2]
    total = None
    for chunk in range(part_ref.shape[0] // CHUNK):
        rows = pl.ds(chunk * CHUNK, CHUNK)
        first = part_ref[rows, :] + expanded(bases_ref, 0, rows, coeffs)
        blocks = range(chunk * CHUNK // SPAN, (chunk + 1) * CHUNK // SPAN)
        column = jnp.concatenate([columns[:, block : block + 1] for block in blocks], axis=0)
        scaled = (column * first).astype(BF16)
        scaled_ref[rows, :] = scaled
        turned = jnp.concatenate([turned_ref[parity, :, rows], turned_ref[parity + 2, :, rows]], axis=0)
        term = jnp.dot(turned, scaled, preferred_element_type=F32)
        total = term if total is None else total + term
    send_ref[0] = total[:rank]
    send_ref[1] = total[rank:]


def kept_again_kernel(ids_ref, turned_ref, vec_ref, high_ref, low_ref):
    other = 1 - ids_ref[0]
    vec = vec_ref[...]
    high_ref[...] = jnp.dot(turned_ref[other], vec, preferred_element_type=F32)
    low_ref[...] = jnp.dot(turned_ref[other + 2], vec, preferred_element_type=F32)


def result_kernel(factors, ids_ref, oriented_ref, own_ref, other_ref, bases_ref, part_ref, result_ref, buf, sems):
    coeffs = coefficients(ids_ref, oriented_ref, 0, own_ref[...], other_ref[...], factors)
    copies = []
    for chunk in range(part_ref.shape[0] // CHUNK):
        rows = pl.ds(chunk * CHUNK, CHUNK)
        total = part_ref[rows, :] + expanded(bases_ref, 0, rows, coeffs)
        buf[rows, :] = total.astype(BF16)
        copies.append(pltpu.make_async_copy(buf.at[rows, :], result_ref.at[rows, :], sems.at[chunk]))
        copies[-1].start()
    for copy in copies:
        copy.wait()


def on_device(signal, leaves, bases, couplings, weights):
    count = lax.axis_size("rows")
    bits = count.bit_length() - 1
    myself = lax.axis_index("rows")
    rows_dev, width = signal.shape
    levels, _, rank = bases.shape
    odd = myself % 2 == 1
    far1, far2, far3, far4 = (1 << (bits - level - 1) for level in range(levels))
    factors = [1.0 / math.sqrt(rows_dev * (count >> level + 1) * rank) for level in range(levels)]
    ids = jnp.stack(
        [myself % 2]
        + [(1 << level) - 1 + (myself >> bits - level) for level in range(levels)]
        + [myself >> bits - level - 1 & 1 for level in range(levels)]
    ).astype(jnp.int32)
    weight_rows = weights.reshape(rows_dev // SPAN, SPAN)
    mults = rows_dev * width * rank * 2
    chunks = rows_dev // CHUNK
    sums_shape = jax.ShapeDtypeStruct((rank, width), F32)
    pair_shape = jax.ShapeDtypeStruct((2, rank, width), F32)
    part_shape = jax.ShapeDtypeStruct((rows_dev, width), F32)
    vec_shape = jax.ShapeDtypeStruct((rows_dev, width), BF16)

    def swap(value, odd_mask, even_mask):
        pairs = [(source, source ^ (odd_mask if source % 2 else even_mask)) for source in range(count)]
        return lax.ppermute(value, "rows", pairs)

    def siblings(send, high, low):
        got = swap(send, 1, 1)
        high = high + got[0]
        low = low + got[1]
        for bit in range(1, bits - levels):
            high = high + swap(high, 1 << bit, 1 << bit)
            low = low + swap(low, 1 << bit, 1 << bit)
        near = swap(high, far1, far2)
        across = swap(high, far1 | far2, far4)
        high = jnp.where(odd, near + across, near)
        low = swap(low, far3, far4)
        high = high + swap(high, far4, far3)
        low = jnp.where(odd, low + swap(low, far4, far4), low)
        high = high + swap(high, far3, far4)
        return (high, swap(high, 1, 1)), (low, swap(low, 1, 1))

    def local(vec, low):
        (part,) = call(
            functools.partial(local_kernel, factors),
            [part_shape],
            ids,
            [oriented, *low, bases, leaves, vec],
            (2 + LEAF // rank) * mults,
        )
        return part

    (send,) = call(
        first_kernel,
        [pair_shape],
        ids,
        [pltpu.with_memory_space_constraint(array, pltpu.HBM) for array in (bases, signal)],
        2 * mults,
        arrays_in=HBM,
        scratch=[
            pltpu.VMEM((rows_dev, 2 * rank), BF16),
            pltpu.VMEM((rows_dev, width), BF16),
            pltpu.SemaphoreType.DMA((chunks, 3)),
        ],
    )
    kept = call(kept_kernel, [sums_shape] * 2, ids, [bases, signal], 2 * mults)
    oriented, turned = call(
        prepare_kernel,
        [
            jax.ShapeDtypeStruct((levels, rank, rank), BF16),
            jax.ShapeDtypeStruct((levels, rank, rows_dev), BF16),
        ],
        ids,
        [couplings, bases],
        mults,
    )
    high, low = siblings(send, *kept)
    scaled, send = call(
        functools.partial(scale_kernel, factors),
        [vec_shape, pair_shape],
        ids,
        [oriented, *high, bases, local(signal, low), turned, weight_rows],
        4 * mults,
    )
    kept = call(kept_again_kernel, [sums_shape] * 2, ids, [turned, scaled], 2 * mults)
    high, low = siblings(send, *kept)
    (result,) = call(
        functools.partial(result_kernel, factors),
        [vec_shape],
        ids,
        [oriented, *high, bases, local(scaled, low)],
        2 * mults,
        outs_in=HBM,
        scratch=[pltpu.VMEM((rows_dev, width), BF16), pltpu.SemaphoreType.DMA((chunks,))],
    )
    return result


def solution(mesh):
    in_specs = (P("rows", None), P("rows", None), P(None, "rows", None), P(), P("rows"))
    out_specs = P("rows", None)
    return jax.shard_map(
        on_device, mesh=mesh, in_specs=in_specs, out_specs=out_specs, check_vma=False
    )
```

time: 56.2 us -> 51.6 us (0.918)
  starting transfers between devices: 25.1 us -> 16.6 us
  waiting for transfers between devices: 18.8 us -> 23.5 us
  local copies, waits for them, and re-layouts: 3.07 us -> 0.11 us
  Pallas kernels: 8.61 us -> 10.8 us
    ppermute x18, starting transfers between devices: 25.1 us -> 16.6 us  [swap(): return lax.ppermute(value, 'rows', pairs)]
    ppermute x18, waiting for transfers between devices: 18.8 us -> 23.5 us  [swap(): return lax.ppermute(value, 'rows', pairs)]
    unnamed x14 -> x10, local copies, waits for them, and re-layouts: 2.29 us -> 0.03 us
    pallas_call x7 -> x8, Pallas kernels: 8.61 us -> 10.8 us  [call(): pl.pallas_call(kernel, out_shape=outs, in_specs=[SMEM] + [arrays_in] * le...]
    squeeze x2 -> x0, local copies, waits for them, and re-layouts: 0.69 us -> none  [siblings(): high, low = (sums[0], sums[1])]
  transfers between devices with their start and end apart: 18 -> 18, of which waited for: 9 -> 12; matrix products, arithmetic and copies ran while one was open for 0% -> 0% of each run, Pallas kernels for 8% -> 10%
where the time goes in v2:
time: 51.6 us; the launch traced here: 51.4 us
  waiting for transfers between devices  23.5 us (46%)
  starting transfers between devices  16.6 us (32%)
  Pallas kernels  10.8 us (21%)
    ppermute x18, waiting for transfers between devices, swap(): return lax.ppermute(value, 'rows', pairs)  23.5 us
    ppermute x18, starting transfers between devices, swap(): return lax.ppermute(value, 'rows', pairs)  16.6 us
    pallas_call x8, Pallas kernels, call(): pl.pallas_call(kernel, out_shape=outs, in_specs=[SMEM] + [arrays_in] * le...  10.8 us
  transfers between devices with their start and end apart: 18, of which 12 were waited for; matrix products, arithmetic and copies ran while one was open for 0% of the time, Pallas kernels for 10%

profile of v2, /device:TPU:0, one launch (start us, length us, event | category | flops | bytes accessed | tf_op | source)
XLA Modules:
  0.0 51.4 jit_solution(11692853185036556684)
XLA Ops:
  0.1 2.4 %shard_map.57 = f32[2,128,256]{2,1,0:T(8,128)S(1)} custom-call(s32[9]{0:T(128)S(1)} %stack.39.ids_ref, bf16[4,1024,128]{2,1,0:T(8,128)(2,1)} %bases_ref.13, bf16[1024,256]{1,0:T(8,128)(2,1)} %vec_ref.5), custom_call_target="tpu_custom_call" | custom-call | flops 134217728 | bytes 1835008 | tf_op jit(solution)/shard_map/pallas_call | solution.py:25
  3.0 0.9 %shard_map.56 = (f32[128,256]{1,0:T(8,128)S(1)}, f32[128,256]{1,0:T(8,128)S(1)}) custom-call(s32[9]{0:T(128)S(1)} %stack.39.ids_ref, bf16[4,1024,128]{2,1,0:T(8,128)(2,1)S(1)} %copy-done, bf16[1024,256]{1,0:T(8,128)(2,1)S(1)} %copy-done.1), custom_call_target="tpu_custom_call" | custom-call | flops 134217728 | bytes 1835008 | tf_op jit(solution)/shard_map/pallas_call | solution.py:25
  4.2 2.9 %collective-permute-start.2 = (f32[128,256]{1,0:T(8,128)S(1)}, f32[128,256]{1,0:T(8,128)S(1)}, u32[]{:S(2)}, u32[]{:S(2)}) collective-permute-start(f32[128,256]{1,0:T(8,128)S(1)} %get-tuple-element.24), channel_id=1, source_target_pairs={{0,2},{1,25},{2,0},{3,27},{4,6},{5,29},{6,4},{7,31},{8,10},{9,17},... | collective-permute-start | bytes 393224 | tf_op jit(solution)/shard_map/ppermute | solution.py:170
  7.1 1.6 %collective-permute-start.1 = (f32[128,256]{1,0:T(8,128)S(1)}, f32[128,256]{1,0:T(8,128)S(1)}, u32[]{:S(2)}, u32[]{:S(2)}) collective-permute-start(f32[128,256]{1,0:T(8,128)S(1)} %get-tuple-element.24), channel_id=1, source_target_pairs={{0,8},{1,17},{2,10},{3,19},{4,12},{5,21},{6,14},{7,23},{8,0},{9,25... | collective-permute-start | bytes 393224 | tf_op jit(solution)/shard_map/ppermute | solution.py:170
  10.1 3.1 %collective-permute-done.1 = f32[128,256]{1,0:T(8,128)S(1)} collective-permute-done((f32[128,256]{1,0:T(8,128)S(1)}, f32[128,256]{1,0:T(8,128)S(1)}, u32[]{:S(2)}, u32[]{:S(2)}) %collective-permute-start.1) | collective-permute-done | bytes 131104 | tf_op jit(solution)/shard_map/ppermute | solution.py:170
  13.2 1.6 %collective-permute-start.3 = (f32[128,256]{1,0:T(8,128)S(1)}, f32[128,256]{1,0:T(8,128)S(1)}, u32[]{:S(2)}, u32[]{:S(2)}) collective-permute-start(f32[128,256]{1,0:T(8,128)S(1)} %add_select_fusion.3), channel_id=1, source_target_pairs={{0,4},{1,3},{2,6},{3,1},{4,0},{5,7},{6,2},{7,5},{8,12},{9,11},{10,... | collective-permute-start | bytes 393224 | tf_op jit(solution)/shard_map/ppermute | solution.py:170
  14.7 0.9 %collective-permute-start.7 = (f32[128,256]{1,0:T(8,128)S(1)}, f32[128,256]{1,0:T(8,128)S(1)}, u32[]{:S(2)}, u32[]{:S(2)}) collective-permute-start(f32[128,256]{1,0:T(8,128)S(1)} %collective-permute-done.6), channel_id=1, source_target_pairs={{0,2},{1,3},{2,0},{3,1},{4,6},{5,7},{6,4},{7,5},{8,10},{9,11},{10,... | collective-permute-start | bytes 393224 | tf_op jit(solution)/shard_map/ppermute | solution.py:170
  15.6 2.5 %collective-permute-done.3 = f32[128,256]{1,0:T(8,128)S(1)} collective-permute-done((f32[128,256]{1,0:T(8,128)S(1)}, f32[128,256]{1,0:T(8,128)S(1)}, u32[]{:S(2)}, u32[]{:S(2)}) %collective-permute-start.3) | collective-permute-done | bytes 131104 | tf_op jit(solution)/shard_map/ppermute | solution.py:170
  18.7 2.3 %collective-permute-done.7 = f32[128,256]{1,0:T(8,128)S(1)} collective-permute-done((f32[128,256]{1,0:T(8,128)S(1)}, f32[128,256]{1,0:T(8,128)S(1)}, u32[]{:S(2)}, u32[]{:S(2)}) %collective-permute-start.7) | collective-permute-done | bytes 131104 | tf_op jit(solution)/shard_map/ppermute | solution.py:170
  21.8 1.5 %collective-permute-done.4 = f32[128,256]{1,0:T(8,128)S(1)} collective-permute-done((f32[128,256]{1,0:T(8,128)S(1)}, f32[128,256]{1,0:T(8,128)S(1)}, u32[]{:S(2)}, u32[]{:S(2)}) %collective-permute-start.4) | collective-permute-done | bytes 131104 | tf_op jit(solution)/shard_map/ppermute | solution.py:170
  23.8 0.9 %shard_map.55 = (bf16[4,128,128]{2,1,0:T(8,128)(2,1)S(1)}, bf16[4,128,1024]{2,1,0:T(8,128)(2,1)S(1)}) custom-call(s32[9]{0:T(128)S(1)} %stack.39.ids_ref, bf16[15,128,128]{2,1,0:T(8,128)(2,1)S(1)} %copy-done.3, bf16[4,1024,128]{2,1,0:T(8,128)(2,1)S(1)} %copy-done), custom_call_target="tpu_custom_call" | custom-call | flops 67108864 | bytes 2719744 | tf_op jit(solution)/shard_map/pallas_call | solution.py:25
  24.8 1.3 %shard_map.58.part_ref = f32[1024,256]{1,0:T(8,128)S(1)} custom-call(s32[9]{0:T(128)S(1)} %stack.39.ids_ref, bf16[4,128,128]{2,1,0:T(8,128)(2,1)S(1)} %get-tuple-element.13.oriented_ref, f32[128,256]{1,0:T(8,128)S(1)} %add_select_fusion.2.own_ref, f32[128,256]{1,0:T(8,128)S(1)} %collective-permute-done.8.other_ref, bf16[4,1024,128]{2,1,0:T(8,128)(2,1)S(1)} %copy-done, ...), custom_call_target="tpu_custom_call" | custom-call | flops 402653184 | bytes 4063232 | tf_op jit(solution)/shard_map/pallas_call | solution.py:25
  26.1 1.4 %shard_map.59 = (bf16[1024,256]{1,0:T(8,128)(2,1)S(1)}, f32[2,128,256]{2,1,0:T(8,128)S(1)}) custom-call(s32[9]{0:T(128)S(1)} %stack.39.ids_ref, bf16[4,128,128]{2,1,0:T(8,128)(2,1)S(1)} %get-tuple-element.13.oriented_ref, f32[128,256]{1,0:T(8,128)S(1)} %add.53.own_ref, f32[128,256]{1,0:T(8,128)S(1)} %collective-permute-done.5.other_ref, ...), custom_call_target="tpu_custom_call" | custom-call | flops 268435456 | bytes 4329472 | tf_op jit(solution)/shard_map/pallas_call | solution.py:25
  29.1 2.0 %collective-permute-start.11 = (f32[128,256]{1,0:T(8,128)S(1)}, f32[128,256]{1,0:T(8,128)S(1)}, u32[]{:S(2)}, u32[]{:S(2)}) collective-permute-start(f32[128,256]{1,0:T(8,128)S(1)} %get-tuple-element.22), channel_id=1, source_target_pairs={{0,2},{1,25},{2,0},{3,27},{4,6},{5,29},{6,4},{7,31},{8,10},{9,17},... | collective-permute-start | bytes 393224 | tf_op jit(solution)/shard_map/ppermute | solution.py:170
  31.1 1.8 %collective-permute-start.15 = (f32[128,256]{1,0:T(8,128)S(1)}, f32[128,256]{1,0:T(8,128)S(1)}, u32[]{:S(2)}, u32[]{:S(2)}) collective-permute-start(f32[128,256]{1,0:T(8,128)S(1)} %get-tuple-element.21), channel_id=1, source_target_pairs={{0,2},{1,5},{2,0},{3,7},{4,6},{5,1},{6,4},{7,3},{8,10},{9,13},{10,... | collective-permute-start | bytes 393224 | tf_op jit(solution)/shard_map/ppermute | solution.py:170
  32.8 1.3 %collective-permute-done.11 = f32[128,256]{1,0:T(8,128)S(1)} collective-permute-done((f32[128,256]{1,0:T(8,128)S(1)}, f32[128,256]{1,0:T(8,128)S(1)}, u32[]{:S(2)}, u32[]{:S(2)}) %collective-permute-start.11) | collective-permute-done | bytes 131104 | tf_op jit(solution)/shard_map/ppermute | solution.py:170
  34.2 3.7 %collective-permute-done.10 = f32[128,256]{1,0:T(8,128)S(1)} collective-permute-done((f32[128,256]{1,0:T(8,128)S(1)}, f32[128,256]{1,0:T(8,128)S(1)}, u32[]{:S(2)}, u32[]{:S(2)}) %collective-permute-start.10) | collective-permute-done | bytes 131104 | tf_op jit(solution)/shard_map/ppermute | solution.py:170
  38.0 1.4 %collective-permute-start.16 = (f32[128,256]{1,0:T(8,128)S(1)}, f32[128,256]{1,0:T(8,128)S(1)}, u32[]{:S(2)}, u32[]{:S(2)}) collective-permute-start(f32[128,256]{1,0:T(8,128)S(1)} %collective-permute-done.15), channel_id=1, source_target_pairs={{0,2},{1,3},{2,0},{3,1},{4,6},{5,7},{6,4},{7,5},{8,10},{9,11},{10,... | collective-permute-start | bytes 393224 | tf_op jit(solution)/shard_map/ppermute | solution.py:170
  39.4 3.5 %collective-permute-done.12 = f32[128,256]{1,0:T(8,128)S(1)} collective-permute-done((f32[128,256]{1,0:T(8,128)S(1)}, f32[128,256]{1,0:T(8,128)S(1)}, u32[]{:S(2)}, u32[]{:S(2)}) %collective-permute-start.12) | collective-permute-done | bytes 131104 | tf_op jit(solution)/shard_map/ppermute | solution.py:170
  43.0 1.4 %collective-permute-done.16 = f32[128,256]{1,0:T(8,128)S(1)} collective-permute-done((f32[128,256]{1,0:T(8,128)S(1)}, f32[128,256]{1,0:T(8,128)S(1)}, u32[]{:S(2)}, u32[]{:S(2)}) %collective-permute-start.16) | collective-permute-done | bytes 131104 | tf_op jit(solution)/shard_map/ppermute | solution.py:170
  44.5 1.2 %collective-permute-start.17 = (f32[128,256]{1,0:T(8,128)S(1)}, f32[128,256]{1,0:T(8,128)S(1)}, u32[]{:S(2)}, u32[]{:S(2)}) collective-permute-start(f32[128,256]{1,0:T(8,128)S(1)} %add_select_fusion.own_ref), channel_id=1, source_target_pairs={{0,1},{1,0},{2,3},{3,2},{4,5},{5,4},{6,7},{7,6},{8,9},{9,8},{10,11... | collective-permute-start | bytes 393224 | tf_op jit(solution)/shard_map/ppermute | solution.py:170
  45.7 2.3 %collective-permute-done.13 = f32[128,256]{1,0:T(8,128)S(1)} collective-permute-done((f32[128,256]{1,0:T(8,128)S(1)}, f32[128,256]{1,0:T(8,128)S(1)}, u32[]{:S(2)}, u32[]{:S(2)}) %collective-permute-start.13) | collective-permute-done | bytes 131104 | tf_op jit(solution)/shard_map/ppermute | solution.py:170
  48.4 1.3 %shard_map.61.part_ref = f32[1024,256]{1,0:T(8,128)S(1)} custom-call(s32[9]{0:T(128)S(1)} %stack.39.ids_ref, bf16[4,128,128]{2,1,0:T(8,128)(2,1)S(1)} %get-tuple-element.13.oriented_ref, f32[128,256]{1,0:T(8,128)S(1)} %add_select_fusion.own_ref, f32[128,256]{1,0:T(8,128)S(1)} %collective-permute-done.17.other_ref, bf16[4,1024,128]{2,1,0:T(8,128)(2,1)S(1)} %copy-done, ...), custom_call_target="tpu_custom_call" | custom-call | flops 402653184 | bytes 4063232 | tf_op jit(solution)/shard_map/pallas_call | solution.py:25
  49.7 1.8 %shard_map.62 = bf16[1024,256]{1,0:T(8,128)(2,1)} custom-call(s32[9]{0:T(128)S(1)} %stack.39.ids_ref, bf16[4,128,128]{2,1,0:T(8,128)(2,1)S(1)} %get-tuple-element.13.oriented_ref, f32[128,256]{1,0:T(8,128)S(1)} %add.59.own_ref, f32[128,256]{1,0:T(8,128)S(1)} %collective-permute-done.14.other_ref, bf16[4,1024,128]{2,1,0:T(8,128)(2,1)S(1)} %copy-done, ...), custom_call_target="tpu_custom_call" | custom-call | flops 134217728 | bytes 3014656 | tf_op jit(solution)/shard_map/pallas_call | solution.py:25
  (41 shorter events, 6.2 us)
Async XLA Ops:
  0.0 3.0 %copy-start = (bf16[4,1024,128]{2,1,0:T(8,128)(2,1)S(1)}, bf16[4,1024,128]{2,1,0:T(8,128)(2,1)}, u32[]{:S(2)}) copy-start(bf16[4,1024,128]{2,1,0:T(8,128)(2,1)} %bases_ref.13) | copy-start | bytes 3145732
  0.1 2.9 %copy-start.1 = (bf16[1024,256]{1,0:T(8,128)(2,1)S(1)}, bf16[1024,256]{1,0:T(8,128)(2,1)}, u32[]{:S(2)}) copy-start(bf16[1024,256]{1,0:T(8,128)(2,1)} %vec_ref.5) | copy-start | bytes 1572868
  2.5 1.7 %collective-permute-start = (f32[2,128,256]{2,1,0:T(8,128)S(1)}, f32[2,128,256]{2,1,0:T(8,128)S(1)}, u32[]{:S(2)}, u32[]{:S(2)}) collective-permute-start(f32[2,128,256]{2,1,0:T(8,128)S(1)} %shard_map.57), channel_id=1, source_target_pairs={{0,1},{1,0},{2,3},{3,2},{4,5},{5,4},{6,7},{7,6},{8,9},{9,8},{10,11... | collective-permute-start | bytes 786440 | tf_op jit(solution)/shard_map/ppermute | solution.py:170
  4.2 5.9 %collective-permute-start.2 = (f32[128,256]{1,0:T(8,128)S(1)}, f32[128,256]{1,0:T(8,128)S(1)}, u32[]{:S(2)}, u32[]{:S(2)}) collective-permute-start(f32[128,256]{1,0:T(8,128)S(1)} %get-tuple-element.24), channel_id=1, source_target_pairs={{0,2},{1,25},{2,0},{3,27},{4,6},{5,29},{6,4},{7,31},{8,10},{9,17},... | collective-permute-start | bytes 393224 | tf_op jit(solution)/shard_map/ppermute | solution.py:170
  7.1 6.0 %collective-permute-start.1 = (f32[128,256]{1,0:T(8,128)S(1)}, f32[128,256]{1,0:T(8,128)S(1)}, u32[]{:S(2)}, u32[]{:S(2)}) collective-permute-start(f32[128,256]{1,0:T(8,128)S(1)} %get-tuple-element.24), channel_id=1, source_target_pairs={{0,8},{1,17},{2,10},{3,19},{4,12},{5,21},{6,14},{7,23},{8,0},{9,25... | collective-permute-start | bytes 393224 | tf_op jit(solution)/shard_map/ppermute | solution.py:170
  8.7 6.0 %collective-permute-start.6 = (f32[128,256]{1,0:T(8,128)S(1)}, f32[128,256]{1,0:T(8,128)S(1)}, u32[]{:S(2)}, u32[]{:S(2)}) collective-permute-start(f32[128,256]{1,0:T(8,128)S(1)} %get-tuple-element.23), channel_id=1, source_target_pairs={{0,2},{1,5},{2,0},{3,7},{4,6},{5,1},{6,4},{7,3},{8,10},{9,13},{10,... | collective-permute-start | bytes 393224 | tf_op jit(solution)/shard_map/ppermute | solution.py:170
  13.2 5.0 %collective-permute-start.3 = (f32[128,256]{1,0:T(8,128)S(1)}, f32[128,256]{1,0:T(8,128)S(1)}, u32[]{:S(2)}, u32[]{:S(2)}) collective-permute-start(f32[128,256]{1,0:T(8,128)S(1)} %add_select_fusion.3), channel_id=1, source_target_pairs={{0,4},{1,3},{2,6},{3,1},{4,0},{5,7},{6,2},{7,5},{8,12},{9,11},{10,... | collective-permute-start | bytes 393224 | tf_op jit(solution)/shard_map/ppermute | solution.py:170
  14.7 6.3 %collective-permute-start.7 = (f32[128,256]{1,0:T(8,128)S(1)}, f32[128,256]{1,0:T(8,128)S(1)}, u32[]{:S(2)}, u32[]{:S(2)}) collective-permute-start(f32[128,256]{1,0:T(8,128)S(1)} %collective-permute-done.6), channel_id=1, source_target_pairs={{0,2},{1,3},{2,0},{3,1},{4,6},{5,7},{6,4},{7,5},{8,10},{9,11},{10,... | collective-permute-start | bytes 393224 | tf_op jit(solution)/shard_map/ppermute | solution.py:170
  18.2 5.6 %copy-start.3 = (bf16[15,128,128]{2,1,0:T(8,128)(2,1)S(1)}, bf16[15,128,128]{2,1,0:T(8,128)(2,1)}, u32[]{:S(2)}) copy-start(bf16[15,128,128]{2,1,0:T(8,128)(2,1)} %couplings_ref.1) | copy-start | bytes 1474564
  18.2 5.0 %collective-permute-start.4 = (f32[128,256]{1,0:T(8,128)S(1)}, f32[128,256]{1,0:T(8,128)S(1)}, u32[]{:S(2)}, u32[]{:S(2)}) collective-permute-start(f32[128,256]{1,0:T(8,128)S(1)} %add.52), channel_id=1, source_target_pairs={{0,2},{1,5},{2,0},{3,7},{4,6},{5,1},{6,4},{7,3},{8,10},{9,13},{10,... | collective-permute-start | bytes 393224 | tf_op jit(solution)/shard_map/ppermute | solution.py:170
  21.1 3.6 %copy-start.2 = (bf16[1024,512]{1,0:T(8,128)(2,1)S(1)}, bf16[1024,512]{1,0:T(8,128)(2,1)}, u32[]{:S(2)}) copy-start(bf16[1024,512]{1,0:T(8,128)(2,1)} %leaves_ref.3) | copy-start | bytes 3145732
  21.1 3.6 %collective-permute-start.8 = (f32[128,256]{1,0:T(8,128)S(1)}, f32[128,256]{1,0:T(8,128)S(1)}, u32[]{:S(2)}, u32[]{:S(2)}) collective-permute-start(f32[128,256]{1,0:T(8,128)S(1)} %add_select_fusion.2.own_ref), channel_id=1, source_target_pairs={{0,1},{1,0},{2,3},{3,2},{4,5},{5,4},{6,7},{7,6},{8,9},{9,8},{10,11... | collective-permute-start | bytes 393224 | tf_op jit(solution)/shard_map/ppermute | solution.py:170
  23.3 2.8 %collective-permute-start.5 = (f32[128,256]{1,0:T(8,128)S(1)}, f32[128,256]{1,0:T(8,128)S(1)}, u32[]{:S(2)}, u32[]{:S(2)}) collective-permute-start(f32[128,256]{1,0:T(8,128)S(1)} %add.53.own_ref), channel_id=1, source_target_pairs={{0,1},{1,0},{2,3},{3,2},{4,5},{5,4},{6,7},{7,6},{8,9},{9,8},{10,11... | collective-permute-start | bytes 393224 | tf_op jit(solution)/shard_map/ppermute | solution.py:170
  24.7 1.3 %copy-start.4 = (f32[1024]{0:T(1024)S(1)}, f32[1024]{0:T(1024)}, u32[]{:S(2)}) copy-start(f32[1024]{0:T(1024)} %param.9) | copy-start | bytes 12292
  27.5 1.6 %collective-permute-start.9 = (f32[2,128,256]{2,1,0:T(8,128)S(1)}, f32[2,128,256]{2,1,0:T(8,128)S(1)}, u32[]{:S(2)}, u32[]{:S(2)}) collective-permute-start(f32[2,128,256]{2,1,0:T(8,128)S(1)} %get-tuple-element.19), channel_id=1, source_target_pairs={{0,1},{1,0},{2,3},{3,2},{4,5},{5,4},{6,7},{7,6},{8,9},{9,8},{10,11... | collective-permute-start | bytes 786440 | tf_op jit(solution)/shard_map/ppermute | solution.py:170
  29.1 5.0 %collective-permute-start.11 = (f32[128,256]{1,0:T(8,128)S(1)}, f32[128,256]{1,0:T(8,128)S(1)}, u32[]{:S(2)}, u32[]{:S(2)}) collective-permute-start(f32[128,256]{1,0:T(8,128)S(1)} %get-tuple-element.22), channel_id=1, source_target_pairs={{0,2},{1,25},{2,0},{3,27},{4,6},{5,29},{6,4},{7,31},{8,10},{9,17},... | collective-permute-start | bytes 393224 | tf_op jit(solution)/shard_map/ppermute | solution.py:170
  31.1 6.8 %collective-permute-start.10 = (f32[128,256]{1,0:T(8,128)S(1)}, f32[128,256]{1,0:T(8,128)S(1)}, u32[]{:S(2)}, u32[]{:S(2)}) collective-permute-start(f32[128,256]{1,0:T(8,128)S(1)} %get-tuple-element.22), channel_id=1, source_target_pairs={{0,8},{1,17},{2,10},{3,19},{4,12},{5,21},{6,14},{7,23},{8,0},{9,25... | collective-permute-start | bytes 393224 | tf_op jit(solution)/shard_map/ppermute | solution.py:170
  31.1 6.9 %collective-permute-start.15 = (f32[128,256]{1,0:T(8,128)S(1)}, f32[128,256]{1,0:T(8,128)S(1)}, u32[]{:S(2)}, u32[]{:S(2)}) collective-permute-start(f32[128,256]{1,0:T(8,128)S(1)} %get-tuple-element.21), channel_id=1, source_target_pairs={{0,2},{1,5},{2,0},{3,7},{4,6},{5,1},{6,4},{7,3},{8,10},{9,13},{10,... | collective-permute-start | bytes 393224 | tf_op jit(solution)/shard_map/ppermute | solution.py:170
  37.9 5.0 %collective-permute-start.12 = (f32[128,256]{1,0:T(8,128)S(1)}, f32[128,256]{1,0:T(8,128)S(1)}, u32[]{:S(2)}, u32[]{:S(2)}) collective-permute-start(f32[128,256]{1,0:T(8,128)S(1)} %add_select_fusion.1), channel_id=1, source_target_pairs={{0,4},{1,3},{2,6},{3,1},{4,0},{5,7},{6,2},{7,5},{8,12},{9,11},{10,... | collective-permute-start | bytes 393224 | tf_op jit(solution)/shard_map/ppermute | solution.py:170
  38.0 6.4 %collective-permute-start.16 = (f32[128,256]{1,0:T(8,128)S(1)}, f32[128,256]{1,0:T(8,128)S(1)}, u32[]{:S(2)}, u32[]{:S(2)}) collective-permute-start(f32[128,256]{1,0:T(8,128)S(1)} %collective-permute-done.15), channel_id=1, source_target_pairs={{0,2},{1,3},{2,0},{3,1},{4,6},{5,7},{6,4},{7,5},{8,10},{9,11},{10,... | collective-permute-start | bytes 393224 | tf_op jit(solution)/shard_map/ppermute | solution.py:170
  43.0 5.0 %collective-permute-start.13 = (f32[128,256]{1,0:T(8,128)S(1)}, f32[128,256]{1,0:T(8,128)S(1)}, u32[]{:S(2)}, u32[]{:S(2)}) collective-permute-start(f32[128,256]{1,0:T(8,128)S(1)} %add.58), channel_id=1, source_target_pairs={{0,2},{1,5},{2,0},{3,7},{4,6},{5,1},{6,4},{7,3},{8,10},{9,13},{10,... | collective-permute-start | bytes 393224 | tf_op jit(solution)/shard_map/ppermute | solution.py:170
  44.5 3.9 %collective-permute-start.17 = (f32[128,256]{1,0:T(8,128)S(1)}, f32[128,256]{1,0:T(8,128)S(1)}, u32[]{:S(2)}, u32[]{:S(2)}) collective-permute-start(f32[128,256]{1,0:T(8,128)S(1)} %add_select_fusion.own_ref), channel_id=1, source_target_pairs={{0,1},{1,0},{2,3},{3,2},{4,5},{5,4},{6,7},{7,6},{8,9},{9,8},{10,11... | collective-permute-start | bytes 393224 | tf_op jit(solution)/shard_map/ppermute | solution.py:170
  48.0 1.6 %collective-permute-start.14 = (f32[128,256]{1,0:T(8,128)S(1)}, f32[128,256]{1,0:T(8,128)S(1)}, u32[]{:S(2)}, u32[]{:S(2)}) collective-permute-start(f32[128,256]{1,0:T(8,128)S(1)} %add.59.own_ref), channel_id=1, source_target_pairs={{0,1},{1,0},{2,3},{3,2},{4,5},{5,4},{6,7},{7,6},{8,9},{9,8},{10,11... | collective-permute-start | bytes 393224 | tf_op jit(solution)/shard_map/ppermute | solution.py:170

commit v3 on v2

--- a/solution.py
+++ b/solution.py
@@ -8,6 +8,7 @@
 from jax.experimental.pallas import tpu as pltpu
 from jax.sharding import PartitionSpec as P
 
+AXIS = "rows"
 LEAF = 512
 CHUNK = 256
 SPAN = 128
@@ -16,29 +17,32 @@
 
 
 VMEM = pl.BlockSpec(memory_space=pltpu.VMEM)
-SMEM = pl.BlockSpec(memory_space=pltpu.SMEM)
 HBM = pl.BlockSpec(memory_space=pltpu.HBM)
 
 
-def call(kernel, outs, scalars, arrays, flops, arrays_in=VMEM, outs_in=VMEM, scratch=()):
+def call(kernel, outs, arrays, flops, arrays_in=VMEM, outs_in=VMEM, scratch=()):
     moved = sum(math.prod(a.shape) * a.dtype.itemsize for a in (*arrays, *outs))
     return pl.pallas_call(
         kernel,
         out_shape=outs,
-        in_specs=[SMEM] + [arrays_in] * len(arrays),
+        in_specs=[arrays_in] * len(arrays),
         out_specs=[outs_in] * len(outs),
         scratch_shapes=scratch,
         compiler_params=pltpu.CompilerParams(vmem_limit_bytes=24 * 2**20),
         cost_estimate=pl.CostEstimate(flops=flops, bytes_accessed=moved, transcendentals=0),
-    )(scalars, *arrays)
+    )(*arrays)
+
+
+def index_bits():
+    return lax.axis_size(AXIS).bit_length() - 1
 
 
 def transposed_dot(basis, vec):
     return lax.dot_general(basis, vec, (((0,), (0,)), ((), ())), preferred_element_type=F32)
 
 
-def first_kernel(ids_ref, bases_ref, vec_ref, out_ref, bases_buf, vec_buf, sems):
-    parity = ids_ref[0]
+def first_kernel(bases_ref, vec_ref, out_ref, bases_buf, vec_buf, sems):
+    parity = lax.axis_index(AXIS) % 2
     rank = bases_ref.shape[2]
     copies = []
     for chunk in range(vec_ref.shape[0] // CHUNK):
@@ -62,8 +66,8 @@
     out_ref[1] = total[rank:]
 
 
-def kept_kernel(ids_ref, bases_ref, vec_ref, high_ref, low_ref):
-    other = 1 - ids_ref[0]
+def kept_kernel(bases_ref, vec_ref, high_ref, low_ref):
+    other = 1 - lax.axis_index(AXIS) % 2
     rank = bases_ref.shape[2]
     both = jnp.concatenate([bases_ref[other], bases_ref[other + 2]], axis=1)
     proj = transposed_dot(both, vec_ref[...])
@@ -71,15 +75,18 @@
     low_ref[...] = proj[rank:]
 
 
-def prepare_kernel(ids_ref, couplings_ref, bases_ref, oriented_ref, turned_ref):
+def prepare_kernel(couplings_ref, bases_ref, oriented_ref, turned_ref):
+    myself = lax.axis_index(AXIS)
+    bits = index_bits()
     for level in range(bases_ref.shape[0]):
-        coupling = couplings_ref[ids_ref[1 + level]].astype(F32)
-        oriented_ref[level] = jnp.where(ids_ref[5 + level] == 0, coupling, coupling.T).astype(BF16)
+        coupling = couplings_ref[(1 << level) - 1 + (myself >> bits - level)].astype(F32)
+        side = myself >> bits - level - 1 & 1
+        oriented_ref[level] = jnp.where(side == 0, coupling, coupling.T).astype(BF16)
         turned_ref[level] = bases_ref[level].T
 
 
-def coefficients(ids_ref, oriented_ref, level, own, other, factors):
-    odd = ids_ref[0] == 1
+def coefficients(oriented_ref, level, own, other, factors):
+    odd = lax.axis_index(AXIS) % 2 == 1
     pieces = []
     for step, sums in enumerate((jnp.where(odd, own, other), jnp.where(odd, other, own))):
         quotient = (sums * factors[level + step]).astype(BF16)
@@ -93,8 +100,8 @@
     return jnp.dot(basis, coeffs, preferred_element_type=F32)
 
 
-def local_kernel(factors, ids_ref, oriented_ref, own_ref, other_ref, bases_ref, leaves_ref, vec_ref, part_ref):
-    coeffs = coefficients(ids_ref, oriented_ref, 2, own_ref[...], other_ref[...], factors)
+def local_kernel(factors, oriented_ref, own_ref, other_ref, bases_ref, leaves_ref, vec_ref, part_ref):
+    coeffs = coefficients(oriented_ref, 2, own_ref[...], other_ref[...], factors)
     for leaf in range(vec_ref.shape[0] // LEAF):
         rows = pl.ds(leaf * LEAF, LEAF)
         near = jnp.dot(leaves_ref[rows, :], vec_ref[rows, :], preferred_element_type=F32)
@@ -102,11 +109,11 @@
 
 
 def scale_kernel(
-    factors, ids_ref, oriented_ref, own_ref, other_ref, bases_ref, part_ref, turned_ref, weights_ref, scaled_ref, send_ref
+    factors, oriented_ref, own_ref, other_ref, bases_ref, part_ref, turned_ref, weights_ref, scaled_ref, send_ref
 ):
-    coeffs = coefficients(ids_ref, oriented_ref, 0, own_ref[...], other_ref[...], factors)
+    coeffs = coefficients(oriented_ref, 0, own_ref[...], other_ref[...], factors)
     columns = weights_ref[...].T
-    parity = ids_ref[0]
+    parity = lax.axis_index(AXIS) % 2
     rank = bases_ref.shape[2]
     total = None
     for chunk in range(part_ref.shape[0] // CHUNK):
@@ -123,15 +130,15 @@
     send_ref[1] = total[rank:]
 
 
-def kept_again_kernel(ids_ref, turned_ref, vec_ref, high_ref, low_ref):
-    other = 1 - ids_ref[0]
+def kept_again_kernel(turned_ref, vec_ref, high_ref, low_ref):
+    other = 1 - lax.axis_index(AXIS) % 2
     vec = vec_ref[...]
     high_ref[...] = jnp.dot(turned_ref[other], vec, preferred_element_type=F32)
     low_ref[...] = jnp.dot(turned_ref[other + 2], vec, preferred_element_type=F32)
 
 
-def result_kernel(factors, ids_ref, oriented_ref, own_ref, other_ref, bases_ref, part_ref, result_ref, buf, sems):
-    coeffs = coefficients(ids_ref, oriented_ref, 0, own_ref[...], other_ref[...], factors)
+def result_kernel(factors, oriented_ref, own_ref, other_ref, bases_ref, part_ref, result_ref, buf, sems):
+    coeffs = coefficients(oriented_ref, 0, own_ref[...], other_ref[...], factors)
     copies = []
     for chunk in range(part_ref.shape[0] // CHUNK):
         rows = pl.ds(chunk * CHUNK, CHUNK)
@@ -144,19 +151,13 @@
 
 
 def on_device(signal, leaves, bases, couplings, weights):
-    count = lax.axis_size("rows")
-    bits = count.bit_length() - 1
-    myself = lax.axis_index("rows")
+    count = lax.axis_size(AXIS)
+    bits = index_bits()
     rows_dev, width = signal.shape
     levels, _, rank = bases.shape
-    odd = myself % 2 == 1
+    odd = lax.axis_index(AXIS) % 2 == 1
     far1, far2, far3, far4 = (1 << (bits - level - 1) for level in range(levels))
     factors = [1.0 / math.sqrt(rows_dev * (count >> level + 1) * rank) for level in range(levels)]
-    ids = jnp.stack(
-        [myself % 2]
-        + [(1 << level) - 1 + (myself >> bits - level) for level in range(levels)]
-        + [myself >> bits - level - 1 & 1 for level in range(levels)]
-    ).astype(jnp.int32)
     weight_rows = weights.reshape(rows_dev // SPAN, SPAN)
     mults = rows_dev * width * rank * 2
     chunks = rows_dev // CHUNK
@@ -167,9 +168,9 @@
 
     def swap(value, odd_mask, even_mask):
         pairs = [(source, source ^ (odd_mask if source % 2 else even_mask)) for source in range(count)]
-        return lax.ppermute(value, "rows", pairs)
-
-    def siblings(send, high, low):
+        return lax.ppermute(value, AXIS, pairs)
+
+    def siblings(send, high, low, riders=()):
         got = swap(send, 1, 1)
         high = high + got[0]
         low = low + got[1]
@@ -178,19 +179,19 @@
             low = low + swap(low, 1 << bit, 1 << bit)
         near = swap(high, far1, far2)
         across = swap(high, far1 | far2, far4)
+        near, across, *riders = lax.optimization_barrier((near, across, *riders))
         high = jnp.where(odd, near + across, near)
         low = swap(low, far3, far4)
         high = high + swap(high, far4, far3)
         low = jnp.where(odd, low + swap(low, far4, far4), low)
         high = high + swap(high, far3, far4)
-        return (high, swap(high, 1, 1)), (low, swap(low, 1, 1))
+        return (high, swap(high, 1, 1)), (low, swap(low, 1, 1)), *riders
 
     def local(vec, low):
         (part,) = call(
             functools.partial(local_kernel, factors),
             [part_shape],
-            ids,
-            [oriented, *low, bases, leaves, vec],
+                [oriented, *low, bases, leaves, vec],
             (2 + LEAF // rank) * mults,
         )
         return part
@@ -198,7 +199,6 @@
     (send,) = call(
         first_kernel,
         [pair_shape],
-        ids,
         [pltpu.with_memory_space_constraint(array, pltpu.HBM) for array in (bases, signal)],
         2 * mults,
         arrays_in=HBM,
@@ -208,31 +208,28 @@
             pltpu.SemaphoreType.DMA((chunks, 3)),
         ],
     )
-    kept = call(kept_kernel, [sums_shape] * 2, ids, [bases, signal], 2 * mults)
-    oriented, turned = call(
+    kept = call(kept_kernel, [sums_shape] * 2, [bases, signal], 2 * mults)
+    prepared = call(
         prepare_kernel,
         [
             jax.ShapeDtypeStruct((levels, rank, rank), BF16),
             jax.ShapeDtypeStruct((levels, rank, rows_dev), BF16),
         ],
-        ids,
         [couplings, bases],
         mults,
     )
-    high, low = siblings(send, *kept)
+    high, low, oriented, turned = siblings(send, *kept, prepared)
     scaled, send = call(
         functools.partial(scale_kernel, factors),
         [vec_shape, pair_shape],
-        ids,
         [oriented, *high, bases, local(signal, low), turned, weight_rows],
         4 * mults,
     )
-    kept = call(kept_again_kernel, [sums_shape] * 2, ids, [turned, scaled], 2 * mults)
+    kept = call(kept_again_kernel, [sums_shape] * 2, [turned, scaled], 2 * mults)
     high, low = siblings(send, *kept)
     (result,) = call(
         functools.partial(result_kernel, factors),
         [vec_shape],
-        ids,
         [oriented, *high, bases, local(scaled, low)],
         2 * mults,
         outs_in=HBM,

time: 51.6 us -> 48.5 us (0.940)
  Pallas kernels: 10.8 us -> 6.58 us
  waiting for transfers between devices: 23.5 us -> 24.2 us
  starting transfers between devices: 16.6 us -> 17.2 us
    pallas_call x8, Pallas kernels: 10.8 us -> 6.58 us  [call(): pl.pallas_call(kernel, out_shape=outs, in_specs=[arrays_in] * len(arrays)...]
    ppermute x18, waiting for transfers between devices: 23.5 us -> 24.2 us  [swap(): return lax.ppermute(value, AXIS, pairs)]
    ppermute x18, starting transfers between devices: 16.6 us -> 17.2 us  [swap(): return lax.ppermute(value, AXIS, pairs)]
  transfers between devices with their start and end apart: 18 -> 18, of which waited for: 12 -> 14; matrix products, arithmetic and copies ran while one was open for 0% -> 0% of each run, Pallas kernels for 10% -> 5%
where the time goes in v3:
time: 48.5 us; the launch traced here: 48.3 us
  waiting for transfers between devices  24.2 us (50%)
  starting transfers between devices  17.2 us (35%)
  Pallas kernels  6.58 us (14%)
    ppermute x18, waiting for transfers between devices, swap(): return lax.ppermute(value, AXIS, pairs)  24.2 us
    ppermute x18, starting transfers between devices, swap(): return lax.ppermute(value, AXIS, pairs)  17.2 us
    pallas_call x8, Pallas kernels, call(): pl.pallas_call(kernel, out_shape=outs, in_specs=[arrays_in] * len(arrays)...  6.58 us
  transfers between devices with their start and end apart: 18, of which 14 were waited for; matrix products, arithmetic and copies ran while one was open for 0% of the time, Pallas kernels for 5%

profile of v3, /device:TPU:0, one launch (start us, length us, event | category | flops | bytes accessed | tf_op | source)
XLA Modules:
  0.0 48.3 jit_solution(10996701520930367195)
XLA Ops:
  0.0 2.0 %shard_map.56 = f32[2,128,256]{2,1,0:T(8,128)S(1)} custom-call(bf16[4,1024,128]{2,1,0:T(8,128)(2,1)} %bases_ref.13, bf16[1024,256]{1,0:T(8,128)(2,1)} %vec_ref.5), custom_call_target="tpu_custom_call" | custom-call | flops 134217728 | bytes 1835008 | tf_op jit(solution)/shard_map/pallas_call | solution.py:25
  2.9 0.8 %collective-permute-done = f32[2,128,256]{2,1,0:T(8,128)S(1)} collective-permute-done((f32[2,128,256]{2,1,0:T(8,128)S(1)}, f32[2,128,256]{2,1,0:T(8,128)S(1)}, u32[]{:S(2)}, u32[]{:S(2)}) %collective-permute-start) | collective-permute-done | bytes 262176 | tf_op jit(solution)/shard_map/ppermute | solution.py:171
  3.7 2.9 %collective-permute-start.2 = (f32[128,256]{1,0:T(8,128)S(1)}, f32[128,256]{1,0:T(8,128)S(1)}, u32[]{:S(2)}, u32[]{:S(2)}) collective-permute-start(f32[128,256]{1,0:T(8,128)S(1)} %get-tuple-element.36), channel_id=1, source_target_pairs={{0,2},{1,25},{2,0},{3,27},{4,6},{5,29},{6,4},{7,31},{8,10},{9,17},... | collective-permute-start | bytes 393224 | tf_op jit(solution)/shard_map/ppermute | solution.py:171
  6.6 1.6 %collective-permute-start.1 = (f32[128,256]{1,0:T(8,128)S(1)}, f32[128,256]{1,0:T(8,128)S(1)}, u32[]{:S(2)}, u32[]{:S(2)}) collective-permute-start(f32[128,256]{1,0:T(8,128)S(1)} %get-tuple-element.36), channel_id=1, source_target_pairs={{0,8},{1,17},{2,10},{3,19},{4,12},{5,21},{6,14},{7,23},{8,0},{9,25... | collective-permute-start | bytes 393224 | tf_op jit(solution)/shard_map/ppermute | solution.py:171
  9.6 3.1 %collective-permute-done.1 = f32[128,256]{1,0:T(8,128)S(1)} collective-permute-done((f32[128,256]{1,0:T(8,128)S(1)}, f32[128,256]{1,0:T(8,128)S(1)}, u32[]{:S(2)}, u32[]{:S(2)}) %collective-permute-start.1) | collective-permute-done | bytes 131104 | tf_op jit(solution)/shard_map/ppermute | solution.py:171
  12.6 1.6 %collective-permute-start.3 = (f32[128,256]{1,0:T(8,128)S(1)}, f32[128,256]{1,0:T(8,128)S(1)}, u32[]{:S(2)}, u32[]{:S(2)}) collective-permute-start(f32[128,256]{1,0:T(8,128)S(1)} %add_select_fusion.3), channel_id=1, source_target_pairs={{0,4},{1,3},{2,6},{3,1},{4,0},{5,7},{6,2},{7,5},{8,12},{9,11},{10,... | collective-permute-start | bytes 393224 | tf_op jit(solution)/shard_map/ppermute | solution.py:171
  14.2 0.9 %collective-permute-start.7 = (f32[128,256]{1,0:T(8,128)S(1)}, f32[128,256]{1,0:T(8,128)S(1)}, u32[]{:S(2)}, u32[]{:S(2)}) collective-permute-start(f32[128,256]{1,0:T(8,128)S(1)} %collective-permute-done.6), channel_id=1, source_target_pairs={{0,2},{1,3},{2,0},{3,1},{4,6},{5,7},{6,4},{7,5},{8,10},{9,11},{10,... | collective-permute-start | bytes 393224 | tf_op jit(solution)/shard_map/ppermute | solution.py:171
  15.1 2.5 %collective-permute-done.3 = f32[128,256]{1,0:T(8,128)S(1)} collective-permute-done((f32[128,256]{1,0:T(8,128)S(1)}, f32[128,256]{1,0:T(8,128)S(1)}, u32[]{:S(2)}, u32[]{:S(2)}) %collective-permute-start.3) | collective-permute-done | bytes 131104 | tf_op jit(solution)/shard_map/ppermute | solution.py:171
  18.2 2.4 %collective-permute-done.7 = f32[128,256]{1,0:T(8,128)S(1)} collective-permute-done((f32[128,256]{1,0:T(8,128)S(1)}, f32[128,256]{1,0:T(8,128)S(1)}, u32[]{:S(2)}, u32[]{:S(2)}) %collective-permute-start.7) | collective-permute-done | bytes 131104 | tf_op jit(solution)/shard_map/ppermute | solution.py:171
  21.2 1.5 %collective-permute-done.4 = f32[128,256]{1,0:T(8,128)S(1)} collective-permute-done((f32[128,256]{1,0:T(8,128)S(1)}, f32[128,256]{1,0:T(8,128)S(1)}, u32[]{:S(2)}, u32[]{:S(2)}) %collective-permute-start.4) | collective-permute-done | bytes 131104 | tf_op jit(solution)/shard_map/ppermute | solution.py:171
  23.5 0.7 %shard_map.58.part_ref = f32[1024,256]{1,0:T(8,128)S(1)} custom-call(bf16[4,128,128]{2,1,0:T(8,128)(2,1)S(1)} %get-tuple-element.22.oriented_ref, f32[128,256]{1,0:T(8,128)S(1)} %add_select_fusion.2.own_ref, f32[128,256]{1,0:T(8,128)S(1)} %collective-permute-done.8.other_ref, bf16[4,1024,128]{2,1,0:T(8,128)(2,1)S(1)} %copy-done, ...), custom_call_target="tpu_custom_call" | custom-call | flops 402653184 | bytes 4063232 | tf_op jit(solution)/shard_map/pallas_call | solution.py:25
  24.5 0.9 %shard_map.59 = (bf16[1024,256]{1,0:T(8,128)(2,1)S(1)}, f32[2,128,256]{2,1,0:T(8,128)S(1)}) custom-call(bf16[4,128,128]{2,1,0:T(8,128)(2,1)S(1)} %get-tuple-element.22.oriented_ref, f32[128,256]{1,0:T(8,128)S(1)} %add.44.own_ref, f32[128,256]{1,0:T(8,128)S(1)} %collective-permute-done.5.other_ref, bf16[4,1024,128]{2,1,0:T(8,128)(2,1)S(1)} %copy-done, ...), custom_call_target="tpu_custom_call" | custom-call | flops 268435456 | bytes 4329472 | tf_op jit(solution)/shard_map/pallas_call | solution.py:25
  26.1 0.9 %collective-permute-done.9 = f32[2,128,256]{2,1,0:T(8,128)S(1)} collective-permute-done((f32[2,128,256]{2,1,0:T(8,128)S(1)}, f32[2,128,256]{2,1,0:T(8,128)S(1)}, u32[]{:S(2)}, u32[]{:S(2)}) %collective-permute-start.9) | collective-permute-done | bytes 262176 | tf_op jit(solution)/shard_map/ppermute | solution.py:171
  27.0 1.8 %collective-permute-start.11 = (f32[128,256]{1,0:T(8,128)S(1)}, f32[128,256]{1,0:T(8,128)S(1)}, u32[]{:S(2)}, u32[]{:S(2)}) collective-permute-start(f32[128,256]{1,0:T(8,128)S(1)} %get-tuple-element.34), channel_id=1, source_target_pairs={{0,2},{1,25},{2,0},{3,27},{4,6},{5,29},{6,4},{7,31},{8,10},{9,17},... | collective-permute-start | bytes 393224 | tf_op jit(solution)/shard_map/ppermute | solution.py:171
  28.8 1.9 %collective-permute-start.15 = (f32[128,256]{1,0:T(8,128)S(1)}, f32[128,256]{1,0:T(8,128)S(1)}, u32[]{:S(2)}, u32[]{:S(2)}) collective-permute-start(f32[128,256]{1,0:T(8,128)S(1)} %get-tuple-element.33), channel_id=1, source_target_pairs={{0,2},{1,5},{2,0},{3,7},{4,6},{5,1},{6,4},{7,3},{8,10},{9,13},{10,... | collective-permute-start | bytes 393224 | tf_op jit(solution)/shard_map/ppermute | solution.py:171
  30.7 1.3 %collective-permute-done.11 = f32[128,256]{1,0:T(8,128)S(1)} collective-permute-done((f32[128,256]{1,0:T(8,128)S(1)}, f32[128,256]{1,0:T(8,128)S(1)}, u32[]{:S(2)}, u32[]{:S(2)}) %collective-permute-start.11) | collective-permute-done | bytes 131104 | tf_op jit(solution)/shard_map/ppermute | solution.py:171
  32.0 3.5 %collective-permute-done.10 = f32[128,256]{1,0:T(8,128)S(1)} collective-permute-done((f32[128,256]{1,0:T(8,128)S(1)}, f32[128,256]{1,0:T(8,128)S(1)}, u32[]{:S(2)}, u32[]{:S(2)}) %collective-permute-start.10) | collective-permute-done | bytes 131104 | tf_op jit(solution)/shard_map/ppermute | solution.py:171
  35.9 1.4 %collective-permute-start.16 = (f32[128,256]{1,0:T(8,128)S(1)}, f32[128,256]{1,0:T(8,128)S(1)}, u32[]{:S(2)}, u32[]{:S(2)}) collective-permute-start(f32[128,256]{1,0:T(8,128)S(1)} %collective-permute-done.15), channel_id=1, source_target_pairs={{0,2},{1,3},{2,0},{3,1},{4,6},{5,7},{6,4},{7,5},{8,10},{9,11},{10,... | collective-permute-start | bytes 393224 | tf_op jit(solution)/shard_map/ppermute | solution.py:171
  37.3 3.3 %collective-permute-done.12 = f32[128,256]{1,0:T(8,128)S(1)} collective-permute-done((f32[128,256]{1,0:T(8,128)S(1)}, f32[128,256]{1,0:T(8,128)S(1)}, u32[]{:S(2)}, u32[]{:S(2)}) %collective-permute-start.12) | collective-permute-done | bytes 131104 | tf_op jit(solution)/shard_map/ppermute | solution.py:171
  40.7 1.5 %collective-permute-done.16 = f32[128,256]{1,0:T(8,128)S(1)} collective-permute-done((f32[128,256]{1,0:T(8,128)S(1)}, f32[128,256]{1,0:T(8,128)S(1)}, u32[]{:S(2)}, u32[]{:S(2)}) %collective-permute-start.16) | collective-permute-done | bytes 131104 | tf_op jit(solution)/shard_map/ppermute | solution.py:171
  42.2 1.1 %collective-permute-start.17 = (f32[128,256]{1,0:T(8,128)S(1)}, f32[128,256]{1,0:T(8,128)S(1)}, u32[]{:S(2)}, u32[]{:S(2)}) collective-permute-start(f32[128,256]{1,0:T(8,128)S(1)} %add_select_fusion.own_ref), channel_id=1, source_target_pairs={{0,1},{1,0},{2,3},{3,2},{4,5},{5,4},{6,7},{7,6},{8,9},{9,8},{10,11... | collective-permute-start | bytes 393224 | tf_op jit(solution)/shard_map/ppermute | solution.py:171
  43.3 2.3 %collective-permute-done.13 = f32[128,256]{1,0:T(8,128)S(1)} collective-permute-done((f32[128,256]{1,0:T(8,128)S(1)}, f32[128,256]{1,0:T(8,128)S(1)}, u32[]{:S(2)}, u32[]{:S(2)}) %collective-permute-start.13) | collective-permute-done | bytes 131104 | tf_op jit(solution)/shard_map/ppermute | solution.py:171
  45.9 0.7 %shard_map.61.part_ref = f32[1024,256]{1,0:T(8,128)S(1)} custom-call(bf16[4,128,128]{2,1,0:T(8,128)(2,1)S(1)} %get-tuple-element.22.oriented_ref, f32[128,256]{1,0:T(8,128)S(1)} %add_select_fusion.own_ref, f32[128,256]{1,0:T(8,128)S(1)} %collective-permute-done.17.other_ref, bf16[4,1024,128]{2,1,0:T(8,128)(2,1)S(1)} %copy-done, ...), custom_call_target="tpu_custom_call" | custom-call | flops 402653184 | bytes 4063232 | tf_op jit(solution)/shard_map/pallas_call | solution.py:25
  47.1 1.2 %shard_map.62 = bf16[1024,256]{1,0:T(8,128)(2,1)} custom-call(bf16[4,128,128]{2,1,0:T(8,128)(2,1)S(1)} %get-tuple-element.22.oriented_ref, f32[128,256]{1,0:T(8,128)S(1)} %add.50.own_ref, f32[128,256]{1,0:T(8,128)S(1)} %collective-permute-done.14.other_ref, bf16[4,1024,128]{2,1,0:T(8,128)(2,1)S(1)} %copy-done, f32[1024,256]{1,0:T(8,128)S(1)} %shard_map.61.part_ref), custom_call_target="tpu_custom_call" | custom-call | flops 134217728 | bytes 3014656 | tf_op jit(solution)/shard_map/pallas_call | solution.py:25
  (40 shorter events, 6.4 us)
Async XLA Ops:
  0.0 2.5 %copy-start = (bf16[4,1024,128]{2,1,0:T(8,128)(2,1)S(1)}, bf16[4,1024,128]{2,1,0:T(8,128)(2,1)}, u32[]{:S(2)}) copy-start(bf16[4,1024,128]{2,1,0:T(8,128)(2,1)} %bases_ref.13) | copy-start | bytes 3145732
  0.0 2.5 %copy-start.1 = (bf16[1024,256]{1,0:T(8,128)(2,1)S(1)}, bf16[1024,256]{1,0:T(8,128)(2,1)}, u32[]{:S(2)}) copy-start(bf16[1024,256]{1,0:T(8,128)(2,1)} %vec_ref.5) | copy-start | bytes 1572868
  2.0 1.7 %collective-permute-start = (f32[2,128,256]{2,1,0:T(8,128)S(1)}, f32[2,128,256]{2,1,0:T(8,128)S(1)}, u32[]{:S(2)}, u32[]{:S(2)}) collective-permute-start(f32[2,128,256]{2,1,0:T(8,128)S(1)} %shard_map.56), channel_id=1, source_target_pairs={{0,1},{1,0},{2,3},{3,2},{4,5},{5,4},{6,7},{7,6},{8,9},{9,8},{10,11... | collective-permute-start | bytes 786440 | tf_op jit(solution)/shard_map/ppermute | solution.py:171
  2.9 5.3 %copy-start.3 = (bf16[15,128,128]{2,1,0:T(8,128)(2,1)S(1)}, bf16[15,128,128]{2,1,0:T(8,128)(2,1)}, u32[]{:S(2)}) copy-start(bf16[15,128,128]{2,1,0:T(8,128)(2,1)} %couplings_ref.1) | copy-start | bytes 1474564
  3.7 5.9 %collective-permute-start.2 = (f32[128,256]{1,0:T(8,128)S(1)}, f32[128,256]{1,0:T(8,128)S(1)}, u32[]{:S(2)}, u32[]{:S(2)}) collective-permute-start(f32[128,256]{1,0:T(8,128)S(1)} %get-tuple-element.36), channel_id=1, source_target_pairs={{0,2},{1,25},{2,0},{3,27},{4,6},{5,29},{6,4},{7,31},{8,10},{9,17},... | collective-permute-start | bytes 393224 | tf_op jit(solution)/shard_map/ppermute | solution.py:171
  6.6 6.0 %collective-permute-start.1 = (f32[128,256]{1,0:T(8,128)S(1)}, f32[128,256]{1,0:T(8,128)S(1)}, u32[]{:S(2)}, u32[]{:S(2)}) collective-permute-start(f32[128,256]{1,0:T(8,128)S(1)} %get-tuple-element.36), channel_id=1, source_target_pairs={{0,8},{1,17},{2,10},{3,19},{4,12},{5,21},{6,14},{7,23},{8,0},{9,25... | collective-permute-start | bytes 393224 | tf_op jit(solution)/shard_map/ppermute | solution.py:171
  8.6 14.9 %copy-start.2 = (bf16[1024,512]{1,0:T(8,128)(2,1)S(1)}, bf16[1024,512]{1,0:T(8,128)(2,1)}, u32[]{:S(2)}) copy-start(bf16[1024,512]{1,0:T(8,128)(2,1)} %leaves_ref.3) | copy-start | bytes 3145732
  8.6 5.6 %collective-permute-start.6 = (f32[128,256]{1,0:T(8,128)S(1)}, f32[128,256]{1,0:T(8,128)S(1)}, u32[]{:S(2)}, u32[]{:S(2)}) collective-permute-start(f32[128,256]{1,0:T(8,128)S(1)} %get-tuple-element.35), channel_id=1, source_target_pairs={{0,2},{1,5},{2,0},{3,7},{4,6},{5,1},{6,4},{7,3},{8,10},{9,13},{10,... | collective-permute-start | bytes 393224 | tf_op jit(solution)/shard_map/ppermute | solution.py:171
  12.6 5.0 %collective-permute-start.3 = (f32[128,256]{1,0:T(8,128)S(1)}, f32[128,256]{1,0:T(8,128)S(1)}, u32[]{:S(2)}, u32[]{:S(2)}) collective-permute-start(f32[128,256]{1,0:T(8,128)S(1)} %add_select_fusion.3), channel_id=1, source_target_pairs={{0,4},{1,3},{2,6},{3,1},{4,0},{5,7},{6,2},{7,5},{8,12},{9,11},{10,... | collective-permute-start | bytes 393224 | tf_op jit(solution)/shard_map/ppermute | solution.py:171
  14.2 6.3 %collective-permute-start.7 = (f32[128,256]{1,0:T(8,128)S(1)}, f32[128,256]{1,0:T(8,128)S(1)}, u32[]{:S(2)}, u32[]{:S(2)}) collective-permute-start(f32[128,256]{1,0:T(8,128)S(1)} %collective-permute-done.6), channel_id=1, source_target_pairs={{0,2},{1,3},{2,0},{3,1},{4,6},{5,7},{6,4},{7,5},{8,10},{9,11},{10,... | collective-permute-start | bytes 393224 | tf_op jit(solution)/shard_map/ppermute | solution.py:171
  17.7 5.0 %collective-permute-start.4 = (f32[128,256]{1,0:T(8,128)S(1)}, f32[128,256]{1,0:T(8,128)S(1)}, u32[]{:S(2)}, u32[]{:S(2)}) collective-permute-start(f32[128,256]{1,0:T(8,128)S(1)} %add.43), channel_id=1, source_target_pairs={{0,2},{1,5},{2,0},{3,7},{4,6},{5,1},{6,4},{7,3},{8,10},{9,13},{10,... | collective-permute-start | bytes 393224 | tf_op jit(solution)/shard_map/ppermute | solution.py:171
  20.6 2.9 %collective-permute-start.8 = (f32[128,256]{1,0:T(8,128)S(1)}, f32[128,256]{1,0:T(8,128)S(1)}, u32[]{:S(2)}, u32[]{:S(2)}) collective-permute-start(f32[128,256]{1,0:T(8,128)S(1)} %add_select_fusion.2.own_ref), channel_id=1, source_target_pairs={{0,1},{1,0},{2,3},{3,2},{4,5},{5,4},{6,7},{7,6},{8,9},{9,8},{10,11... | collective-permute-start | bytes 393224 | tf_op jit(solution)/shard_map/ppermute | solution.py:171
  22.7 1.7 %collective-permute-start.5 = (f32[128,256]{1,0:T(8,128)S(1)}, f32[128,256]{1,0:T(8,128)S(1)}, u32[]{:S(2)}, u32[]{:S(2)}) collective-permute-start(f32[128,256]{1,0:T(8,128)S(1)} %add.44.own_ref), channel_id=1, source_target_pairs={{0,1},{1,0},{2,3},{3,2},{4,5},{5,4},{6,7},{7,6},{8,9},{9,8},{10,11... | collective-permute-start | bytes 393224 | tf_op jit(solution)/shard_map/ppermute | solution.py:171
  23.5 1.0 %copy-start.4 = (f32[1024]{0:T(1024)S(1)}, f32[1024]{0:T(1024)}, u32[]{:S(2)}) copy-start(f32[1024]{0:T(1024)} %param.9) | copy-start | bytes 12292
  25.3 1.6 %collective-permute-start.9 = (f32[2,128,256]{2,1,0:T(8,128)S(1)}, f32[2,128,256]{2,1,0:T(8,128)S(1)}, u32[]{:S(2)}, u32[]{:S(2)}) collective-permute-start(f32[2,128,256]{2,1,0:T(8,128)S(1)} %get-tuple-element.29), channel_id=1, source_target_pairs={{0,1},{1,0},{2,3},{3,2},{4,5},{5,4},{6,7},{7,6},{8,9},{9,8},{10,11... | collective-permute-start | bytes 786440 | tf_op jit(solution)/shard_map/ppermute | solution.py:171
  27.0 5.0 %collective-permute-start.11 = (f32[128,256]{1,0:T(8,128)S(1)}, f32[128,256]{1,0:T(8,128)S(1)}, u32[]{:S(2)}, u32[]{:S(2)}) collective-permute-start(f32[128,256]{1,0:T(8,128)S(1)} %get-tuple-element.34), channel_id=1, source_target_pairs={{0,2},{1,25},{2,0},{3,27},{4,6},{5,29},{6,4},{7,31},{8,10},{9,17},... | collective-permute-start | bytes 393224 | tf_op jit(solution)/shard_map/ppermute | solution.py:171
  28.7 6.8 %collective-permute-start.10 = (f32[128,256]{1,0:T(8,128)S(1)}, f32[128,256]{1,0:T(8,128)S(1)}, u32[]{:S(2)}, u32[]{:S(2)}) collective-permute-start(f32[128,256]{1,0:T(8,128)S(1)} %get-tuple-element.34), channel_id=1, source_target_pairs={{0,8},{1,17},{2,10},{3,19},{4,12},{5,21},{6,14},{7,23},{8,0},{9,25... | collective-permute-start | bytes 393224 | tf_op jit(solution)/shard_map/ppermute | solution.py:171
  28.8 7.1 %collective-permute-start.15 = (f32[128,256]{1,0:T(8,128)S(1)}, f32[128,256]{1,0:T(8,128)S(1)}, u32[]{:S(2)}, u32[]{:S(2)}) collective-permute-start(f32[128,256]{1,0:T(8,128)S(1)} %get-tuple-element.33), channel_id=1, source_target_pairs={{0,2},{1,5},{2,0},{3,7},{4,6},{5,1},{6,4},{7,3},{8,10},{9,13},{10,... | collective-permute-start | bytes 393224 | tf_op jit(solution)/shard_map/ppermute | solution.py:171
  35.6 5.0 %collective-permute-start.12 = (f32[128,256]{1,0:T(8,128)S(1)}, f32[128,256]{1,0:T(8,128)S(1)}, u32[]{:S(2)}, u32[]{:S(2)}) collective-permute-start(f32[128,256]{1,0:T(8,128)S(1)} %add_select_fusion.1), channel_id=1, source_target_pairs={{0,4},{1,3},{2,6},{3,1},{4,0},{5,7},{6,2},{7,5},{8,12},{9,11},{10,... | collective-permute-start | bytes 393224 | tf_op jit(solution)/shard_map/ppermute | solution.py:171
  35.9 6.3 %collective-permute-start.16 = (f32[128,256]{1,0:T(8,128)S(1)}, f32[128,256]{1,0:T(8,128)S(1)}, u32[]{:S(2)}, u32[]{:S(2)}) collective-permute-start(f32[128,256]{1,0:T(8,128)S(1)} %collective-permute-done.15), channel_id=1, source_target_pairs={{0,2},{1,3},{2,0},{3,1},{4,6},{5,7},{6,4},{7,5},{8,10},{9,11},{10,... | collective-permute-start | bytes 393224 | tf_op jit(solution)/shard_map/ppermute | solution.py:171
  40.6 5.0 %collective-permute-start.13 = (f32[128,256]{1,0:T(8,128)S(1)}, f32[128,256]{1,0:T(8,128)S(1)}, u32[]{:S(2)}, u32[]{:S(2)}) collective-permute-start(f32[128,256]{1,0:T(8,128)S(1)} %add.49), channel_id=1, source_target_pairs={{0,2},{1,5},{2,0},{3,7},{4,6},{5,1},{6,4},{7,3},{8,10},{9,13},{10,... | collective-permute-start | bytes 393224 | tf_op jit(solution)/shard_map/ppermute | solution.py:171
  42.2 3.7 %collective-permute-start.17 = (f32[128,256]{1,0:T(8,128)S(1)}, f32[128,256]{1,0:T(8,128)S(1)}, u32[]{:S(2)}, u32[]{:S(2)}) collective-permute-start(f32[128,256]{1,0:T(8,128)S(1)} %add_select_fusion.own_ref), channel_id=1, source_target_pairs={{0,1},{1,0},{2,3},{3,2},{4,5},{5,4},{6,7},{7,6},{8,9},{9,8},{10,11... | collective-permute-start | bytes 393224 | tf_op jit(solution)/shard_map/ppermute | solution.py:171
  45.7 1.4 %collective-permute-start.14 = (f32[128,256]{1,0:T(8,128)S(1)}, f32[128,256]{1,0:T(8,128)S(1)}, u32[]{:S(2)}, u32[]{:S(2)}) collective-permute-start(f32[128,256]{1,0:T(8,128)S(1)} %add.50.own_ref), channel_id=1, source_target_pairs={{0,1},{1,0},{2,3},{3,2},{4,5},{5,4},{6,7},{7,6},{8,9},{9,8},{10,11... | collective-permute-start | bytes 393224 | tf_op jit(solution)/shard_map/ppermute | solution.py:171

commit v4 on v3

--- a/solution.py
+++ b/solution.py
@@ -41,29 +41,35 @@
     return lax.dot_general(basis, vec, (((0,), (0,)), ((), ())), preferred_element_type=F32)
 
 
-def first_kernel(bases_ref, vec_ref, out_ref, bases_buf, vec_buf, sems):
+def first_kernel(bases_in, vec_in, out_ref, bases_ref, vec_ref, sems):
     parity = lax.axis_index(AXIS) % 2
-    rank = bases_ref.shape[2]
+    rank = bases_in.shape[2]
+    rows_dev = vec_in.shape[0]
+    chunks = rows_dev // CHUNK
+
+    def basis_copy(level, rows, sem):
+        return pltpu.make_async_copy(bases_in.at[level, rows, :], bases_ref.at[level, rows, :], sem)
+
     copies = []
-    for chunk in range(vec_ref.shape[0] // CHUNK):
-        rows = pl.ds(chunk * CHUNK, CHUNK)
-        own = [pltpu.make_async_copy(vec_ref.at[rows, :], vec_buf.at[rows, :], sems.at[chunk, 0])]
-        for slot in range(2):
-            source = bases_ref.at[parity + 2 * slot, rows, :]
-            target = bases_buf.at[rows, pl.ds(slot * rank, rank)]
-            own.append(pltpu.make_async_copy(source, target, sems.at[chunk, 1 + slot]))
-        for copy in own:
-            copy.start()
-        copies.append(own)
+    for chunk in range(chunks):
+        rows = pl.ds(chunk * CHUNK, CHUNK)
+        copies.append([pltpu.make_async_copy(vec_in.at[rows, :], vec_ref.at[rows, :], sems.at[chunk, 0])])
+        copies[-1] += [basis_copy(parity + 2 * slot, rows, sems.at[chunk, 1 + slot]) for slot in range(2)]
+    copies.append([basis_copy(1 - parity + 2 * slot, pl.ds(0, rows_dev), sems.at[chunks, slot]) for slot in range(2)])
+    for copy in sum(copies, []):
+        copy.start()
     total = None
-    for chunk, own in enumerate(copies):
-        for copy in own:
+    for chunk in range(chunks):
+        for copy in copies[chunk]:
             copy.wait()
-        rows = slice(chunk * CHUNK, (chunk + 1) * CHUNK)
-        term = transposed_dot(bases_buf[rows, :], vec_buf[rows, :])
+        rows = pl.ds(chunk * CHUNK, CHUNK)
+        basis = jnp.concatenate([bases_ref[parity, rows, :], bases_ref[parity + 2, rows, :]], axis=1)
+        term = transposed_dot(basis, vec_ref[rows, :])
         total = term if total is None else total + term
     out_ref[0] = total[:rank]
     out_ref[1] = total[rank:]
+    for copy in copies[chunks]:
+        copy.wait()
 
 
 def kept_kernel(bases_ref, vec_ref, high_ref, low_ref):
@@ -177,14 +183,15 @@
         for bit in range(1, bits - levels):
             high = high + swap(high, 1 << bit, 1 << bit)
             low = low + swap(low, 1 << bit, 1 << bit)
-        near = swap(high, far1, far2)
-        across = swap(high, far1 | far2, far4)
+        near = swap(high, far1, far4)
+        across = swap(high, far1 | far2, far3)
         near, across, *riders = lax.optimization_barrier((near, across, *riders))
-        high = jnp.where(odd, near + across, near)
+        high = jnp.where(odd, near + across, high + near)
         low = swap(low, far3, far4)
+        got = swap(high, far3, far2)
+        high = jnp.where(odd, high + got, got)
+        low = jnp.where(odd, low + swap(low, far4, far4), low)
         high = high + swap(high, far4, far3)
-        low = jnp.where(odd, low + swap(low, far4, far4), low)
-        high = high + swap(high, far3, far4)
         return (high, swap(high, 1, 1)), (low, swap(low, 1, 1)), *riders
 
     def local(vec, low):
@@ -196,17 +203,17 @@
         )
         return part
 
-    (send,) = call(
+    send, bases, signal = call(
         first_kernel,
-        [pair_shape],
+        [
+            pair_shape,
+            jax.ShapeDtypeStruct(bases.shape, BF16),
+            jax.ShapeDtypeStruct(signal.shape, BF16),
+        ],
         [pltpu.with_memory_space_constraint(array, pltpu.HBM) for array in (bases, signal)],
         2 * mults,
         arrays_in=HBM,
-        scratch=[
-            pltpu.VMEM((rows_dev, 2 * rank), BF16),
-            pltpu.VMEM((rows_dev, width), BF16),
-            pltpu.SemaphoreType.DMA((chunks, 3)),
-        ],
+        scratch=[pltpu.SemaphoreType.DMA((chunks + 1, 3))],
     )
     kept = call(kept_kernel, [sums_shape] * 2, [bases, signal], 2 * mults)
     prepared = call(

time: 48.5 us -> 45.3 us (0.934)
  waiting for transfers between devices: 24.2 us -> 18.8 us
  starting transfers between devices: 17.2 us -> 19.5 us
    ppermute x18, waiting for transfers between devices: 24.2 us -> 18.8 us  [swap(): return lax.ppermute(value, AXIS, pairs)]
    ppermute x18, starting transfers between devices: 17.2 us -> 19.5 us  [swap(): return lax.ppermute(value, AXIS, pairs)]
  transfers between devices with their start and end apart: 18 -> 18, of which waited for: 14 -> 16; matrix products, arithmetic and copies ran while one was open for 0% -> 0% of each run, Pallas kernels for 5% -> 6%
where the time goes in v4:
time: 45.3 us; the launch traced here: 45.1 us
  starting transfers between devices  19.5 us (43%)
  waiting for transfers between devices  18.8 us (42%)
  Pallas kernels  6.49 us (14%)
    ppermute x18, starting transfers between devices, swap(): return lax.ppermute(value, AXIS, pairs)  19.5 us
    ppermute x18, waiting for transfers between devices, swap(): return lax.ppermute(value, AXIS, pairs)  18.8 us
    pallas_call x8, Pallas kernels, call(): pl.pallas_call(kernel, out_shape=outs, in_specs=[arrays_in] * len(arrays)...  6.49 us
  transfers between devices with their start and end apart: 18, of which 16 were waited for; matrix products, arithmetic and copies ran while one was open for 0% of the time, Pallas kernels for 6%

profile of v4, /device:TPU:0, one launch (start us, length us, event | category | flops | bytes accessed | tf_op | source)
XLA Modules:
  0.0 45.1 jit_solution(15911793940404183231)
XLA Ops:
  0.0 1.9 %shard_map.55 = (f32[2,128,256]{2,1,0:T(8,128)S(1)}, bf16[4,1024,128]{2,1,0:T(8,128)(2,1)S(1)}, bf16[1024,256]{1,0:T(8,128)(2,1)S(1)}) custom-call(bf16[4,1024,128]{2,1,0:T(8,128)(2,1)} %bases_in.1, bf16[1024,256]{1,0:T(8,128)(2,1)} %vec_in.1), custom_call_target="tpu_custom_call" | custom-call | flops 134217728 | bytes 3407872 | tf_op jit(solution)/shard_map/pallas_call | solution.py:25
  3.6 3.0 %collective-permute-start.2 = (f32[128,256]{1,0:T(8,128)S(1)}, f32[128,256]{1,0:T(8,128)S(1)}, u32[]{:S(2)}, u32[]{:S(2)}) collective-permute-start(f32[128,256]{1,0:T(8,128)S(1)} %get-tuple-element.42), channel_id=1, source_target_pairs={{0,4},{1,25},{2,6},{3,27},{4,0},{5,29},{6,2},{7,31},{8,12},{9,17},... | collective-permute-start | bytes 393224 | tf_op jit(solution)/shard_map/ppermute | solution.py:177
  6.5 1.5 %collective-permute-start.1 = (f32[128,256]{1,0:T(8,128)S(1)}, f32[128,256]{1,0:T(8,128)S(1)}, u32[]{:S(2)}, u32[]{:S(2)}) collective-permute-start(f32[128,256]{1,0:T(8,128)S(1)} %get-tuple-element.42), channel_id=1, source_target_pairs={{0,2},{1,17},{2,0},{3,19},{4,6},{5,21},{6,4},{7,23},{8,10},{9,25},... | collective-permute-start | bytes 393224 | tf_op jit(solution)/shard_map/ppermute | solution.py:177
  9.5 2.0 %collective-permute-done.1 = f32[128,256]{1,0:T(8,128)S(1)} collective-permute-done((f32[128,256]{1,0:T(8,128)S(1)}, f32[128,256]{1,0:T(8,128)S(1)}, u32[]{:S(2)}, u32[]{:S(2)}) %collective-permute-start.1) | collective-permute-done | bytes 131104 | tf_op jit(solution)/shard_map/ppermute | solution.py:177
  11.5 1.6 %collective-permute-start.3 = (f32[128,256]{1,0:T(8,128)S(1)}, f32[128,256]{1,0:T(8,128)S(1)}, u32[]{:S(2)}, u32[]{:S(2)}) collective-permute-start(f32[128,256]{1,0:T(8,128)S(1)} %add_select_fusion.5), channel_id=1, source_target_pairs={{0,8},{1,5},{2,10},{3,7},{4,12},{5,1},{6,14},{7,3},{8,0},{9,13},{1... | collective-permute-start | bytes 393224 | tf_op jit(solution)/shard_map/ppermute | solution.py:177
  13.5 1.2 %collective-permute-start.7 = (f32[128,256]{1,0:T(8,128)S(1)}, f32[128,256]{1,0:T(8,128)S(1)}, u32[]{:S(2)}, u32[]{:S(2)}) collective-permute-start(f32[128,256]{1,0:T(8,128)S(1)} %collective-permute-done.6), channel_id=1, source_target_pairs={{0,2},{1,3},{2,0},{3,1},{4,6},{5,7},{6,4},{7,5},{8,10},{9,11},{10,... | collective-permute-start | bytes 393224 | tf_op jit(solution)/shard_map/ppermute | solution.py:177
  14.7 1.9 %collective-permute-done.3 = f32[128,256]{1,0:T(8,128)S(1)} collective-permute-done((f32[128,256]{1,0:T(8,128)S(1)}, f32[128,256]{1,0:T(8,128)S(1)}, u32[]{:S(2)}, u32[]{:S(2)}) %collective-permute-start.3) | collective-permute-done | bytes 131104 | tf_op jit(solution)/shard_map/ppermute | solution.py:177
  16.6 0.8 %collective-permute-start.4 = (f32[128,256]{1,0:T(8,128)S(1)}, f32[128,256]{1,0:T(8,128)S(1)}, u32[]{:S(2)}, u32[]{:S(2)}) collective-permute-start(f32[128,256]{1,0:T(8,128)S(1)} %add_select_fusion.3), channel_id=1, source_target_pairs={{0,4},{1,3},{2,6},{3,1},{4,0},{5,7},{6,2},{7,5},{8,12},{9,11},{10,... | collective-permute-start | bytes 393224 | tf_op jit(solution)/shard_map/ppermute | solution.py:177
  17.4 1.2 %collective-permute-done.7 = f32[128,256]{1,0:T(8,128)S(1)} collective-permute-done((f32[128,256]{1,0:T(8,128)S(1)}, f32[128,256]{1,0:T(8,128)S(1)}, u32[]{:S(2)}, u32[]{:S(2)}) %collective-permute-start.7) | collective-permute-done | bytes 131104 | tf_op jit(solution)/shard_map/ppermute | solution.py:177
  18.7 1.1 %collective-permute-start.8 = (f32[128,256]{1,0:T(8,128)S(1)}, f32[128,256]{1,0:T(8,128)S(1)}, u32[]{:S(2)}, u32[]{:S(2)}) collective-permute-start(f32[128,256]{1,0:T(8,128)S(1)} %add_select_fusion.2.own_ref), channel_id=1, source_target_pairs={{0,1},{1,0},{2,3},{3,2},{4,5},{5,4},{6,7},{7,6},{8,9},{9,8},{10,11... | collective-permute-start | bytes 393224 | tf_op jit(solution)/shard_map/ppermute | solution.py:177
  19.8 1.9 %collective-permute-done.4 = f32[128,256]{1,0:T(8,128)S(1)} collective-permute-done((f32[128,256]{1,0:T(8,128)S(1)}, f32[128,256]{1,0:T(8,128)S(1)}, u32[]{:S(2)}, u32[]{:S(2)}) %collective-permute-start.4) | collective-permute-done | bytes 131104 | tf_op jit(solution)/shard_map/ppermute | solution.py:177
  23.4 0.9 %shard_map.59 = (bf16[1024,256]{1,0:T(8,128)(2,1)S(1)}, f32[2,128,256]{2,1,0:T(8,128)S(1)}) custom-call(bf16[4,128,128]{2,1,0:T(8,128)(2,1)S(1)} %get-tuple-element.28.oriented_ref, f32[128,256]{1,0:T(8,128)S(1)} %add.51.own_ref, f32[128,256]{1,0:T(8,128)S(1)} %collective-permute-done.5.other_ref, bf16[4,1024,128]{2,1,0:T(8,128)(2,1)S(1)} %get-tuple-element.22.bases_ref, ...), custom_call_target="tpu_custom_call" | custom-call | flops 268435456 | bytes 4329472 | tf_op jit(solution)/shard_map/pallas_call | solution.py:25
  25.0 0.9 %collective-permute-done.9 = f32[2,128,256]{2,1,0:T(8,128)S(1)} collective-permute-done((f32[2,128,256]{2,1,0:T(8,128)S(1)}, f32[2,128,256]{2,1,0:T(8,128)S(1)}, u32[]{:S(2)}, u32[]{:S(2)}) %collective-permute-start.9) | collective-permute-done | bytes 262176 | tf_op jit(solution)/shard_map/ppermute | solution.py:177
  25.9 1.4 %collective-permute-start.11 = (f32[128,256]{1,0:T(8,128)S(1)}, f32[128,256]{1,0:T(8,128)S(1)}, u32[]{:S(2)}, u32[]{:S(2)}) collective-permute-start(f32[128,256]{1,0:T(8,128)S(1)} %get-tuple-element.40), channel_id=1, source_target_pairs={{0,4},{1,25},{2,6},{3,27},{4,0},{5,29},{6,2},{7,31},{8,12},{9,17},... | collective-permute-start | bytes 393224 | tf_op jit(solution)/shard_map/ppermute | solution.py:177
  27.3 1.4 %collective-permute-start.10 = (f32[128,256]{1,0:T(8,128)S(1)}, f32[128,256]{1,0:T(8,128)S(1)}, u32[]{:S(2)}, u32[]{:S(2)}) collective-permute-start(f32[128,256]{1,0:T(8,128)S(1)} %get-tuple-element.40), channel_id=1, source_target_pairs={{0,2},{1,17},{2,0},{3,19},{4,6},{5,21},{6,4},{7,23},{8,10},{9,25},... | collective-permute-start | bytes 393224 | tf_op jit(solution)/shard_map/ppermute | solution.py:177
  29.3 1.6 %collective-permute-done.11 = f32[128,256]{1,0:T(8,128)S(1)} collective-permute-done((f32[128,256]{1,0:T(8,128)S(1)}, f32[128,256]{1,0:T(8,128)S(1)}, u32[]{:S(2)}, u32[]{:S(2)}) %collective-permute-start.11) | collective-permute-done | bytes 131104 | tf_op jit(solution)/shard_map/ppermute | solution.py:177
  31.0 1.3 %collective-permute-done.10 = f32[128,256]{1,0:T(8,128)S(1)} collective-permute-done((f32[128,256]{1,0:T(8,128)S(1)}, f32[128,256]{1,0:T(8,128)S(1)}, u32[]{:S(2)}, u32[]{:S(2)}) %collective-permute-start.10) | collective-permute-done | bytes 131104 | tf_op jit(solution)/shard_map/ppermute | solution.py:177
  32.8 0.9 %collective-permute-done.15 = f32[128,256]{1,0:T(8,128)S(1)} collective-permute-done((f32[128,256]{1,0:T(8,128)S(1)}, f32[128,256]{1,0:T(8,128)S(1)}, u32[]{:S(2)}, u32[]{:S(2)}) %collective-permute-start.15) | collective-permute-done | bytes 131104 | tf_op jit(solution)/shard_map/ppermute | solution.py:177
  33.7 1.4 %collective-permute-start.16 = (f32[128,256]{1,0:T(8,128)S(1)}, f32[128,256]{1,0:T(8,128)S(1)}, u32[]{:S(2)}, u32[]{:S(2)}) collective-permute-start(f32[128,256]{1,0:T(8,128)S(1)} %collective-permute-done.15), channel_id=1, source_target_pairs={{0,2},{1,3},{2,0},{3,1},{4,6},{5,7},{6,4},{7,5},{8,10},{9,11},{10,... | collective-permute-start | bytes 393224 | tf_op jit(solution)/shard_map/ppermute | solution.py:177
  35.1 2.2 %collective-permute-done.12 = f32[128,256]{1,0:T(8,128)S(1)} collective-permute-done((f32[128,256]{1,0:T(8,128)S(1)}, f32[128,256]{1,0:T(8,128)S(1)}, u32[]{:S(2)}, u32[]{:S(2)}) %collective-permute-start.12) | collective-permute-done | bytes 131104 | tf_op jit(solution)/shard_map/ppermute | solution.py:177
  37.3 0.8 %collective-permute-start.13 = (f32[128,256]{1,0:T(8,128)S(1)}, f32[128,256]{1,0:T(8,128)S(1)}, u32[]{:S(2)}, u32[]{:S(2)}) collective-permute-start(f32[128,256]{1,0:T(8,128)S(1)} %add_select_fusion.1), channel_id=1, source_target_pairs={{0,4},{1,3},{2,6},{3,1},{4,0},{5,7},{6,2},{7,5},{8,12},{9,11},{10,... | collective-permute-start | bytes 393224 | tf_op jit(solution)/shard_map/ppermute | solution.py:177
  38.8 1.4 %collective-permute-start.17 = (f32[128,256]{1,0:T(8,128)S(1)}, f32[128,256]{1,0:T(8,128)S(1)}, u32[]{:S(2)}, u32[]{:S(2)}) collective-permute-start(f32[128,256]{1,0:T(8,128)S(1)} %add_select_fusion.own_ref), channel_id=1, source_target_pairs={{0,1},{1,0},{2,3},{3,2},{4,5},{5,4},{6,7},{7,6},{8,9},{9,8},{10,11... | collective-permute-start | bytes 393224 | tf_op jit(solution)/shard_map/ppermute | solution.py:177
  40.2 2.2 %collective-permute-done.13 = f32[128,256]{1,0:T(8,128)S(1)} collective-permute-done((f32[128,256]{1,0:T(8,128)S(1)}, f32[128,256]{1,0:T(8,128)S(1)}, u32[]{:S(2)}, u32[]{:S(2)}) %collective-permute-start.13) | collective-permute-done | bytes 131104 | tf_op jit(solution)/shard_map/ppermute | solution.py:177
  43.9 1.2 %shard_map.62 = bf16[1024,256]{1,0:T(8,128)(2,1)} custom-call(bf16[4,128,128]{2,1,0:T(8,128)(2,1)S(1)} %get-tuple-element.28.oriented_ref, f32[128,256]{1,0:T(8,128)S(1)} %add.58.own_ref, f32[128,256]{1,0:T(8,128)S(1)} %collective-permute-done.14.other_ref, bf16[4,1024,128]{2,1,0:T(8,128)(2,1)S(1)} %get-tuple-element.22.bases_ref, ...), custom_call_target="tpu_custom_call" | custom-call | flops 134217728 | bytes 3014656 | tf_op jit(solution)/shard_map/pallas_call | solution.py:25
  (36 shorter events, 9.4 us)
Async XLA Ops:
  1.9 1.7 %collective-permute-start = (f32[2,128,256]{2,1,0:T(8,128)S(1)}, f32[2,128,256]{2,1,0:T(8,128)S(1)}, u32[]{:S(2)}, u32[]{:S(2)}) collective-permute-start(f32[2,128,256]{2,1,0:T(8,128)S(1)} %get-tuple-element.25), channel_id=1, source_target_pairs={{0,1},{1,0},{2,3},{3,2},{4,5},{5,4},{6,7},{7,6},{8,9},{9,8},{10,11... | collective-permute-start | bytes 786440 | tf_op jit(solution)/shard_map/ppermute | solution.py:177
  2.8 5.3 %copy-start.1 = (bf16[15,128,128]{2,1,0:T(8,128)(2,1)S(1)}, bf16[15,128,128]{2,1,0:T(8,128)(2,1)}, u32[]{:S(2)}) copy-start(bf16[15,128,128]{2,1,0:T(8,128)(2,1)} %couplings_ref.1) | copy-start | bytes 1474564
  3.6 5.9 %collective-permute-start.2 = (f32[128,256]{1,0:T(8,128)S(1)}, f32[128,256]{1,0:T(8,128)S(1)}, u32[]{:S(2)}, u32[]{:S(2)}) collective-permute-start(f32[128,256]{1,0:T(8,128)S(1)} %get-tuple-element.42), channel_id=1, source_target_pairs={{0,4},{1,25},{2,6},{3,27},{4,0},{5,29},{6,2},{7,31},{8,12},{9,17},... | collective-permute-start | bytes 393224 | tf_op jit(solution)/shard_map/ppermute | solution.py:177
  6.5 5.0 %collective-permute-start.1 = (f32[128,256]{1,0:T(8,128)S(1)}, f32[128,256]{1,0:T(8,128)S(1)}, u32[]{:S(2)}, u32[]{:S(2)}) collective-permute-start(f32[128,256]{1,0:T(8,128)S(1)} %get-tuple-element.42), channel_id=1, source_target_pairs={{0,2},{1,17},{2,0},{3,19},{4,6},{5,21},{6,4},{7,23},{8,10},{9,25},... | collective-permute-start | bytes 393224 | tf_op jit(solution)/shard_map/ppermute | solution.py:177
  8.4 14.0 %copy-start = (bf16[1024,512]{1,0:T(8,128)(2,1)S(1)}, bf16[1024,512]{1,0:T(8,128)(2,1)}, u32[]{:S(2)}) copy-start(bf16[1024,512]{1,0:T(8,128)(2,1)} %leaves_ref.3) | copy-start | bytes 3145732
  8.4 5.0 %collective-permute-start.6 = (f32[128,256]{1,0:T(8,128)S(1)}, f32[128,256]{1,0:T(8,128)S(1)}, u32[]{:S(2)}, u32[]{:S(2)}) collective-permute-start(f32[128,256]{1,0:T(8,128)S(1)} %get-tuple-element.41), channel_id=1, source_target_pairs={{0,2},{1,5},{2,0},{3,7},{4,6},{5,1},{6,4},{7,3},{8,10},{9,13},{10,... | collective-permute-start | bytes 393224 | tf_op jit(solution)/shard_map/ppermute | solution.py:177
  11.5 5.0 %collective-permute-start.3 = (f32[128,256]{1,0:T(8,128)S(1)}, f32[128,256]{1,0:T(8,128)S(1)}, u32[]{:S(2)}, u32[]{:S(2)}) collective-permute-start(f32[128,256]{1,0:T(8,128)S(1)} %add_select_fusion.5), channel_id=1, source_target_pairs={{0,8},{1,5},{2,10},{3,7},{4,12},{5,1},{6,14},{7,3},{8,0},{9,13},{1... | collective-permute-start | bytes 393224 | tf_op jit(solution)/shard_map/ppermute | solution.py:177
  13.5 5.2 %collective-permute-start.7 = (f32[128,256]{1,0:T(8,128)S(1)}, f32[128,256]{1,0:T(8,128)S(1)}, u32[]{:S(2)}, u32[]{:S(2)}) collective-permute-start(f32[128,256]{1,0:T(8,128)S(1)} %collective-permute-done.6), channel_id=1, source_target_pairs={{0,2},{1,3},{2,0},{3,1},{4,6},{5,7},{6,4},{7,5},{8,10},{9,11},{10,... | collective-permute-start | bytes 393224 | tf_op jit(solution)/shard_map/ppermute | solution.py:177
  16.6 5.0 %collective-permute-start.4 = (f32[128,256]{1,0:T(8,128)S(1)}, f32[128,256]{1,0:T(8,128)S(1)}, u32[]{:S(2)}, u32[]{:S(2)}) collective-permute-start(f32[128,256]{1,0:T(8,128)S(1)} %add_select_fusion.3), channel_id=1, source_target_pairs={{0,4},{1,3},{2,6},{3,1},{4,0},{5,7},{6,2},{7,5},{8,12},{9,11},{10,... | collective-permute-start | bytes 393224 | tf_op jit(solution)/shard_map/ppermute | solution.py:177
  18.7 3.7 %collective-permute-start.8 = (f32[128,256]{1,0:T(8,128)S(1)}, f32[128,256]{1,0:T(8,128)S(1)}, u32[]{:S(2)}, u32[]{:S(2)}) collective-permute-start(f32[128,256]{1,0:T(8,128)S(1)} %add_select_fusion.2.own_ref), channel_id=1, source_target_pairs={{0,1},{1,0},{2,3},{3,2},{4,5},{5,4},{6,7},{7,6},{8,9},{9,8},{10,11... | collective-permute-start | bytes 393224 | tf_op jit(solution)/shard_map/ppermute | solution.py:177
  21.7 1.7 %collective-permute-start.5 = (f32[128,256]{1,0:T(8,128)S(1)}, f32[128,256]{1,0:T(8,128)S(1)}, u32[]{:S(2)}, u32[]{:S(2)}) collective-permute-start(f32[128,256]{1,0:T(8,128)S(1)} %add.51.own_ref), channel_id=1, source_target_pairs={{0,1},{1,0},{2,3},{3,2},{4,5},{5,4},{6,7},{7,6},{8,9},{9,8},{10,11... | collective-permute-start | bytes 393224 | tf_op jit(solution)/shard_map/ppermute | solution.py:177
  22.4 1.0 %copy-start.2 = (f32[1024]{0:T(1024)S(1)}, f32[1024]{0:T(1024)}, u32[]{:S(2)}) copy-start(f32[1024]{0:T(1024)} %param.9) | copy-start | bytes 12292
  24.3 1.6 %collective-permute-start.9 = (f32[2,128,256]{2,1,0:T(8,128)S(1)}, f32[2,128,256]{2,1,0:T(8,128)S(1)}, u32[]{:S(2)}, u32[]{:S(2)}) collective-permute-start(f32[2,128,256]{2,1,0:T(8,128)S(1)} %get-tuple-element.35), channel_id=1, source_target_pairs={{0,1},{1,0},{2,3},{3,2},{4,5},{5,4},{6,7},{7,6},{8,9},{9,8},{10,11... | collective-permute-start | bytes 786440 | tf_op jit(solution)/shard_map/ppermute | solution.py:177
  25.9 5.0 %collective-permute-start.11 = (f32[128,256]{1,0:T(8,128)S(1)}, f32[128,256]{1,0:T(8,128)S(1)}, u32[]{:S(2)}, u32[]{:S(2)}) collective-permute-start(f32[128,256]{1,0:T(8,128)S(1)} %get-tuple-element.40), channel_id=1, source_target_pairs={{0,4},{1,25},{2,6},{3,27},{4,0},{5,29},{6,2},{7,31},{8,12},{9,17},... | collective-permute-start | bytes 393224 | tf_op jit(solution)/shard_map/ppermute | solution.py:177
  27.3 5.0 %collective-permute-start.10 = (f32[128,256]{1,0:T(8,128)S(1)}, f32[128,256]{1,0:T(8,128)S(1)}, u32[]{:S(2)}, u32[]{:S(2)}) collective-permute-start(f32[128,256]{1,0:T(8,128)S(1)} %get-tuple-element.40), channel_id=1, source_target_pairs={{0,2},{1,17},{2,0},{3,19},{4,6},{5,21},{6,4},{7,23},{8,10},{9,25},... | collective-permute-start | bytes 393224 | tf_op jit(solution)/shard_map/ppermute | solution.py:177
  28.7 5.0 %collective-permute-start.15 = (f32[128,256]{1,0:T(8,128)S(1)}, f32[128,256]{1,0:T(8,128)S(1)}, u32[]{:S(2)}, u32[]{:S(2)}) collective-permute-start(f32[128,256]{1,0:T(8,128)S(1)} %get-tuple-element.39), channel_id=1, source_target_pairs={{0,2},{1,5},{2,0},{3,7},{4,6},{5,1},{6,4},{7,3},{8,10},{9,13},{10,... | collective-permute-start | bytes 393224 | tf_op jit(solution)/shard_map/ppermute | solution.py:177
  32.3 5.0 %collective-permute-start.12 = (f32[128,256]{1,0:T(8,128)S(1)}, f32[128,256]{1,0:T(8,128)S(1)}, u32[]{:S(2)}, u32[]{:S(2)}) collective-permute-start(f32[128,256]{1,0:T(8,128)S(1)} %add_select_fusion.4), channel_id=1, source_target_pairs={{0,8},{1,5},{2,10},{3,7},{4,12},{5,1},{6,14},{7,3},{8,0},{9,13},{1... | collective-permute-start | bytes 393224 | tf_op jit(solution)/shard_map/ppermute | solution.py:177
  33.7 5.1 %collective-permute-start.16 = (f32[128,256]{1,0:T(8,128)S(1)}, f32[128,256]{1,0:T(8,128)S(1)}, u32[]{:S(2)}, u32[]{:S(2)}) collective-permute-start(f32[128,256]{1,0:T(8,128)S(1)} %collective-permute-done.15), channel_id=1, source_target_pairs={{0,2},{1,3},{2,0},{3,1},{4,6},{5,7},{6,4},{7,5},{8,10},{9,11},{10,... | collective-permute-start | bytes 393224 | tf_op jit(solution)/shard_map/ppermute | solution.py:177
  37.3 5.0 %collective-permute-start.13 = (f32[128,256]{1,0:T(8,128)S(1)}, f32[128,256]{1,0:T(8,128)S(1)}, u32[]{:S(2)}, u32[]{:S(2)}) collective-permute-start(f32[128,256]{1,0:T(8,128)S(1)} %add_select_fusion.1), channel_id=1, source_target_pairs={{0,4},{1,3},{2,6},{3,1},{4,0},{5,7},{6,2},{7,5},{8,12},{9,11},{10,... | collective-permute-start | bytes 393224 | tf_op jit(solution)/shard_map/ppermute | solution.py:177
  38.8 4.1 %collective-permute-start.17 = (f32[128,256]{1,0:T(8,128)S(1)}, f32[128,256]{1,0:T(8,128)S(1)}, u32[]{:S(2)}, u32[]{:S(2)}) collective-permute-start(f32[128,256]{1,0:T(8,128)S(1)} %add_select_fusion.own_ref), channel_id=1, source_target_pairs={{0,1},{1,0},{2,3},{3,2},{4,5},{5,4},{6,7},{7,6},{8,9},{9,8},{10,11... | collective-permute-start | bytes 393224 | tf_op jit(solution)/shard_map/ppermute | solution.py:177
  42.4 1.5 %collective-permute-start.14 = (f32[128,256]{1,0:T(8,128)S(1)}, f32[128,256]{1,0:T(8,128)S(1)}, u32[]{:S(2)}, u32[]{:S(2)}) collective-permute-start(f32[128,256]{1,0:T(8,128)S(1)} %add.58.own_ref), channel_id=1, source_target_pairs={{0,1},{1,0},{2,3},{3,2},{4,5},{5,4},{6,7},{7,6},{8,9},{9,8},{10,11... | collective-permute-start | bytes 393224 | tf_op jit(solution)/shard_map/ppermute | solution.py:177

commit v5 on v4

v5 whole, which is shorter than its diff:
```python
import functools
import math

import jax
import jax.numpy as jnp
from jax import lax
from jax.experimental import pallas as pl
from jax.experimental.pallas import tpu as pltpu
from jax.sharding import PartitionSpec as P

AXIS = "rows"
LEAF = 512
CHUNK = 256
SPAN = 128
F32 = jnp.float32
BF16 = jnp.bfloat16


VMEM = pl.BlockSpec(memory_space=pltpu.VMEM)
HBM = pl.BlockSpec(memory_space=pltpu.HBM)


def call(kernel, outs, arrays, flops, arrays_in=VMEM, outs_in=VMEM, scratch=()):
    moved = sum(math.prod(a.shape) * a.dtype.itemsize for a in (*arrays, *outs))
    return pl.pallas_call(
        kernel,
        out_shape=outs,
        in_specs=[arrays_in] * len(arrays),
        out_specs=[outs_in] * len(outs),
        scratch_shapes=scratch,
        compiler_params=pltpu.CompilerParams(vmem_limit_bytes=24 * 2**20),
        cost_estimate=pl.CostEstimate(flops=flops, bytes_accessed=moved, transcendentals=0),
    )(*arrays)


def index_bits():
    return lax.axis_size(AXIS).bit_length() - 1


def transposed_dot(basis, vec):
    return lax.dot_general(basis, vec, (((0,), (0,)), ((), ())), preferred_element_type=F32)


def parity_of():
    return lax.axis_index(AXIS) % 2


def own_level(slot):
    return 1 - parity_of() + 2 * slot


def other_level(slot):
    return parity_of() + 2 * slot


def first_kernel(bases_in, vec_in, out_ref, bases_ref, vec_ref, sems):
    rank = bases_in.shape[2]

    def basis_copy(level, sem):
        return pltpu.make_async_copy(bases_in.at[level], bases_ref.at[level], sem)

    copies = [pltpu.make_async_copy(vec_in, vec_ref, sems.at[0])]
    copies += [basis_copy(other_level(slot), sems.at[1 + slot]) for slot in range(2)]
    later = [basis_copy(own_level(slot), sems.at[3 + slot]) for slot in range(2)]
    for copy in copies + later:
        copy.start()
    for copy in copies:
        copy.wait()
    basis = jnp.concatenate([bases_ref[other_level(slot)] for slot in range(2)], axis=1)
    proj = transposed_dot(basis, vec_ref[...])
    out_ref[0] = proj[:rank]
    out_ref[1] = proj[rank:]
    for copy in later:
        copy.wait()


def kept_kernel(bases_ref, vec_ref, high_ref, low_ref):
    rank = bases_ref.shape[2]
    both = jnp.concatenate([bases_ref[own_level(slot)] for slot in range(2)], axis=1)
    proj = transposed_dot(both, vec_ref[...])
    high_ref[...] = proj[:rank]
    low_ref[...] = proj[rank:]


def prepare_kernel(couplings_ref, bases_ref, oriented_ref, turned_ref):
    myself = lax.axis_index(AXIS)
    bits = index_bits()
    rank = bases_ref.shape[2]
    for level in range(bases_ref.shape[0]):
        coupling = couplings_ref[(1 << level) - 1 + (myself >> bits - level)].astype(F32)
        side = myself >> bits - level - 1 & 1
        oriented_ref[level] = jnp.where(side == 0, coupling, coupling.T).astype(BF16)
    for slot in range(2):
        turned_ref[pl.ds(slot * rank, rank), :] = bases_ref[other_level(slot)].T
        turned_ref[pl.ds((2 + slot) * rank, rank), :] = bases_ref[own_level(slot)].T


def weighted(weights_ref, values, rows):
    columns = weights_ref[...].T
    blocks = range(rows.start // SPAN, rows.stop // SPAN)
    column = jnp.concatenate([columns[:, block : block + 1] for block in blocks], axis=0)
    return (column * values).astype(BF16)


def base_kernel(leaves_ref, vec_ref, weights_ref, turned_ref, part_ref, base_ref):
    total = None
    for leaf in range(vec_ref.shape[0] // LEAF):
        rows = slice(leaf * LEAF, (leaf + 1) * LEAF)
        near = jnp.dot(leaves_ref[rows, :], vec_ref[rows, :], preferred_element_type=F32)
        part_ref[rows, :] = near
        term = jnp.dot(turned_ref[:, rows], weighted(weights_ref, near, rows), preferred_element_type=F32)
        total = term if total is None else total + term
    base_ref[...] = total


def gram_kernel(bases_ref, weights_ref, turned_ref, keep_ref, send_ref):
    rank, rows_dev = bases_ref.shape[2], bases_ref.shape[1]
    total = None
    for chunk in range(rows_dev // CHUNK):
        rows = slice(chunk * CHUNK, (chunk + 1) * CHUNK)
        order = [other_level(slot) for slot in range(2)] + [own_level(slot) for slot in range(2)]
        basis = jnp.concatenate([bases_ref[level, rows, :] for level in order], axis=1)
        basis = weighted(weights_ref, basis.astype(F32), rows)
        term = jnp.dot(turned_ref[:, rows], basis, preferred_element_type=F32)
        total = term if total is None else total + term
    keep_ref[...] = total[:, 2 * rank :]
    send_ref[: 2 * rank, :] = total[2 * rank :, : 2 * rank]
    send_ref[2 * rank :, :] = total[: 2 * rank, : 2 * rank]


def coefficients(oriented_ref, level, factor, sums):
    quotient = (sums * factor).astype(BF16)
    return jnp.dot(oriented_ref[level], quotient, preferred_element_type=F32).astype(BF16)


def own_coefficients(oriented_ref, slot, sums, factors):
    factor = jnp.where(parity_of() == 1, factors[2 * slot], factors[2 * slot + 1])
    return coefficients(oriented_ref, own_level(slot), factor, sums)


def other_coefficients(oriented_ref, slot, sums, factors):
    factor = jnp.where(parity_of() == 1, factors[2 * slot + 1], factors[2 * slot])
    return coefficients(oriented_ref, other_level(slot), factor, sums)


def low_kernel(factors, oriented_ref, low_ref, keep_ref, got_ref, base_ref, sums_ref, gram_ref):
    gram = keep_ref[...] + got_ref[...]
    rough = gram.astype(BF16)
    rest = (gram - rough.astype(F32)).astype(BF16)
    rank = low_ref.shape[0]
    both = jnp.concatenate([rough[:, rank:], rest[:, rank:]], axis=1)
    coeffs = own_coefficients(oriented_ref, 1, low_ref[...], factors)
    delta = jnp.dot(both, jnp.concatenate([coeffs] * 2, axis=0), preferred_element_type=F32)
    sums_ref[...] = base_ref[...] + delta
    gram_ref[:, :rank] = rough[:, :rank]
    gram_ref[:, rank:] = rest[:, :rank]


def middle_kernel(factors, oriented_ref, high_ref, gram_ref, sums_ref, send_ref, keep_high_ref, keep_low_ref):
    coeffs = own_coefficients(oriented_ref, 0, high_ref[...], factors)
    delta = jnp.dot(gram_ref[...], jnp.concatenate([coeffs] * 2, axis=0), preferred_element_type=F32)
    proj = sums_ref[...] + delta
    rank = high_ref.shape[0]
    send_ref[0] = proj[:rank]
    send_ref[1] = proj[rank : 2 * rank]
    keep_high_ref[...] = proj[2 * rank : 3 * rank]
    keep_low_ref[...] = proj[3 * rank :]


def second_part_kernel(
    factors, oriented_ref, high_ref, low_ref, high_other_ref, low_other_ref, bases_ref, part_ref, weights_ref, leaves_ref, out_ref, buf
):
    pieces = []
    order = []
    for slot, (own_ref, other_ref) in enumerate(((high_ref, high_other_ref), (low_ref, low_other_ref))):
        pieces += [own_coefficients(oriented_ref, slot, own_ref[...], factors)]
        pieces += [other_coefficients(oriented_ref, slot, other_ref[...], factors)]
        order += [own_level(slot), other_level(slot)]
    coeffs = jnp.concatenate(pieces, axis=0)
    for leaf in range(part_ref.shape[0] // LEAF):
        rows = slice(leaf * LEAF, (leaf + 1) * LEAF)
        basis = jnp.concatenate([bases_ref[level, rows, :] for level in order], axis=1)
        first = part_ref[rows, :] + jnp.dot(basis, coeffs, preferred_element_type=F32)
        buf[rows, :] = weighted(weights_ref, first, rows)
        out_ref[rows, :] = jnp.dot(leaves_ref[rows, :], buf[rows, :], preferred_element_type=F32)


def near_result_kernel(factors, oriented_ref, high_ref, low_ref, other_ref, bases_ref, part_ref, out_ref):
    pieces = [
        own_coefficients(oriented_ref, 0, high_ref[...], factors),
        own_coefficients(oriented_ref, 1, low_ref[...], factors),
        other_coefficients(oriented_ref, 1, other_ref[...], factors),
    ]
    order = [own_level(0), own_level(1), other_level(1)]
    basis = jnp.concatenate([bases_ref[level] for level in order], axis=1)
    coeffs = jnp.concatenate(pieces, axis=0)
    out_ref[...] = part_ref[...] + jnp.dot(basis, coeffs, preferred_element_type=F32)


def result_kernel(factors, oriented_ref, other_ref, bases_ref, part_ref, result_ref, buf, sems):
    coeffs = other_coefficients(oriented_ref, 0, other_ref[...], factors)
    copies = []
    for chunk in range(part_ref.shape[0] // CHUNK):
        rows = pl.ds(chunk * CHUNK, CHUNK)
        basis = bases_ref[other_level(0), rows, :]
        total = part_ref[rows, :] + jnp.dot(basis, coeffs, preferred_element_type=F32)
        buf[rows, :] = total.astype(BF16)
        copies.append(pltpu.make_async_copy(buf.at[rows, :], result_ref.at[rows, :], sems.at[chunk]))
        copies[-1].start()
    for copy in copies:
        copy.wait()


def on_device(signal, leaves, bases, couplings, weights):
    count = lax.axis_size(AXIS)
    bits = index_bits()
    rows_dev, width = signal.shape
    levels, _, rank = bases.shape
    odd = parity_of() == 1
    far1, far2, far3, far4 = (1 << (bits - level - 1) for level in range(levels))
    factors = [1.0 / math.sqrt(rows_dev * (count >> level + 1) * rank) for level in range(levels)]
    weight_rows = weights.reshape(rows_dev // SPAN, SPAN)
    mults = rows_dev * width * rank * 2
    chunks = rows_dev // CHUNK
    sums_shape = jax.ShapeDtypeStruct((rank, width), F32)
    pair_shape = jax.ShapeDtypeStruct((2, rank, width), F32)
    part_shape = jax.ShapeDtypeStruct((rows_dev, width), F32)
    gram_shape = jax.ShapeDtypeStruct((levels * rank, 2 * rank), F32)

    def swap(value, odd_mask, even_mask):
        pairs = [(source, source ^ (odd_mask if source % 2 else even_mask)) for source in range(count)]
        return lax.ppermute(value, AXIS, pairs)

    def beside(arrays, *riders):
        return lax.optimization_barrier((*arrays, *riders))

    def begin(send, high, low):
        got = swap(send, 1, 1)
        high = high + got[0]
        low = low + got[1]
        for bit in range(1, bits - levels):
            high = high + swap(high, 1 << bit, 1 << bit)
            low = low + swap(low, 1 << bit, 1 << bit)
        return high, low

    def rounds(high, low, rider_one, rider_two, rider_three, passenger=None):
        near = swap(high, far1, far4)
        across = swap(high, far1 | far2, far3)
        near, across, *ridden = beside((near, across), *rider_one())
        high = jnp.where(odd, near + across, high + near)
        got = swap(high, far3, far2)
        low, passenger = beside((swap(low, far3, far4),), ridden.pop() if passenger is None else passenger)
        passenger = swap(passenger, 1, 1)
        got, *ridden = beside((got,), *rider_two(*ridden))
        high = jnp.where(odd, high + got, got)
        low = jnp.where(odd, low + swap(low, far4, far4), low)
        got = swap(high, far4, far3)
        got, *ridden = beside((got,), *rider_three(low, passenger, *ridden))
        return high + got, low, *ridden

    send, bases, signal = call(
        first_kernel,
        [pair_shape, jax.ShapeDtypeStruct(bases.shape, BF16), jax.ShapeDtypeStruct(signal.shape, BF16)],
        [pltpu.with_memory_space_constraint(array, pltpu.HBM) for array in (bases, signal)],
        2 * mults,
        arrays_in=HBM,
        scratch=[pltpu.SemaphoreType.DMA((5,))],
    )
    kept = call(kept_kernel, [sums_shape] * 2, [bases, signal], 2 * mults)

    def first_riders():
        oriented, turned = call(
            prepare_kernel,
            [
                jax.ShapeDtypeStruct((levels, rank, rank), BF16),
                jax.ShapeDtypeStruct((levels * rank, rows_dev), BF16),
            ],
            [couplings, bases],
            mults,
        )
        keep, send = call(gram_kernel, [gram_shape] * 2, [bases, weight_rows, turned], 2 * levels * mults)
        return oriented, turned, keep, send

    def second_riders(oriented, turned, keep):
        part, base = call(
            base_kernel,
            [part_shape, jax.ShapeDtypeStruct((levels * rank, width), F32)],
            [leaves, signal, weight_rows, turned],
            (LEAF // rank + levels) * mults,
        )
        return oriented, keep, part, base

    def third_riders(low, got, oriented, keep, part, base):
        sums, gram = call(
            functools.partial(low_kernel, factors),
            [
                jax.ShapeDtypeStruct((levels * rank, width), F32),
                jax.ShapeDtypeStruct((levels * rank, 2 * rank), BF16),
            ],
            [oriented, low, keep, got, base],
            mults,
        )
        return oriented, part, sums, gram

    high, low, oriented, part, sums, gram = rounds(
        *begin(send, *kept), first_riders, second_riders, third_riders
    )
    high, low_other = beside((high, swap(low, 1, 1)))
    send, *kept = call(
        functools.partial(middle_kernel, factors),
        [pair_shape, sums_shape, sums_shape],
        [oriented, high, gram, sums],
        mults,
    )
    next_high, next_low, high, low = beside(begin(send, *kept), high, low)

    def second_part(_, high_other):
        return call(
            functools.partial(second_part_kernel, factors),
            [part_shape],
            [oriented, high, low, high_other, low_other, bases, part, weight_rows, leaves],
            (LEAF // rank + levels) * mults,
            scratch=[pltpu.VMEM((rows_dev, width), BF16)],
        )

    high, low, part = rounds(next_high, next_low, tuple, tuple, second_part, high)
    low_other, high_other = swap(low, 1, 1), swap(high, 1, 1)
    (part,) = call(
        functools.partial(near_result_kernel, factors),
        [part_shape],
        [oriented, high, low, low_other, bases, part],
        3 * mults,
    )
    (result,) = call(
        functools.partial(result_kernel, factors),
        [jax.ShapeDtypeStruct((rows_dev, width), BF16)],
        [oriented, high_other, bases, part],
        mults,
        outs_in=HBM,
        scratch=[pltpu.VMEM((rows_dev, width), BF16), pltpu.SemaphoreType.DMA((chunks,))],
    )
    return result


def solution(mesh):
    in_specs = (P("rows", None), P("rows", None), P(None, "rows", None), P(), P("rows"))
    out_specs = P("rows", None)
    return jax.shard_map(
        on_device, mesh=mesh, in_specs=in_specs, out_specs=out_specs, check_vma=False
    )
```

time: 45.3 us -> 43.9 us (0.969)
  waiting for transfers between devices: 18.8 us -> 13.8 us
  Pallas kernels: 6.49 us -> 8.46 us
  starting transfers between devices: 19.5 us -> 20.8 us
    ppermute x18 -> x19, waiting for transfers between devices: 18.8 us -> 13.8 us  [swap(): return lax.ppermute(value, AXIS, pairs)]
    pallas_call x8 -> x10, Pallas kernels: 6.49 us -> 8.46 us  [call(): pl.pallas_call(kernel, out_shape=outs, in_specs=[arrays_in] * len(arrays)...]
    ppermute x18 -> x19, starting transfers between devices: 19.5 us -> 20.8 us  [swap(): return lax.ppermute(value, AXIS, pairs)]
  transfers between devices with their start and end apart: 18 -> 19, of which waited for: 16 -> 12; matrix products, arithmetic and copies ran while one was open for 0% -> 0% of each run, Pallas kernels for 6% -> 12%
where the time goes in v5:
time: 43.9 us; the launch traced here: 43.7 us
  starting transfers between devices  20.8 us (47%)
  waiting for transfers between devices  13.8 us (31%)
  Pallas kernels  8.46 us (19%)
    ppermute x19, starting transfers between devices, swap(): return lax.ppermute(value, AXIS, pairs)  20.8 us
    ppermute x19, waiting for transfers between devices, swap(): return lax.ppermute(value, AXIS, pairs)  13.8 us
    pallas_call x10, Pallas kernels, call(): pl.pallas_call(kernel, out_shape=outs, in_specs=[arrays_in] * len(arrays)...  8.46 us
  transfers between devices with their start and end apart: 19, of which 12 were waited for; matrix products, arithmetic and copies ran while one was open for 0% of the time, Pallas kernels for 12%

profile of v5, /device:TPU:0, one launch (start us, length us, event | category | flops | bytes accessed | tf_op | source)
XLA Modules:
  0.0 43.7 jit_solution(14581914396186339441)
XLA Ops:
  0.0 1.6 %shard_map.55 = (f32[2,128,256]{2,1,0:T(8,128)S(1)}, bf16[4,1024,128]{2,1,0:T(8,128)(2,1)S(1)}, bf16[1024,256]{1,0:T(8,128)(2,1)S(1)}) custom-call(bf16[4,1024,128]{2,1,0:T(8,128)(2,1)} %bases_in.1, bf16[1024,256]{1,0:T(8,128)(2,1)} %vec_in.1), custom_call_target="tpu_custom_call" | custom-call | flops 134217728 | bytes 3407872 | tf_op jit(solution)/shard_map/pallas_call | solution.py:25
  2.5 0.8 %collective-permute-done = f32[2,128,256]{2,1,0:T(8,128)S(1)} collective-permute-done((f32[2,128,256]{2,1,0:T(8,128)S(1)}, f32[2,128,256]{2,1,0:T(8,128)S(1)}, u32[]{:S(2)}, u32[]{:S(2)}) %collective-permute-start) | collective-permute-done | bytes 262176 | tf_op jit(solution)/shard_map/ppermute | solution.py:232
  3.3 2.9 %collective-permute-start.1 = (f32[128,256]{1,0:T(8,128)S(1)}, f32[128,256]{1,0:T(8,128)S(1)}, u32[]{:S(2)}, u32[]{:S(2)}) collective-permute-start(f32[128,256]{1,0:T(8,128)S(1)} %get-tuple-element.100), channel_id=1, source_target_pairs={{0,2},{1,17},{2,0},{3,19},{4,6},{5,21},{6,4},{7,23},{8,10},{9,25},... | collective-permute-start | bytes 393224 | tf_op jit(solution)/shard_map/ppermute | solution.py:232
  6.2 1.5 %collective-permute-start.2 = (f32[128,256]{1,0:T(8,128)S(1)}, f32[128,256]{1,0:T(8,128)S(1)}, u32[]{:S(2)}, u32[]{:S(2)}) collective-permute-start(f32[128,256]{1,0:T(8,128)S(1)} %get-tuple-element.100), channel_id=1, source_target_pairs={{0,4},{1,25},{2,6},{3,27},{4,0},{5,29},{6,2},{7,31},{8,12},{9,17},... | collective-permute-start | bytes 393224 | tf_op jit(solution)/shard_map/ppermute | solution.py:232
  8.4 1.0 %shard_map.58 = (f32[512,256]{1,0:T(8,128)S(1)}, f32[512,256]{1,0:T(8,128)S(1)}) custom-call(bf16[4,1024,128]{2,1,0:T(8,128)(2,1)S(1)} %get-tuple-element.51.bases_ref, f32[8,128]{1,0:T(8,128)S(1)} %bitcast.17, bf16[512,1024]{1,0:T(8,128)(2,1)S(1)} %get-tuple-element.63.turned_ref), custom_call_target="tpu_custom_call" | custom-call | flops 536870912 | bytes 3149824 | tf_op jit(solution)/shard_map/pallas_call | solution.py:25
  10.0 1.2 %collective-permute-done.2 = f32[128,256]{1,0:T(8,128)S(1)} collective-permute-done((f32[128,256]{1,0:T(8,128)S(1)}, f32[128,256]{1,0:T(8,128)S(1)}, u32[]{:S(2)}, u32[]{:S(2)}) %collective-permute-start.2) | collective-permute-done | bytes 131104 | tf_op jit(solution)/shard_map/ppermute | solution.py:232
  11.2 1.6 %collective-permute-start.3 = (f32[128,256]{1,0:T(8,128)S(1)}, f32[128,256]{1,0:T(8,128)S(1)}, u32[]{:S(2)}, u32[]{:S(2)}) collective-permute-start(f32[128,256]{1,0:T(8,128)S(1)} %add_select_fusion.5), channel_id=1, source_target_pairs={{0,8},{1,5},{2,10},{3,7},{4,12},{5,1},{6,14},{7,3},{8,0},{9,13},{1... | collective-permute-start | bytes 393224 | tf_op jit(solution)/shard_map/ppermute | solution.py:232
  12.9 1.6 %collective-permute-done.5 = f32[128,256]{1,0:T(8,128)S(1)} collective-permute-done((f32[128,256]{1,0:T(8,128)S(1)}, f32[128,256]{1,0:T(8,128)S(1)}, u32[]{:S(2)}, u32[]{:S(2)}) %collective-permute-start.5) | collective-permute-done | bytes 131104 | tf_op jit(solution)/shard_map/ppermute | solution.py:232
  15.5 1.3 %shard_map.59 = (f32[1024,256]{1,0:T(8,128)S(1)}, f32[512,256]{1,0:T(8,128)S(1)}) custom-call(bf16[1024,512]{1,0:T(8,128)(2,1)S(1)} %copy-done, bf16[1024,256]{1,0:T(8,128)(2,1)S(1)} %get-tuple-element.52.vec_ref, f32[8,128]{1,0:T(8,128)S(1)} %bitcast.18, bf16[512,1024]{1,0:T(8,128)(2,1)S(1)} %get-tuple-element.63.turned_ref), custom_call_target="tpu_custom_call" | custom-call | flops 536870912 | bytes 4198400 | tf_op jit(solution)/shard_map/pallas_call | solution.py:25
  16.8 1.4 %collective-permute-start.4 = (f32[128,256]{1,0:T(8,128)S(1)}, f32[128,256]{1,0:T(8,128)S(1)}, u32[]{:S(2)}, u32[]{:S(2)}) collective-permute-start(f32[128,256]{1,0:T(8,128)S(1)} %add_select_fusion.3), channel_id=1, source_target_pairs={{0,4},{1,3},{2,6},{3,1},{4,0},{5,7},{6,2},{7,5},{8,12},{9,11},{10,... | collective-permute-start | bytes 393224 | tf_op jit(solution)/shard_map/ppermute | solution.py:232
  18.3 1.4 %collective-permute-done.6 = f32[128,256]{1,0:T(8,128)S(1)} collective-permute-done((f32[128,256]{1,0:T(8,128)S(1)}, f32[128,256]{1,0:T(8,128)S(1)}, u32[]{:S(2)}, u32[]{:S(2)}) %collective-permute-start.6) | collective-permute-done | bytes 131104 | tf_op jit(solution)/shard_map/ppermute | solution.py:232
  20.2 1.7 %collective-permute-done.4 = f32[128,256]{1,0:T(8,128)S(1)} collective-permute-done((f32[128,256]{1,0:T(8,128)S(1)}, f32[128,256]{1,0:T(8,128)S(1)}, u32[]{:S(2)}, u32[]{:S(2)}) %collective-permute-start.4) | collective-permute-done | bytes 131104 | tf_op jit(solution)/shard_map/ppermute | solution.py:232
  22.4 1.5 %collective-permute-done.9 = f32[2,128,256]{2,1,0:T(8,128)S(1)} collective-permute-done((f32[2,128,256]{2,1,0:T(8,128)S(1)}, f32[2,128,256]{2,1,0:T(8,128)S(1)}, u32[]{:S(2)}, u32[]{:S(2)}) %collective-permute-start.9) | collective-permute-done | bytes 262176 | tf_op jit(solution)/shard_map/ppermute | solution.py:232
  23.9 1.1 %collective-permute-start.10 = (f32[128,256]{1,0:T(8,128)S(1)}, f32[128,256]{1,0:T(8,128)S(1)}, u32[]{:S(2)}, u32[]{:S(2)}) collective-permute-start(f32[128,256]{1,0:T(8,128)S(1)} %get-tuple-element.85), channel_id=1, source_target_pairs={{0,2},{1,17},{2,0},{3,19},{4,6},{5,21},{6,4},{7,23},{8,10},{9,25},... | collective-permute-start | bytes 393224 | tf_op jit(solution)/shard_map/ppermute | solution.py:232
  25.8 1.6 %collective-permute-start.14 = (f32[128,256]{1,0:T(8,128)S(1)}, f32[128,256]{1,0:T(8,128)S(1)}, u32[]{:S(2)}, u32[]{:S(2)}) collective-permute-start(f32[128,256]{1,0:T(8,128)S(1)} %get-tuple-element.90), channel_id=1, source_target_pairs={{0,2},{1,5},{2,0},{3,7},{4,6},{5,1},{6,4},{7,3},{8,10},{9,13},{10,... | collective-permute-start | bytes 393224 | tf_op jit(solution)/shard_map/ppermute | solution.py:232
  27.4 1.6 %collective-permute-done.10 = f32[128,256]{1,0:T(8,128)S(1)} collective-permute-done((f32[128,256]{1,0:T(8,128)S(1)}, f32[128,256]{1,0:T(8,128)S(1)}, u32[]{:S(2)}, u32[]{:S(2)}) %collective-permute-start.10) | collective-permute-done | bytes 131104 | tf_op jit(solution)/shard_map/ppermute | solution.py:232
  29.0 1.0 %collective-permute-done.11 = f32[128,256]{1,0:T(8,128)S(1)} collective-permute-done((f32[128,256]{1,0:T(8,128)S(1)}, f32[128,256]{1,0:T(8,128)S(1)}, u32[]{:S(2)}, u32[]{:S(2)}) %collective-permute-start.11) | collective-permute-done | bytes 131104 | tf_op jit(solution)/shard_map/ppermute | solution.py:232
  30.0 2.4 %collective-permute-start.12 = (f32[128,256]{1,0:T(8,128)S(1)}, f32[128,256]{1,0:T(8,128)S(1)}, u32[]{:S(2)}, u32[]{:S(2)}) collective-permute-start(f32[128,256]{1,0:T(8,128)S(1)} %add_select_fusion.4), channel_id=1, source_target_pairs={{0,8},{1,5},{2,10},{3,7},{4,12},{5,1},{6,14},{7,3},{8,0},{9,13},{1... | collective-permute-start | bytes 393224 | tf_op jit(solution)/shard_map/ppermute | solution.py:232
  32.4 1.8 %collective-permute-start.17 = (f32[128,256]{1,0:T(8,128)S(1)}, f32[128,256]{1,0:T(8,128)S(1)}, u32[]{:S(2)}, u32[]{:S(2)}) collective-permute-start(f32[128,256]{1,0:T(8,128)S(1)} %collective-permute-done.14), channel_id=1, source_target_pairs={{0,2},{1,3},{2,0},{3,1},{4,6},{5,7},{6,4},{7,5},{8,10},{9,11},{10,... | collective-permute-start | bytes 393224 | tf_op jit(solution)/shard_map/ppermute | solution.py:232
  35.3 1.5 %collective-permute-start.13 = (f32[128,256]{1,0:T(8,128)S(1)}, f32[128,256]{1,0:T(8,128)S(1)}, u32[]{:S(2)}, u32[]{:S(2)}) collective-permute-start(f32[128,256]{1,0:T(8,128)S(1)} %add_select_fusion.1), channel_id=1, source_target_pairs={{0,4},{1,3},{2,6},{3,1},{4,0},{5,7},{6,2},{7,5},{8,12},{9,11},{10,... | collective-permute-start | bytes 393224 | tf_op jit(solution)/shard_map/ppermute | solution.py:232
  36.9 1.6 %collective-permute-done.17 = f32[128,256]{1,0:T(8,128)S(1)} collective-permute-done((f32[128,256]{1,0:T(8,128)S(1)}, f32[128,256]{1,0:T(8,128)S(1)}, u32[]{:S(2)}, u32[]{:S(2)}) %collective-permute-start.17) | collective-permute-done | bytes 131104 | tf_op jit(solution)/shard_map/ppermute | solution.py:232
  38.7 1.2 %shard_map.62.part_ref = f32[1024,256]{1,0:T(8,128)S(1)} custom-call(bf16[4,128,128]{2,1,0:T(8,128)(2,1)S(1)} %get-tuple-element.77.oriented_ref, f32[128,256]{1,0:T(8,128)S(1)} %add.53.high_ref, f32[128,256]{1,0:T(8,128)S(1)} %add_select_fusion.2.low_ref, f32[128,256]{1,0:T(8,128)S(1)} %collective-permute-done.15.high_other_ref, ...), custom_call_target="tpu_custom_call" | custom-call | flops 536870912 | bytes 4853760 | tf_op jit(solution)/shard_map/pallas_call | solution.py:25
  40.4 1.2 %collective-permute-start.16 = (f32[128,256]{1,0:T(8,128)S(1)}, f32[128,256]{1,0:T(8,128)S(1)}, u32[]{:S(2)}, u32[]{:S(2)}) collective-permute-start(f32[128,256]{1,0:T(8,128)S(1)} %add.59.high_ref), channel_id=1, source_target_pairs={{0,1},{1,0},{2,3},{3,2},{4,5},{5,4},{6,7},{7,6},{8,9},{9,8},{10,11... | collective-permute-start | bytes 393224 | tf_op jit(solution)/shard_map/ppermute | solution.py:232
  42.6 1.2 %shard_map.64 = bf16[1024,256]{1,0:T(8,128)(2,1)} custom-call(bf16[4,128,128]{2,1,0:T(8,128)(2,1)S(1)} %get-tuple-element.77.oriented_ref, f32[128,256]{1,0:T(8,128)S(1)} %collective-permute-done.16.other_ref, bf16[4,1024,128]{2,1,0:T(8,128)(2,1)S(1)} %get-tuple-element.51.bases_ref, f32[1024,256]{1,0:T(8,128)S(1)} %shard_map.63.part_ref), custom_call_target="tpu_custom_call" | custom-call | flops 67108864 | bytes 2883584 | tf_op jit(solution)/shard_map/pallas_call | solution.py:25
  (40 shorter events, 7.9 us)
Async XLA Ops:
  1.6 1.7 %collective-permute-start = (f32[2,128,256]{2,1,0:T(8,128)S(1)}, f32[2,128,256]{2,1,0:T(8,128)S(1)}, u32[]{:S(2)}, u32[]{:S(2)}) collective-permute-start(f32[2,128,256]{2,1,0:T(8,128)S(1)} %get-tuple-element.54), channel_id=1, source_target_pairs={{0,1},{1,0},{2,3},{3,2},{4,5},{5,4},{6,7},{7,6},{8,9},{9,8},{10,11... | collective-permute-start | bytes 786440 | tf_op jit(solution)/shard_map/ppermute | solution.py:232
  2.5 5.3 %copy-start.1 = (bf16[15,128,128]{2,1,0:T(8,128)(2,1)S(1)}, bf16[15,128,128]{2,1,0:T(8,128)(2,1)}, u32[]{:S(2)}) copy-start(bf16[15,128,128]{2,1,0:T(8,128)(2,1)} %couplings_ref.1) | copy-start | bytes 1474564
  3.3 6.7 %collective-permute-start.1 = (f32[128,256]{1,0:T(8,128)S(1)}, f32[128,256]{1,0:T(8,128)S(1)}, u32[]{:S(2)}, u32[]{:S(2)}) collective-permute-start(f32[128,256]{1,0:T(8,128)S(1)} %get-tuple-element.100), channel_id=1, source_target_pairs={{0,2},{1,17},{2,0},{3,19},{4,6},{5,21},{6,4},{7,23},{8,10},{9,25},... | collective-permute-start | bytes 393224 | tf_op jit(solution)/shard_map/ppermute | solution.py:232
  6.2 5.0 %collective-permute-start.2 = (f32[128,256]{1,0:T(8,128)S(1)}, f32[128,256]{1,0:T(8,128)S(1)}, u32[]{:S(2)}, u32[]{:S(2)}) collective-permute-start(f32[128,256]{1,0:T(8,128)S(1)} %get-tuple-element.100), channel_id=1, source_target_pairs={{0,4},{1,25},{2,6},{3,27},{4,0},{5,29},{6,2},{7,31},{8,12},{9,17},... | collective-permute-start | bytes 393224 | tf_op jit(solution)/shard_map/ppermute | solution.py:232
  7.8 0.7 %copy-start.2 = (f32[1024]{0:T(1024)S(1)}, f32[1024]{0:T(1024)}, u32[]{:S(2)}) copy-start(f32[1024]{0:T(1024)} %param.9) | copy-start | bytes 12292
  8.4 7.0 %copy-start = (bf16[1024,512]{1,0:T(8,128)(2,1)S(1)}, bf16[1024,512]{1,0:T(8,128)(2,1)}, u32[]{:S(2)}) copy-start(bf16[1024,512]{1,0:T(8,128)(2,1)} %leaves_ref.3) | copy-start | bytes 3145732
  9.4 5.0 %collective-permute-start.5 = (f32[128,256]{1,0:T(8,128)S(1)}, f32[128,256]{1,0:T(8,128)S(1)}, u32[]{:S(2)}, u32[]{:S(2)}) collective-permute-start(f32[128,256]{1,0:T(8,128)S(1)} %get-tuple-element.99), channel_id=1, source_target_pairs={{0,2},{1,5},{2,0},{3,7},{4,6},{5,1},{6,4},{7,3},{8,10},{9,13},{10,... | collective-permute-start | bytes 393224 | tf_op jit(solution)/shard_map/ppermute | solution.py:232
  11.2 5.6 %collective-permute-start.3 = (f32[128,256]{1,0:T(8,128)S(1)}, f32[128,256]{1,0:T(8,128)S(1)}, u32[]{:S(2)}, u32[]{:S(2)}) collective-permute-start(f32[128,256]{1,0:T(8,128)S(1)} %add_select_fusion.5), channel_id=1, source_target_pairs={{0,8},{1,5},{2,10},{3,7},{4,12},{5,1},{6,14},{7,3},{8,0},{9,13},{1... | collective-permute-start | bytes 393224 | tf_op jit(solution)/shard_map/ppermute | solution.py:232
  14.4 5.3 %collective-permute-start.6 = (f32[128,256]{1,0:T(8,128)S(1)}, f32[128,256]{1,0:T(8,128)S(1)}, u32[]{:S(2)}, u32[]{:S(2)}) collective-permute-start(f32[128,256]{1,0:T(8,128)S(1)} %collective-permute-done.5), channel_id=1, source_target_pairs={{0,2},{1,3},{2,0},{3,1},{4,6},{5,7},{6,4},{7,5},{8,10},{9,11},{10,... | collective-permute-start | bytes 393224 | tf_op jit(solution)/shard_map/ppermute | solution.py:232
  15.0 4.8 %collective-permute-start.7 = (f32[512,256]{1,0:T(8,128)S(1)}, f32[512,256]{1,0:T(8,128)S(1)}, u32[]{:S(2)}, u32[]{:S(2)}) collective-permute-start(f32[512,256]{1,0:T(8,128)S(1)} %get-tuple-element.73), channel_id=1, source_target_pairs={{0,1},{1,0},{2,3},{3,2},{4,5},{5,4},{6,7},{7,6},{8,9},{9,8},{10,11... | collective-permute-start | bytes 1572872 | tf_op jit(solution)/shard_map/ppermute | solution.py:232
  16.8 5.0 %collective-permute-start.4 = (f32[128,256]{1,0:T(8,128)S(1)}, f32[128,256]{1,0:T(8,128)S(1)}, u32[]{:S(2)}, u32[]{:S(2)}) collective-permute-start(f32[128,256]{1,0:T(8,128)S(1)} %add_select_fusion.3), channel_id=1, source_target_pairs={{0,4},{1,3},{2,6},{3,1},{4,0},{5,7},{6,2},{7,5},{8,12},{9,11},{10,... | collective-permute-start | bytes 393224 | tf_op jit(solution)/shard_map/ppermute | solution.py:232
  19.7 2.2 %collective-permute-start.8 = (f32[128,256]{1,0:T(8,128)S(1)}, f32[128,256]{1,0:T(8,128)S(1)}, u32[]{:S(2)}, u32[]{:S(2)}) collective-permute-start(f32[128,256]{1,0:T(8,128)S(1)} %add_select_fusion.2.low_ref), channel_id=1, source_target_pairs={{0,1},{1,0},{2,3},{3,2},{4,5},{5,4},{6,7},{7,6},{8,9},{9,8},{10,11... | collective-permute-start | bytes 393224 | tf_op jit(solution)/shard_map/ppermute | solution.py:232
  22.3 1.6 %collective-permute-start.9 = (f32[2,128,256]{2,1,0:T(8,128)S(1)}, f32[2,128,256]{2,1,0:T(8,128)S(1)}, u32[]{:S(2)}, u32[]{:S(2)}) collective-permute-start(f32[2,128,256]{2,1,0:T(8,128)S(1)} %get-tuple-element.83), channel_id=1, source_target_pairs={{0,1},{1,0},{2,3},{3,2},{4,5},{5,4},{6,7},{7,6},{8,9},{9,8},{10,11... | collective-permute-start | bytes 786440 | tf_op jit(solution)/shard_map/ppermute | solution.py:232
  23.9 5.0 %collective-permute-start.10 = (f32[128,256]{1,0:T(8,128)S(1)}, f32[128,256]{1,0:T(8,128)S(1)}, u32[]{:S(2)}, u32[]{:S(2)}) collective-permute-start(f32[128,256]{1,0:T(8,128)S(1)} %get-tuple-element.85), channel_id=1, source_target_pairs={{0,2},{1,17},{2,0},{3,19},{4,6},{5,21},{6,4},{7,23},{8,10},{9,25},... | collective-permute-start | bytes 393224 | tf_op jit(solution)/shard_map/ppermute | solution.py:232
  25.0 5.0 %collective-permute-start.11 = (f32[128,256]{1,0:T(8,128)S(1)}, f32[128,256]{1,0:T(8,128)S(1)}, u32[]{:S(2)}, u32[]{:S(2)}) collective-permute-start(f32[128,256]{1,0:T(8,128)S(1)} %get-tuple-element.85), channel_id=1, source_target_pairs={{0,4},{1,25},{2,6},{3,27},{4,0},{5,29},{6,2},{7,31},{8,12},{9,17},... | collective-permute-start | bytes 393224 | tf_op jit(solution)/shard_map/ppermute | solution.py:232
  25.8 6.6 %collective-permute-start.14 = (f32[128,256]{1,0:T(8,128)S(1)}, f32[128,256]{1,0:T(8,128)S(1)}, u32[]{:S(2)}, u32[]{:S(2)}) collective-permute-start(f32[128,256]{1,0:T(8,128)S(1)} %get-tuple-element.90), channel_id=1, source_target_pairs={{0,2},{1,5},{2,0},{3,7},{4,6},{5,1},{6,4},{7,3},{8,10},{9,13},{10,... | collective-permute-start | bytes 393224 | tf_op jit(solution)/shard_map/ppermute | solution.py:232
  30.0 5.3 %collective-permute-start.12 = (f32[128,256]{1,0:T(8,128)S(1)}, f32[128,256]{1,0:T(8,128)S(1)}, u32[]{:S(2)}, u32[]{:S(2)}) collective-permute-start(f32[128,256]{1,0:T(8,128)S(1)} %add_select_fusion.4), channel_id=1, source_target_pairs={{0,8},{1,5},{2,10},{3,7},{4,12},{5,1},{6,14},{7,3},{8,0},{9,13},{1... | collective-permute-start | bytes 393224 | tf_op jit(solution)/shard_map/ppermute | solution.py:232
  32.4 6.1 %collective-permute-start.17 = (f32[128,256]{1,0:T(8,128)S(1)}, f32[128,256]{1,0:T(8,128)S(1)}, u32[]{:S(2)}, u32[]{:S(2)}) collective-permute-start(f32[128,256]{1,0:T(8,128)S(1)} %collective-permute-done.14), channel_id=1, source_target_pairs={{0,2},{1,3},{2,0},{3,1},{4,6},{5,7},{6,4},{7,5},{8,10},{9,11},{10,... | collective-permute-start | bytes 393224 | tf_op jit(solution)/shard_map/ppermute | solution.py:232
  34.2 4.5 %collective-permute-start.15 = (f32[128,256]{1,0:T(8,128)S(1)}, f32[128,256]{1,0:T(8,128)S(1)}, u32[]{:S(2)}, u32[]{:S(2)}) collective-permute-start(f32[128,256]{1,0:T(8,128)S(1)} %add.53.high_ref), channel_id=1, source_target_pairs={{0,1},{1,0},{2,3},{3,2},{4,5},{5,4},{6,7},{7,6},{8,9},{9,8},{10,11... | collective-permute-start | bytes 393224 | tf_op jit(solution)/shard_map/ppermute | solution.py:232
  35.3 5.0 %collective-permute-start.13 = (f32[128,256]{1,0:T(8,128)S(1)}, f32[128,256]{1,0:T(8,128)S(1)}, u32[]{:S(2)}, u32[]{:S(2)}) collective-permute-start(f32[128,256]{1,0:T(8,128)S(1)} %add_select_fusion.1), channel_id=1, source_target_pairs={{0,4},{1,3},{2,6},{3,1},{4,0},{5,7},{6,2},{7,5},{8,12},{9,11},{10,... | collective-permute-start | bytes 393224 | tf_op jit(solution)/shard_map/ppermute | solution.py:232
  38.5 3.1 %collective-permute-start.18 = (f32[128,256]{1,0:T(8,128)S(1)}, f32[128,256]{1,0:T(8,128)S(1)}, u32[]{:S(2)}, u32[]{:S(2)}) collective-permute-start(f32[128,256]{1,0:T(8,128)S(1)} %add_select_fusion.low_ref), channel_id=1, source_target_pairs={{0,1},{1,0},{2,3},{3,2},{4,5},{5,4},{6,7},{7,6},{8,9},{9,8},{10,11... | collective-permute-start | bytes 393224 | tf_op jit(solution)/shard_map/ppermute | solution.py:232
  40.4 2.2 %collective-permute-start.16 = (f32[128,256]{1,0:T(8,128)S(1)}, f32[128,256]{1,0:T(8,128)S(1)}, u32[]{:S(2)}, u32[]{:S(2)}) collective-permute-start(f32[128,256]{1,0:T(8,128)S(1)} %add.59.high_ref), channel_id=1, source_target_pairs={{0,1},{1,0},{2,3},{3,2},{4,5},{5,4},{6,7},{7,6},{8,9},{9,8},{10,11... | collective-permute-start | bytes 393224 | tf_op jit(solution)/shard_map/ppermute | solution.py:232

commit v6 on v5

--- a/solution.py
+++ b/solution.py
@@ -102,15 +102,10 @@
     return (column * values).astype(BF16)
 
 
-def base_kernel(leaves_ref, vec_ref, weights_ref, turned_ref, part_ref, base_ref):
-    total = None
+def near_kernel(leaves_ref, vec_ref, part_ref):
     for leaf in range(vec_ref.shape[0] // LEAF):
         rows = slice(leaf * LEAF, (leaf + 1) * LEAF)
-        near = jnp.dot(leaves_ref[rows, :], vec_ref[rows, :], preferred_element_type=F32)
-        part_ref[rows, :] = near
-        term = jnp.dot(turned_ref[:, rows], weighted(weights_ref, near, rows), preferred_element_type=F32)
-        total = term if total is None else total + term
-    base_ref[...] = total
+        part_ref[rows, :] = jnp.dot(leaves_ref[rows, :], vec_ref[rows, :], preferred_element_type=F32)
 
 
 def gram_kernel(bases_ref, weights_ref, turned_ref, keep_ref, send_ref):
@@ -143,15 +138,21 @@
     return coefficients(oriented_ref, other_level(slot), factor, sums)
 
 
-def low_kernel(factors, oriented_ref, low_ref, keep_ref, got_ref, base_ref, sums_ref, gram_ref):
+def low_kernel(
+    factors, oriented_ref, low_ref, keep_ref, got_ref, part_ref, weights_ref, turned_ref, sums_ref, gram_ref
+):
     gram = keep_ref[...] + got_ref[...]
     rough = gram.astype(BF16)
     rest = (gram - rough.astype(F32)).astype(BF16)
     rank = low_ref.shape[0]
     both = jnp.concatenate([rough[:, rank:], rest[:, rank:]], axis=1)
     coeffs = own_coefficients(oriented_ref, 1, low_ref[...], factors)
-    delta = jnp.dot(both, jnp.concatenate([coeffs] * 2, axis=0), preferred_element_type=F32)
-    sums_ref[...] = base_ref[...] + delta
+    total = jnp.dot(both, jnp.concatenate([coeffs] * 2, axis=0), preferred_element_type=F32)
+    for leaf in range(part_ref.shape[0] // LEAF):
+        rows = slice(leaf * LEAF, (leaf + 1) * LEAF)
+        near = weighted(weights_ref, part_ref[rows, :], rows)
+        total = total + jnp.dot(turned_ref[:, rows], near, preferred_element_type=F32)
+    sums_ref[...] = total
     gram_ref[:, :rank] = rough[:, :rank]
     gram_ref[:, rank:] = rest[:, :rank]
 
@@ -253,7 +254,7 @@
         passenger = swap(passenger, 1, 1)
         got, *ridden = beside((got,), *rider_two(*ridden))
         high = jnp.where(odd, high + got, got)
-        low = jnp.where(odd, low + swap(low, far4, far4), low)
+        low = jnp.where(odd, low + swap(low, far4, far2), low)
         got = swap(high, far4, far3)
         got, *ridden = beside((got,), *rider_three(low, passenger, *ridden))
         return high + got, low, *ridden
@@ -282,23 +283,18 @@
         return oriented, turned, keep, send
 
     def second_riders(oriented, turned, keep):
-        part, base = call(
-            base_kernel,
-            [part_shape, jax.ShapeDtypeStruct((levels * rank, width), F32)],
-            [leaves, signal, weight_rows, turned],
-            (LEAF // rank + levels) * mults,
-        )
-        return oriented, keep, part, base
-
-    def third_riders(low, got, oriented, keep, part, base):
+        (part,) = call(near_kernel, [part_shape], [leaves, signal], LEAF // rank * mults)
+        return oriented, turned, keep, part
+
+    def third_riders(low, got, oriented, turned, keep, part):
         sums, gram = call(
             functools.partial(low_kernel, factors),
             [
                 jax.ShapeDtypeStruct((levels * rank, width), F32),
                 jax.ShapeDtypeStruct((levels * rank, 2 * rank), BF16),
             ],
-            [oriented, low, keep, got, base],
-            mults,
+            [oriented, low, keep, got, part, weight_rows, turned],
+            (1 + levels) * mults,
         )
         return oriented, part, sums, gram
 

time: 43.9 us -> 43.3 us (0.986)
  waiting for transfers between devices: 13.8 us -> 12.4 us
  starting transfers between devices: 20.8 us -> 21.9 us
  Pallas kernels: 8.46 us -> 7.91 us
    ppermute x19, waiting for transfers between devices: 13.8 us -> 12.4 us  [swap(): return lax.ppermute(value, AXIS, pairs)]
    ppermute x19, starting transfers between devices: 20.8 us -> 21.9 us  [swap(): return lax.ppermute(value, AXIS, pairs)]
    pallas_call x10, Pallas kernels: 8.46 us -> 7.91 us  [call(): pl.pallas_call(kernel, out_shape=outs, in_specs=[arrays_in] * len(arrays)...]
  transfers between devices with their start and end apart: 19 -> 19, of which waited for: 12 -> 13; matrix products, arithmetic and copies ran while one was open for 0% -> 0% of each run, Pallas kernels for 12% -> 11%
where the time goes in v6:
time: 43.3 us; the launch traced here: 43 us
  starting transfers between devices  21.9 us (51%)
  waiting for transfers between devices  12.4 us (29%)
  Pallas kernels  7.91 us (18%)
    ppermute x19, starting transfers between devices, swap(): return lax.ppermute(value, AXIS, pairs)  21.9 us
    ppermute x19, waiting for transfers between devices, swap(): return lax.ppermute(value, AXIS, pairs)  12.4 us
    pallas_call x10, Pallas kernels, call(): pl.pallas_call(kernel, out_shape=outs, in_specs=[arrays_in] * len(arrays)...  7.91 us
  transfers between devices with their start and end apart: 19, of which 13 were waited for; matrix products, arithmetic and copies ran while one was open for 0% of the time, Pallas kernels for 11%

profile of v6, /device:TPU:0, one launch (start us, length us, event | category | flops | bytes accessed | tf_op | source)
XLA Modules:
  0.0 43.0 jit_solution(12134252812013069246)
XLA Ops:
  0.0 1.6 %shard_map.55 = (f32[2,128,256]{2,1,0:T(8,128)S(1)}, bf16[4,1024,128]{2,1,0:T(8,128)(2,1)S(1)}, bf16[1024,256]{1,0:T(8,128)(2,1)S(1)}) custom-call(bf16[4,1024,128]{2,1,0:T(8,128)(2,1)} %bases_in.1, bf16[1024,256]{1,0:T(8,128)(2,1)} %vec_in.1), custom_call_target="tpu_custom_call" | custom-call | flops 134217728 | bytes 3407872 | tf_op jit(solution)/shard_map/pallas_call | solution.py:25
  2.5 0.8 %collective-permute-done = f32[2,128,256]{2,1,0:T(8,128)S(1)} collective-permute-done((f32[2,128,256]{2,1,0:T(8,128)S(1)}, f32[2,128,256]{2,1,0:T(8,128)S(1)}, u32[]{:S(2)}, u32[]{:S(2)}) %collective-permute-start) | collective-permute-done | bytes 262176 | tf_op jit(solution)/shard_map/ppermute | solution.py:233
  3.3 2.9 %collective-permute-start.1 = (f32[128,256]{1,0:T(8,128)S(1)}, f32[128,256]{1,0:T(8,128)S(1)}, u32[]{:S(2)}, u32[]{:S(2)}) collective-permute-start(f32[128,256]{1,0:T(8,128)S(1)} %get-tuple-element.96), channel_id=1, source_target_pairs={{0,2},{1,17},{2,0},{3,19},{4,6},{5,21},{6,4},{7,23},{8,10},{9,25},... | collective-permute-start | bytes 393224 | tf_op jit(solution)/shard_map/ppermute | solution.py:233
  6.2 1.5 %collective-permute-start.2 = (f32[128,256]{1,0:T(8,128)S(1)}, f32[128,256]{1,0:T(8,128)S(1)}, u32[]{:S(2)}, u32[]{:S(2)}) collective-permute-start(f32[128,256]{1,0:T(8,128)S(1)} %get-tuple-element.96), channel_id=1, source_target_pairs={{0,4},{1,25},{2,6},{3,27},{4,0},{5,29},{6,2},{7,31},{8,12},{9,17},... | collective-permute-start | bytes 393224 | tf_op jit(solution)/shard_map/ppermute | solution.py:233
  8.4 1.0 %shard_map.58 = (f32[512,256]{1,0:T(8,128)S(1)}, f32[512,256]{1,0:T(8,128)S(1)}) custom-call(bf16[4,1024,128]{2,1,0:T(8,128)(2,1)S(1)} %get-tuple-element.49.bases_ref, f32[8,128]{1,0:T(8,128)S(1)} %bitcast.17, bf16[512,1024]{1,0:T(8,128)(2,1)S(1)} %get-tuple-element.70.turned_ref), custom_call_target="tpu_custom_call" | custom-call | flops 536870912 | bytes 3149824 | tf_op jit(solution)/shard_map/pallas_call | solution.py:25
  10.0 1.2 %collective-permute-done.2 = f32[128,256]{1,0:T(8,128)S(1)} collective-permute-done((f32[128,256]{1,0:T(8,128)S(1)}, f32[128,256]{1,0:T(8,128)S(1)}, u32[]{:S(2)}, u32[]{:S(2)}) %collective-permute-start.2) | collective-permute-done | bytes 131104 | tf_op jit(solution)/shard_map/ppermute | solution.py:233
  11.2 1.6 %collective-permute-start.3 = (f32[128,256]{1,0:T(8,128)S(1)}, f32[128,256]{1,0:T(8,128)S(1)}, u32[]{:S(2)}, u32[]{:S(2)}) collective-permute-start(f32[128,256]{1,0:T(8,128)S(1)} %add_select_fusion.5), channel_id=1, source_target_pairs={{0,8},{1,5},{2,10},{3,7},{4,12},{5,1},{6,14},{7,3},{8,0},{9,13},{1... | collective-permute-start | bytes 393224 | tf_op jit(solution)/shard_map/ppermute | solution.py:233
  13.3 1.1 %collective-permute-done.5 = f32[128,256]{1,0:T(8,128)S(1)} collective-permute-done((f32[128,256]{1,0:T(8,128)S(1)}, f32[128,256]{1,0:T(8,128)S(1)}, u32[]{:S(2)}, u32[]{:S(2)}) %collective-permute-start.5) | collective-permute-done | bytes 131104 | tf_op jit(solution)/shard_map/ppermute | solution.py:233
  14.4 1.6 %collective-permute-start.6 = (f32[128,256]{1,0:T(8,128)S(1)}, f32[128,256]{1,0:T(8,128)S(1)}, u32[]{:S(2)}, u32[]{:S(2)}) collective-permute-start(f32[128,256]{1,0:T(8,128)S(1)} %collective-permute-done.5), channel_id=1, source_target_pairs={{0,8},{1,3},{2,10},{3,1},{4,12},{5,7},{6,14},{7,5},{8,0},{9,11},{1... | collective-permute-start | bytes 393224 | tf_op jit(solution)/shard_map/ppermute | solution.py:233
  16.3 1.6 %collective-permute-start.4 = (f32[128,256]{1,0:T(8,128)S(1)}, f32[128,256]{1,0:T(8,128)S(1)}, u32[]{:S(2)}, u32[]{:S(2)}) collective-permute-start(f32[128,256]{1,0:T(8,128)S(1)} %add_select_fusion.3), channel_id=1, source_target_pairs={{0,4},{1,3},{2,6},{3,1},{4,0},{5,7},{6,2},{7,5},{8,12},{9,11},{10,... | collective-permute-start | bytes 393224 | tf_op jit(solution)/shard_map/ppermute | solution.py:233
  17.9 1.5 %collective-permute-done.6 = f32[128,256]{1,0:T(8,128)S(1)} collective-permute-done((f32[128,256]{1,0:T(8,128)S(1)}, f32[128,256]{1,0:T(8,128)S(1)}, u32[]{:S(2)}, u32[]{:S(2)}) %collective-permute-start.6) | collective-permute-done | bytes 131104 | tf_op jit(solution)/shard_map/ppermute | solution.py:233
  19.5 0.8 %shard_map.60 = (f32[512,256]{1,0:T(8,128)S(1)}, bf16[512,256]{1,0:T(8,128)(2,1)S(1)}) custom-call(bf16[4,128,128]{2,1,0:T(8,128)(2,1)S(1)} %get-tuple-element.73.oriented_ref, f32[128,256]{1,0:T(8,128)S(1)} %add_select_fusion.2.low_ref, f32[512,256]{1,0:T(8,128)S(1)} %get-tuple-element.68.keep_ref, f32[512,256]{1,0:T(8,128)S(1)} %collective-permute-done.7.got_ref, ...), custom_call_target="tpu_custom_call" | custom-call | flops 335544320 | bytes 4198400 | tf_op jit(solution)/shard_map/pallas_call | solution.py:25
  20.3 1.0 %collective-permute-done.4 = f32[128,256]{1,0:T(8,128)S(1)} collective-permute-done((f32[128,256]{1,0:T(8,128)S(1)}, f32[128,256]{1,0:T(8,128)S(1)}, u32[]{:S(2)}, u32[]{:S(2)}) %collective-permute-start.4) | collective-permute-done | bytes 131104 | tf_op jit(solution)/shard_map/ppermute | solution.py:233
  21.8 1.5 %collective-permute-done.9 = f32[2,128,256]{2,1,0:T(8,128)S(1)} collective-permute-done((f32[2,128,256]{2,1,0:T(8,128)S(1)}, f32[2,128,256]{2,1,0:T(8,128)S(1)}, u32[]{:S(2)}, u32[]{:S(2)}) %collective-permute-start.9) | collective-permute-done | bytes 262176 | tf_op jit(solution)/shard_map/ppermute | solution.py:233
  24.0 1.8 %collective-permute-start.11 = (f32[128,256]{1,0:T(8,128)S(1)}, f32[128,256]{1,0:T(8,128)S(1)}, u32[]{:S(2)}, u32[]{:S(2)}) collective-permute-start(f32[128,256]{1,0:T(8,128)S(1)} %get-tuple-element.81), channel_id=1, source_target_pairs={{0,4},{1,25},{2,6},{3,27},{4,0},{5,29},{6,2},{7,31},{8,12},{9,17},... | collective-permute-start | bytes 393224 | tf_op jit(solution)/shard_map/ppermute | solution.py:233
  25.8 1.2 %collective-permute-start.14 = (f32[128,256]{1,0:T(8,128)S(1)}, f32[128,256]{1,0:T(8,128)S(1)}, u32[]{:S(2)}, u32[]{:S(2)}) collective-permute-start(f32[128,256]{1,0:T(8,128)S(1)} %get-tuple-element.86), channel_id=1, source_target_pairs={{0,2},{1,5},{2,0},{3,7},{4,6},{5,1},{6,4},{7,3},{8,10},{9,13},{10,... | collective-permute-start | bytes 393224 | tf_op jit(solution)/shard_map/ppermute | solution.py:233
  27.0 1.4 %collective-permute-done.10 = f32[128,256]{1,0:T(8,128)S(1)} collective-permute-done((f32[128,256]{1,0:T(8,128)S(1)}, f32[128,256]{1,0:T(8,128)S(1)}, u32[]{:S(2)}, u32[]{:S(2)}) %collective-permute-start.10) | collective-permute-done | bytes 131104 | tf_op jit(solution)/shard_map/ppermute | solution.py:233
  29.0 3.3 %collective-permute-start.12 = (f32[128,256]{1,0:T(8,128)S(1)}, f32[128,256]{1,0:T(8,128)S(1)}, u32[]{:S(2)}, u32[]{:S(2)}) collective-permute-start(f32[128,256]{1,0:T(8,128)S(1)} %add_select_fusion.4), channel_id=1, source_target_pairs={{0,8},{1,5},{2,10},{3,7},{4,12},{5,1},{6,14},{7,3},{8,0},{9,13},{1... | collective-permute-start | bytes 393224 | tf_op jit(solution)/shard_map/ppermute | solution.py:233
  32.3 1.1 %collective-permute-start.15 = (f32[128,256]{1,0:T(8,128)S(1)}, f32[128,256]{1,0:T(8,128)S(1)}, u32[]{:S(2)}, u32[]{:S(2)}) collective-permute-start(f32[128,256]{1,0:T(8,128)S(1)} %add.53.high_ref), channel_id=1, source_target_pairs={{0,1},{1,0},{2,3},{3,2},{4,5},{5,4},{6,7},{7,6},{8,9},{9,8},{10,11... | collective-permute-start | bytes 393224 | tf_op jit(solution)/shard_map/ppermute | solution.py:233
  33.4 1.5 %collective-permute-start.17 = (f32[128,256]{1,0:T(8,128)S(1)}, f32[128,256]{1,0:T(8,128)S(1)}, u32[]{:S(2)}, u32[]{:S(2)}) collective-permute-start(f32[128,256]{1,0:T(8,128)S(1)} %collective-permute-done.14), channel_id=1, source_target_pairs={{0,8},{1,3},{2,10},{3,1},{4,12},{5,7},{6,14},{7,5},{8,0},{9,11},{1... | collective-permute-start | bytes 393224 | tf_op jit(solution)/shard_map/ppermute | solution.py:233
  35.3 1.6 %collective-permute-start.13 = (f32[128,256]{1,0:T(8,128)S(1)}, f32[128,256]{1,0:T(8,128)S(1)}, u32[]{:S(2)}, u32[]{:S(2)}) collective-permute-start(f32[128,256]{1,0:T(8,128)S(1)} %add_select_fusion.1), channel_id=1, source_target_pairs={{0,4},{1,3},{2,6},{3,1},{4,0},{5,7},{6,2},{7,5},{8,12},{9,11},{10,... | collective-permute-start | bytes 393224 | tf_op jit(solution)/shard_map/ppermute | solution.py:233
  36.9 1.5 %collective-permute-done.17 = f32[128,256]{1,0:T(8,128)S(1)} collective-permute-done((f32[128,256]{1,0:T(8,128)S(1)}, f32[128,256]{1,0:T(8,128)S(1)}, u32[]{:S(2)}, u32[]{:S(2)}) %collective-permute-start.17) | collective-permute-done | bytes 131104 | tf_op jit(solution)/shard_map/ppermute | solution.py:233
  38.5 1.2 %shard_map.62.part_ref = f32[1024,256]{1,0:T(8,128)S(1)} custom-call(bf16[4,128,128]{2,1,0:T(8,128)(2,1)S(1)} %get-tuple-element.73.oriented_ref, f32[128,256]{1,0:T(8,128)S(1)} %add.53.high_ref, f32[128,256]{1,0:T(8,128)S(1)} %add_select_fusion.2.low_ref, f32[128,256]{1,0:T(8,128)S(1)} %collective-permute-done.15.high_other_ref, ...), custom_call_target="tpu_custom_call" | custom-call | flops 536870912 | bytes 4853760 | tf_op jit(solution)/shard_map/pallas_call | solution.py:25
  41.8 1.2 %shard_map.64 = bf16[1024,256]{1,0:T(8,128)(2,1)} custom-call(bf16[4,128,128]{2,1,0:T(8,128)(2,1)S(1)} %get-tuple-element.73.oriented_ref, f32[128,256]{1,0:T(8,128)S(1)} %collective-permute-done.16.other_ref, bf16[4,1024,128]{2,1,0:T(8,128)(2,1)S(1)} %get-tuple-element.49.bases_ref, f32[1024,256]{1,0:T(8,128)S(1)} %shard_map.63.part_ref), custom_call_target="tpu_custom_call" | custom-call | flops 67108864 | bytes 2883584 | tf_op jit(solution)/shard_map/pallas_call | solution.py:25
  (40 shorter events, 7.1 us)
Async XLA Ops:
  1.6 1.7 %collective-permute-start = (f32[2,128,256]{2,1,0:T(8,128)S(1)}, f32[2,128,256]{2,1,0:T(8,128)S(1)}, u32[]{:S(2)}, u32[]{:S(2)}) collective-permute-start(f32[2,128,256]{2,1,0:T(8,128)S(1)} %get-tuple-element.52), channel_id=1, source_target_pairs={{0,1},{1,0},{2,3},{3,2},{4,5},{5,4},{6,7},{7,6},{8,9},{9,8},{10,11... | collective-permute-start | bytes 786440 | tf_op jit(solution)/shard_map/ppermute | solution.py:233
  2.5 5.3 %copy-start.1 = (bf16[15,128,128]{2,1,0:T(8,128)(2,1)S(1)}, bf16[15,128,128]{2,1,0:T(8,128)(2,1)}, u32[]{:S(2)}) copy-start(bf16[15,128,128]{2,1,0:T(8,128)(2,1)} %couplings_ref.1) | copy-start | bytes 1474564
  3.3 6.7 %collective-permute-start.1 = (f32[128,256]{1,0:T(8,128)S(1)}, f32[128,256]{1,0:T(8,128)S(1)}, u32[]{:S(2)}, u32[]{:S(2)}) collective-permute-start(f32[128,256]{1,0:T(8,128)S(1)} %get-tuple-element.96), channel_id=1, source_target_pairs={{0,2},{1,17},{2,0},{3,19},{4,6},{5,21},{6,4},{7,23},{8,10},{9,25},... | collective-permute-start | bytes 393224 | tf_op jit(solution)/shard_map/ppermute | solution.py:233
  6.2 5.0 %collective-permute-start.2 = (f32[128,256]{1,0:T(8,128)S(1)}, f32[128,256]{1,0:T(8,128)S(1)}, u32[]{:S(2)}, u32[]{:S(2)}) collective-permute-start(f32[128,256]{1,0:T(8,128)S(1)} %get-tuple-element.96), channel_id=1, source_target_pairs={{0,4},{1,25},{2,6},{3,27},{4,0},{5,29},{6,2},{7,31},{8,12},{9,17},... | collective-permute-start | bytes 393224 | tf_op jit(solution)/shard_map/ppermute | solution.py:233
  7.8 0.7 %copy-start.2 = (f32[1024]{0:T(1024)S(1)}, f32[1024]{0:T(1024)}, u32[]{:S(2)}) copy-start(f32[1024]{0:T(1024)} %param.9) | copy-start | bytes 12292
  8.4 4.4 %copy-start = (bf16[1024,512]{1,0:T(8,128)(2,1)S(1)}, bf16[1024,512]{1,0:T(8,128)(2,1)}, u32[]{:S(2)}) copy-start(bf16[1024,512]{1,0:T(8,128)(2,1)} %leaves_ref.3) | copy-start | bytes 3145732
  9.4 5.0 %collective-permute-start.5 = (f32[128,256]{1,0:T(8,128)S(1)}, f32[128,256]{1,0:T(8,128)S(1)}, u32[]{:S(2)}, u32[]{:S(2)}) collective-permute-start(f32[128,256]{1,0:T(8,128)S(1)} %get-tuple-element.95), channel_id=1, source_target_pairs={{0,2},{1,5},{2,0},{3,7},{4,6},{5,1},{6,4},{7,3},{8,10},{9,13},{10,... | collective-permute-start | bytes 393224 | tf_op jit(solution)/shard_map/ppermute | solution.py:233
  11.2 5.0 %collective-permute-start.3 = (f32[128,256]{1,0:T(8,128)S(1)}, f32[128,256]{1,0:T(8,128)S(1)}, u32[]{:S(2)}, u32[]{:S(2)}) collective-permute-start(f32[128,256]{1,0:T(8,128)S(1)} %add_select_fusion.5), channel_id=1, source_target_pairs={{0,8},{1,5},{2,10},{3,7},{4,12},{5,1},{6,14},{7,3},{8,0},{9,13},{1... | collective-permute-start | bytes 393224 | tf_op jit(solution)/shard_map/ppermute | solution.py:233
  14.4 5.0 %collective-permute-start.6 = (f32[128,256]{1,0:T(8,128)S(1)}, f32[128,256]{1,0:T(8,128)S(1)}, u32[]{:S(2)}, u32[]{:S(2)}) collective-permute-start(f32[128,256]{1,0:T(8,128)S(1)} %collective-permute-done.5), channel_id=1, source_target_pairs={{0,8},{1,3},{2,10},{3,1},{4,12},{5,7},{6,14},{7,5},{8,0},{9,11},{1... | collective-permute-start | bytes 393224 | tf_op jit(solution)/shard_map/ppermute | solution.py:233
  16.0 3.5 %collective-permute-start.7 = (f32[512,256]{1,0:T(8,128)S(1)}, f32[512,256]{1,0:T(8,128)S(1)}, u32[]{:S(2)}, u32[]{:S(2)}) collective-permute-start(f32[512,256]{1,0:T(8,128)S(1)} %get-tuple-element.69), channel_id=1, source_target_pairs={{0,1},{1,0},{2,3},{3,2},{4,5},{5,4},{6,7},{7,6},{8,9},{9,8},{10,11... | collective-permute-start | bytes 1572872 | tf_op jit(solution)/shard_map/ppermute | solution.py:233
  16.3 5.0 %collective-permute-start.4 = (f32[128,256]{1,0:T(8,128)S(1)}, f32[128,256]{1,0:T(8,128)S(1)}, u32[]{:S(2)}, u32[]{:S(2)}) collective-permute-start(f32[128,256]{1,0:T(8,128)S(1)} %add_select_fusion.3), channel_id=1, source_target_pairs={{0,4},{1,3},{2,6},{3,1},{4,0},{5,7},{6,2},{7,5},{8,12},{9,11},{10,... | collective-permute-start | bytes 393224 | tf_op jit(solution)/shard_map/ppermute | solution.py:233
  19.4 1.9 %collective-permute-start.8 = (f32[128,256]{1,0:T(8,128)S(1)}, f32[128,256]{1,0:T(8,128)S(1)}, u32[]{:S(2)}, u32[]{:S(2)}) collective-permute-start(f32[128,256]{1,0:T(8,128)S(1)} %add_select_fusion.2.low_ref), channel_id=1, source_target_pairs={{0,1},{1,0},{2,3},{3,2},{4,5},{5,4},{6,7},{7,6},{8,9},{9,8},{10,11... | collective-permute-start | bytes 393224 | tf_op jit(solution)/shard_map/ppermute | solution.py:233
  21.8 1.6 %collective-permute-start.9 = (f32[2,128,256]{2,1,0:T(8,128)S(1)}, f32[2,128,256]{2,1,0:T(8,128)S(1)}, u32[]{:S(2)}, u32[]{:S(2)}) collective-permute-start(f32[2,128,256]{2,1,0:T(8,128)S(1)} %get-tuple-element.79), channel_id=1, source_target_pairs={{0,1},{1,0},{2,3},{3,2},{4,5},{5,4},{6,7},{7,6},{8,9},{9,8},{10,11... | collective-permute-start | bytes 786440 | tf_op jit(solution)/shard_map/ppermute | solution.py:233
  23.4 5.0 %collective-permute-start.10 = (f32[128,256]{1,0:T(8,128)S(1)}, f32[128,256]{1,0:T(8,128)S(1)}, u32[]{:S(2)}, u32[]{:S(2)}) collective-permute-start(f32[128,256]{1,0:T(8,128)S(1)} %get-tuple-element.81), channel_id=1, source_target_pairs={{0,2},{1,17},{2,0},{3,19},{4,6},{5,21},{6,4},{7,23},{8,10},{9,25},... | collective-permute-start | bytes 393224 | tf_op jit(solution)/shard_map/ppermute | solution.py:233
  24.0 5.0 %collective-permute-start.11 = (f32[128,256]{1,0:T(8,128)S(1)}, f32[128,256]{1,0:T(8,128)S(1)}, u32[]{:S(2)}, u32[]{:S(2)}) collective-permute-start(f32[128,256]{1,0:T(8,128)S(1)} %get-tuple-element.81), channel_id=1, source_target_pairs={{0,4},{1,25},{2,6},{3,27},{4,0},{5,29},{6,2},{7,31},{8,12},{9,17},... | collective-permute-start | bytes 393224 | tf_op jit(solution)/shard_map/ppermute | solution.py:233
  25.8 6.5 %collective-permute-start.14 = (f32[128,256]{1,0:T(8,128)S(1)}, f32[128,256]{1,0:T(8,128)S(1)}, u32[]{:S(2)}, u32[]{:S(2)}) collective-permute-start(f32[128,256]{1,0:T(8,128)S(1)} %get-tuple-element.86), channel_id=1, source_target_pairs={{0,2},{1,5},{2,0},{3,7},{4,6},{5,1},{6,4},{7,3},{8,10},{9,13},{10,... | collective-permute-start | bytes 393224 | tf_op jit(solution)/shard_map/ppermute | solution.py:233
  29.0 6.3 %collective-permute-start.12 = (f32[128,256]{1,0:T(8,128)S(1)}, f32[128,256]{1,0:T(8,128)S(1)}, u32[]{:S(2)}, u32[]{:S(2)}) collective-permute-start(f32[128,256]{1,0:T(8,128)S(1)} %add_select_fusion.4), channel_id=1, source_target_pairs={{0,8},{1,5},{2,10},{3,7},{4,12},{5,1},{6,14},{7,3},{8,0},{9,13},{1... | collective-permute-start | bytes 393224 | tf_op jit(solution)/shard_map/ppermute | solution.py:233
  32.3 6.2 %collective-permute-start.15 = (f32[128,256]{1,0:T(8,128)S(1)}, f32[128,256]{1,0:T(8,128)S(1)}, u32[]{:S(2)}, u32[]{:S(2)}) collective-permute-start(f32[128,256]{1,0:T(8,128)S(1)} %add.53.high_ref), channel_id=1, source_target_pairs={{0,1},{1,0},{2,3},{3,2},{4,5},{5,4},{6,7},{7,6},{8,9},{9,8},{10,11... | collective-permute-start | bytes 393224 | tf_op jit(solution)/shard_map/ppermute | solution.py:233
  33.4 5.0 %collective-permute-start.17 = (f32[128,256]{1,0:T(8,128)S(1)}, f32[128,256]{1,0:T(8,128)S(1)}, u32[]{:S(2)}, u32[]{:S(2)}) collective-permute-start(f32[128,256]{1,0:T(8,128)S(1)} %collective-permute-done.14), channel_id=1, source_target_pairs={{0,8},{1,3},{2,10},{3,1},{4,12},{5,7},{6,14},{7,5},{8,0},{9,11},{1... | collective-permute-start | bytes 393224 | tf_op jit(solution)/shard_map/ppermute | solution.py:233
  35.3 5.0 %collective-permute-start.13 = (f32[128,256]{1,0:T(8,128)S(1)}, f32[128,256]{1,0:T(8,128)S(1)}, u32[]{:S(2)}, u32[]{:S(2)}) collective-permute-start(f32[128,256]{1,0:T(8,128)S(1)} %add_select_fusion.1), channel_id=1, source_target_pairs={{0,4},{1,3},{2,6},{3,1},{4,0},{5,7},{6,2},{7,5},{8,12},{9,11},{10,... | collective-permute-start | bytes 393224 | tf_op jit(solution)/shard_map/ppermute | solution.py:233
  38.4 2.1 %collective-permute-start.18 = (f32[128,256]{1,0:T(8,128)S(1)}, f32[128,256]{1,0:T(8,128)S(1)}, u32[]{:S(2)}, u32[]{:S(2)}) collective-permute-start(f32[128,256]{1,0:T(8,128)S(1)} %add_select_fusion.low_ref), channel_id=1, source_target_pairs={{0,1},{1,0},{2,3},{3,2},{4,5},{5,4},{6,7},{7,6},{8,9},{9,8},{10,11... | collective-permute-start | bytes 393224 | tf_op jit(solution)/shard_map/ppermute | solution.py:233
  40.4 1.4 %collective-permute-start.16 = (f32[128,256]{1,0:T(8,128)S(1)}, f32[128,256]{1,0:T(8,128)S(1)}, u32[]{:S(2)}, u32[]{:S(2)}) collective-permute-start(f32[128,256]{1,0:T(8,128)S(1)} %add.59.high_ref), channel_id=1, source_target_pairs={{0,1},{1,0},{2,3},{3,2},{4,5},{5,4},{6,7},{7,6},{8,9},{9,8},{10,11... | collective-permute-start | bytes 393224 | tf_op jit(solution)/shard_map/ppermute | solution.py:233

commit v7 on v6

--- a/solution.py
+++ b/solution.py
@@ -246,7 +246,7 @@
 
     def rounds(high, low, rider_one, rider_two, rider_three, passenger=None):
         near = swap(high, far1, far4)
-        across = swap(high, far1 | far2, far3)
+        across = swap(high, far1 | far2, far4)
         near, across, *ridden = beside((near, across), *rider_one())
         high = jnp.where(odd, near + across, high + near)
         got = swap(high, far3, far2)

time: 43.3 us -> 42.8 us (0.988)
  waiting for transfers between devices: 12.4 us -> 11.8 us
    ppermute x19, waiting for transfers between devices: 12.4 us -> 11.8 us  [swap(): return lax.ppermute(value, AXIS, pairs)]
  transfers between devices with their start and end apart: 19 -> 19, of which waited for: 13 -> 11; matrix products, arithmetic and copies ran while one was open for 0% -> 0% of each run, Pallas kernels for 11% -> 11%
where the time goes in v7:
time: 42.8 us; the launch traced here: 42.6 us
  starting transfers between devices  22.3 us (52%)
  waiting for transfers between devices  11.8 us (28%)
  Pallas kernels  7.9 us (18%)
    ppermute x19, starting transfers between devices, swap(): return lax.ppermute(value, AXIS, pairs)  22.3 us
    ppermute x19, waiting for transfers between devices, swap(): return lax.ppermute(value, AXIS, pairs)  11.8 us
    pallas_call x10, Pallas kernels, call(): pl.pallas_call(kernel, out_shape=outs, in_specs=[arrays_in] * len(arrays)...  7.9 us
  transfers between devices with their start and end apart: 19, of which 11 were waited for; matrix products, arithmetic and copies ran while one was open for 0% of the time, Pallas kernels for 11%

profile of v7, /device:TPU:0, one launch (start us, length us, event | category | flops | bytes accessed | tf_op | source)
XLA Modules:
  0.0 42.6 jit_solution(1390338328135732438)
XLA Ops:
  0.0 1.6 %shard_map.55 = (f32[2,128,256]{2,1,0:T(8,128)S(1)}, bf16[4,1024,128]{2,1,0:T(8,128)(2,1)S(1)}, bf16[1024,256]{1,0:T(8,128)(2,1)S(1)}) custom-call(bf16[4,1024,128]{2,1,0:T(8,128)(2,1)} %bases_in.1, bf16[1024,256]{1,0:T(8,128)(2,1)} %vec_in.1), custom_call_target="tpu_custom_call" | custom-call | flops 134217728 | bytes 3407872 | tf_op jit(solution)/shard_map/pallas_call | solution.py:25
  2.5 0.8 %collective-permute-done = f32[2,128,256]{2,1,0:T(8,128)S(1)} collective-permute-done((f32[2,128,256]{2,1,0:T(8,128)S(1)}, f32[2,128,256]{2,1,0:T(8,128)S(1)}, u32[]{:S(2)}, u32[]{:S(2)}) %collective-permute-start) | collective-permute-done | bytes 262176 | tf_op jit(solution)/shard_map/ppermute | solution.py:233
  3.3 2.9 %collective-permute-start.1 = (f32[128,256]{1,0:T(8,128)S(1)}, f32[128,256]{1,0:T(8,128)S(1)}, u32[]{:S(2)}, u32[]{:S(2)}) collective-permute-start(f32[128,256]{1,0:T(8,128)S(1)} %get-tuple-element.96), channel_id=1, source_target_pairs={{0,2},{1,17},{2,0},{3,19},{4,6},{5,21},{6,4},{7,23},{8,10},{9,25},... | collective-permute-start | bytes 393224 | tf_op jit(solution)/shard_map/ppermute | solution.py:233
  7.0 1.0 %shard_map.58 = (f32[512,256]{1,0:T(8,128)S(1)}, f32[512,256]{1,0:T(8,128)S(1)}) custom-call(bf16[4,1024,128]{2,1,0:T(8,128)(2,1)S(1)} %get-tuple-element.49.bases_ref, f32[8,128]{1,0:T(8,128)S(1)} %bitcast.17, bf16[512,1024]{1,0:T(8,128)(2,1)S(1)} %get-tuple-element.70.turned_ref), custom_call_target="tpu_custom_call" | custom-call | flops 536870912 | bytes 3149824 | tf_op jit(solution)/shard_map/pallas_call | solution.py:25
  8.0 2.0 %collective-permute-start.5 = (f32[128,256]{1,0:T(8,128)S(1)}, f32[128,256]{1,0:T(8,128)S(1)}, u32[]{:S(2)}, u32[]{:S(2)}) collective-permute-start(f32[128,256]{1,0:T(8,128)S(1)} %get-tuple-element.95), channel_id=1, source_target_pairs={{0,2},{1,5},{2,0},{3,7},{4,6},{5,1},{6,4},{7,3},{8,10},{9,13},{10,... | collective-permute-start | bytes 393224 | tf_op jit(solution)/shard_map/ppermute | solution.py:233
  10.0 1.2 %collective-permute-done.2 = f32[128,256]{1,0:T(8,128)S(1)} collective-permute-done((f32[128,256]{1,0:T(8,128)S(1)}, f32[128,256]{1,0:T(8,128)S(1)}, u32[]{:S(2)}, u32[]{:S(2)}) %collective-permute-start.2) | collective-permute-done | bytes 131104 | tf_op jit(solution)/shard_map/ppermute | solution.py:233
  11.2 1.6 %collective-permute-start.3 = (f32[128,256]{1,0:T(8,128)S(1)}, f32[128,256]{1,0:T(8,128)S(1)}, u32[]{:S(2)}, u32[]{:S(2)}) collective-permute-start(f32[128,256]{1,0:T(8,128)S(1)} %add_select_fusion.5), channel_id=1, source_target_pairs={{0,8},{1,5},{2,10},{3,7},{4,12},{5,1},{6,14},{7,3},{8,0},{9,13},{1... | collective-permute-start | bytes 393224 | tf_op jit(solution)/shard_map/ppermute | solution.py:233
  13.3 1.7 %collective-permute-start.6 = (f32[128,256]{1,0:T(8,128)S(1)}, f32[128,256]{1,0:T(8,128)S(1)}, u32[]{:S(2)}, u32[]{:S(2)}) collective-permute-start(f32[128,256]{1,0:T(8,128)S(1)} %collective-permute-done.5), channel_id=1, source_target_pairs={{0,8},{1,3},{2,10},{3,1},{4,12},{5,7},{6,14},{7,5},{8,0},{9,11},{1... | collective-permute-start | bytes 393224 | tf_op jit(solution)/shard_map/ppermute | solution.py:233
  15.0 0.9 %collective-permute-start.7 = (f32[512,256]{1,0:T(8,128)S(1)}, f32[512,256]{1,0:T(8,128)S(1)}, u32[]{:S(2)}, u32[]{:S(2)}) collective-permute-start(f32[512,256]{1,0:T(8,128)S(1)} %get-tuple-element.69), channel_id=1, source_target_pairs={{0,1},{1,0},{2,3},{3,2},{4,5},{5,4},{6,7},{7,6},{8,9},{9,8},{10,11... | collective-permute-start | bytes 1572872 | tf_op jit(solution)/shard_map/ppermute | solution.py:233
  16.3 1.6 %collective-permute-start.4 = (f32[128,256]{1,0:T(8,128)S(1)}, f32[128,256]{1,0:T(8,128)S(1)}, u32[]{:S(2)}, u32[]{:S(2)}) collective-permute-start(f32[128,256]{1,0:T(8,128)S(1)} %add_select_fusion.3), channel_id=1, source_target_pairs={{0,4},{1,3},{2,6},{3,1},{4,0},{5,7},{6,2},{7,5},{8,12},{9,11},{10,... | collective-permute-start | bytes 393224 | tf_op jit(solution)/shard_map/ppermute | solution.py:233
  18.7 0.8 %shard_map.60 = (f32[512,256]{1,0:T(8,128)S(1)}, bf16[512,256]{1,0:T(8,128)(2,1)S(1)}) custom-call(bf16[4,128,128]{2,1,0:T(8,128)(2,1)S(1)} %get-tuple-element.73.oriented_ref, f32[128,256]{1,0:T(8,128)S(1)} %add_select_fusion.2.low_ref, f32[512,256]{1,0:T(8,128)S(1)} %get-tuple-element.68.keep_ref, f32[512,256]{1,0:T(8,128)S(1)} %collective-permute-done.7.got_ref, ...), custom_call_target="tpu_custom_call" | custom-call | flops 335544320 | bytes 4198400 | tf_op jit(solution)/shard_map/pallas_call | solution.py:25
  19.4 1.9 %collective-permute-done.4 = f32[128,256]{1,0:T(8,128)S(1)} collective-permute-done((f32[128,256]{1,0:T(8,128)S(1)}, f32[128,256]{1,0:T(8,128)S(1)}, u32[]{:S(2)}, u32[]{:S(2)}) %collective-permute-start.4) | collective-permute-done | bytes 131104 | tf_op jit(solution)/shard_map/ppermute | solution.py:233
  21.8 1.5 %collective-permute-done.9 = f32[2,128,256]{2,1,0:T(8,128)S(1)} collective-permute-done((f32[2,128,256]{2,1,0:T(8,128)S(1)}, f32[2,128,256]{2,1,0:T(8,128)S(1)}, u32[]{:S(2)}, u32[]{:S(2)}) %collective-permute-start.9) | collective-permute-done | bytes 262176 | tf_op jit(solution)/shard_map/ppermute | solution.py:233
  23.4 1.5 %collective-permute-start.10 = (f32[128,256]{1,0:T(8,128)S(1)}, f32[128,256]{1,0:T(8,128)S(1)}, u32[]{:S(2)}, u32[]{:S(2)}) collective-permute-start(f32[128,256]{1,0:T(8,128)S(1)} %get-tuple-element.81), channel_id=1, source_target_pairs={{0,2},{1,17},{2,0},{3,19},{4,6},{5,21},{6,4},{7,23},{8,10},{9,25},... | collective-permute-start | bytes 393224 | tf_op jit(solution)/shard_map/ppermute | solution.py:233
  25.5 1.4 %collective-permute-start.14 = (f32[128,256]{1,0:T(8,128)S(1)}, f32[128,256]{1,0:T(8,128)S(1)}, u32[]{:S(2)}, u32[]{:S(2)}) collective-permute-start(f32[128,256]{1,0:T(8,128)S(1)} %get-tuple-element.86), channel_id=1, source_target_pairs={{0,2},{1,5},{2,0},{3,7},{4,6},{5,1},{6,4},{7,3},{8,10},{9,13},{10,... | collective-permute-start | bytes 393224 | tf_op jit(solution)/shard_map/ppermute | solution.py:233
  26.9 1.5 %collective-permute-done.10 = f32[128,256]{1,0:T(8,128)S(1)} collective-permute-done((f32[128,256]{1,0:T(8,128)S(1)}, f32[128,256]{1,0:T(8,128)S(1)}, u32[]{:S(2)}, u32[]{:S(2)}) %collective-permute-start.10) | collective-permute-done | bytes 131104 | tf_op jit(solution)/shard_map/ppermute | solution.py:233
  28.4 1.4 %collective-permute-done.11 = f32[128,256]{1,0:T(8,128)S(1)} collective-permute-done((f32[128,256]{1,0:T(8,128)S(1)}, f32[128,256]{1,0:T(8,128)S(1)}, u32[]{:S(2)}, u32[]{:S(2)}) %collective-permute-start.11) | collective-permute-done | bytes 131104 | tf_op jit(solution)/shard_map/ppermute | solution.py:233
  29.9 1.6 %collective-permute-start.12 = (f32[128,256]{1,0:T(8,128)S(1)}, f32[128,256]{1,0:T(8,128)S(1)}, u32[]{:S(2)}, u32[]{:S(2)}) collective-permute-start(f32[128,256]{1,0:T(8,128)S(1)} %add_select_fusion.4), channel_id=1, source_target_pairs={{0,8},{1,5},{2,10},{3,7},{4,12},{5,1},{6,14},{7,3},{8,0},{9,13},{1... | collective-permute-start | bytes 393224 | tf_op jit(solution)/shard_map/ppermute | solution.py:233
  31.5 1.9 %collective-permute-start.15 = (f32[128,256]{1,0:T(8,128)S(1)}, f32[128,256]{1,0:T(8,128)S(1)}, u32[]{:S(2)}, u32[]{:S(2)}) collective-permute-start(f32[128,256]{1,0:T(8,128)S(1)} %add.53.high_ref), channel_id=1, source_target_pairs={{0,1},{1,0},{2,3},{3,2},{4,5},{5,4},{6,7},{7,6},{8,9},{9,8},{10,11... | collective-permute-start | bytes 393224 | tf_op jit(solution)/shard_map/ppermute | solution.py:233
  33.4 1.5 %collective-permute-start.17 = (f32[128,256]{1,0:T(8,128)S(1)}, f32[128,256]{1,0:T(8,128)S(1)}, u32[]{:S(2)}, u32[]{:S(2)}) collective-permute-start(f32[128,256]{1,0:T(8,128)S(1)} %collective-permute-done.14), channel_id=1, source_target_pairs={{0,8},{1,3},{2,10},{3,1},{4,12},{5,7},{6,14},{7,5},{8,0},{9,11},{1... | collective-permute-start | bytes 393224 | tf_op jit(solution)/shard_map/ppermute | solution.py:233
  35.0 1.5 %collective-permute-start.13 = (f32[128,256]{1,0:T(8,128)S(1)}, f32[128,256]{1,0:T(8,128)S(1)}, u32[]{:S(2)}, u32[]{:S(2)}) collective-permute-start(f32[128,256]{1,0:T(8,128)S(1)} %add_select_fusion.1), channel_id=1, source_target_pairs={{0,4},{1,3},{2,6},{3,1},{4,0},{5,7},{6,2},{7,5},{8,12},{9,11},{10,... | collective-permute-start | bytes 393224 | tf_op jit(solution)/shard_map/ppermute | solution.py:233
  36.5 1.9 %collective-permute-done.17 = f32[128,256]{1,0:T(8,128)S(1)} collective-permute-done((f32[128,256]{1,0:T(8,128)S(1)}, f32[128,256]{1,0:T(8,128)S(1)}, u32[]{:S(2)}, u32[]{:S(2)}) %collective-permute-start.17) | collective-permute-done | bytes 131104 | tf_op jit(solution)/shard_map/ppermute | solution.py:233
  38.5 1.2 %shard_map.62.part_ref = f32[1024,256]{1,0:T(8,128)S(1)} custom-call(bf16[4,128,128]{2,1,0:T(8,128)(2,1)S(1)} %get-tuple-element.73.oriented_ref, f32[128,256]{1,0:T(8,128)S(1)} %add.53.high_ref, f32[128,256]{1,0:T(8,128)S(1)} %add_select_fusion.2.low_ref, f32[128,256]{1,0:T(8,128)S(1)} %collective-permute-done.15.high_other_ref, ...), custom_call_target="tpu_custom_call" | custom-call | flops 536870912 | bytes 4853760 | tf_op jit(solution)/shard_map/pallas_call | solution.py:25
  41.4 1.2 %shard_map.64 = bf16[1024,256]{1,0:T(8,128)(2,1)} custom-call(bf16[4,128,128]{2,1,0:T(8,128)(2,1)S(1)} %get-tuple-element.73.oriented_ref, f32[128,256]{1,0:T(8,128)S(1)} %collective-permute-done.16.other_ref, bf16[4,1024,128]{2,1,0:T(8,128)(2,1)S(1)} %get-tuple-element.49.bases_ref, f32[1024,256]{1,0:T(8,128)S(1)} %shard_map.63.part_ref), custom_call_target="tpu_custom_call" | custom-call | flops 67108864 | bytes 2883584 | tf_op jit(solution)/shard_map/pallas_call | solution.py:25
  (40 shorter events, 6.2 us)
Async XLA Ops:
  1.6 1.7 %collective-permute-start = (f32[2,128,256]{2,1,0:T(8,128)S(1)}, f32[2,128,256]{2,1,0:T(8,128)S(1)}, u32[]{:S(2)}, u32[]{:S(2)}) collective-permute-start(f32[2,128,256]{2,1,0:T(8,128)S(1)} %get-tuple-element.52), channel_id=1, source_target_pairs={{0,1},{1,0},{2,3},{3,2},{4,5},{5,4},{6,7},{7,6},{8,9},{9,8},{10,11... | collective-permute-start | bytes 786440 | tf_op jit(solution)/shard_map/ppermute | solution.py:233
  2.5 3.8 %copy-start.1 = (bf16[15,128,128]{2,1,0:T(8,128)(2,1)S(1)}, bf16[15,128,128]{2,1,0:T(8,128)(2,1)}, u32[]{:S(2)}) copy-start(bf16[15,128,128]{2,1,0:T(8,128)(2,1)} %couplings_ref.1) | copy-start | bytes 1474564
  3.3 6.7 %collective-permute-start.1 = (f32[128,256]{1,0:T(8,128)S(1)}, f32[128,256]{1,0:T(8,128)S(1)}, u32[]{:S(2)}, u32[]{:S(2)}) collective-permute-start(f32[128,256]{1,0:T(8,128)S(1)} %get-tuple-element.96), channel_id=1, source_target_pairs={{0,2},{1,17},{2,0},{3,19},{4,6},{5,21},{6,4},{7,23},{8,10},{9,25},... | collective-permute-start | bytes 393224 | tf_op jit(solution)/shard_map/ppermute | solution.py:233
  6.2 5.0 %collective-permute-start.2 = (f32[128,256]{1,0:T(8,128)S(1)}, f32[128,256]{1,0:T(8,128)S(1)}, u32[]{:S(2)}, u32[]{:S(2)}) collective-permute-start(f32[128,256]{1,0:T(8,128)S(1)} %get-tuple-element.96), channel_id=1, source_target_pairs={{0,2},{1,25},{2,0},{3,27},{4,6},{5,29},{6,4},{7,31},{8,10},{9,17},... | collective-permute-start | bytes 393224 | tf_op jit(solution)/shard_map/ppermute | solution.py:233
  6.3 0.7 %copy-start.2 = (f32[1024]{0:T(1024)S(1)}, f32[1024]{0:T(1024)}, u32[]{:S(2)}) copy-start(f32[1024]{0:T(1024)} %param.9) | copy-start | bytes 12292
  7.0 5.9 %copy-start = (bf16[1024,512]{1,0:T(8,128)(2,1)S(1)}, bf16[1024,512]{1,0:T(8,128)(2,1)}, u32[]{:S(2)}) copy-start(bf16[1024,512]{1,0:T(8,128)(2,1)} %leaves_ref.3) | copy-start | bytes 3145732
  8.0 5.4 %collective-permute-start.5 = (f32[128,256]{1,0:T(8,128)S(1)}, f32[128,256]{1,0:T(8,128)S(1)}, u32[]{:S(2)}, u32[]{:S(2)}) collective-permute-start(f32[128,256]{1,0:T(8,128)S(1)} %get-tuple-element.95), channel_id=1, source_target_pairs={{0,2},{1,5},{2,0},{3,7},{4,6},{5,1},{6,4},{7,3},{8,10},{9,13},{10,... | collective-permute-start | bytes 393224 | tf_op jit(solution)/shard_map/ppermute | solution.py:233
  11.2 5.0 %collective-permute-start.3 = (f32[128,256]{1,0:T(8,128)S(1)}, f32[128,256]{1,0:T(8,128)S(1)}, u32[]{:S(2)}, u32[]{:S(2)}) collective-permute-start(f32[128,256]{1,0:T(8,128)S(1)} %add_select_fusion.5), channel_id=1, source_target_pairs={{0,8},{1,5},{2,10},{3,7},{4,12},{5,1},{6,14},{7,3},{8,0},{9,13},{1... | collective-permute-start | bytes 393224 | tf_op jit(solution)/shard_map/ppermute | solution.py:233
  13.3 5.0 %collective-permute-start.6 = (f32[128,256]{1,0:T(8,128)S(1)}, f32[128,256]{1,0:T(8,128)S(1)}, u32[]{:S(2)}, u32[]{:S(2)}) collective-permute-start(f32[128,256]{1,0:T(8,128)S(1)} %collective-permute-done.5), channel_id=1, source_target_pairs={{0,8},{1,3},{2,10},{3,1},{4,12},{5,7},{6,14},{7,5},{8,0},{9,11},{1... | collective-permute-start | bytes 393224 | tf_op jit(solution)/shard_map/ppermute | solution.py:233
  15.0 3.6 %collective-permute-start.7 = (f32[512,256]{1,0:T(8,128)S(1)}, f32[512,256]{1,0:T(8,128)S(1)}, u32[]{:S(2)}, u32[]{:S(2)}) collective-permute-start(f32[512,256]{1,0:T(8,128)S(1)} %get-tuple-element.69), channel_id=1, source_target_pairs={{0,1},{1,0},{2,3},{3,2},{4,5},{5,4},{6,7},{7,6},{8,9},{9,8},{10,11... | collective-permute-start | bytes 1572872 | tf_op jit(solution)/shard_map/ppermute | solution.py:233
  16.3 5.0 %collective-permute-start.4 = (f32[128,256]{1,0:T(8,128)S(1)}, f32[128,256]{1,0:T(8,128)S(1)}, u32[]{:S(2)}, u32[]{:S(2)}) collective-permute-start(f32[128,256]{1,0:T(8,128)S(1)} %add_select_fusion.3), channel_id=1, source_target_pairs={{0,4},{1,3},{2,6},{3,1},{4,0},{5,7},{6,2},{7,5},{8,12},{9,11},{10,... | collective-permute-start | bytes 393224 | tf_op jit(solution)/shard_map/ppermute | solution.py:233
  18.4 3.0 %collective-permute-start.8 = (f32[128,256]{1,0:T(8,128)S(1)}, f32[128,256]{1,0:T(8,128)S(1)}, u32[]{:S(2)}, u32[]{:S(2)}) collective-permute-start(f32[128,256]{1,0:T(8,128)S(1)} %add_select_fusion.2.low_ref), channel_id=1, source_target_pairs={{0,1},{1,0},{2,3},{3,2},{4,5},{5,4},{6,7},{7,6},{8,9},{9,8},{10,11... | collective-permute-start | bytes 393224 | tf_op jit(solution)/shard_map/ppermute | solution.py:233
  21.8 1.6 %collective-permute-start.9 = (f32[2,128,256]{2,1,0:T(8,128)S(1)}, f32[2,128,256]{2,1,0:T(8,128)S(1)}, u32[]{:S(2)}, u32[]{:S(2)}) collective-permute-start(f32[2,128,256]{2,1,0:T(8,128)S(1)} %get-tuple-element.79), channel_id=1, source_target_pairs={{0,1},{1,0},{2,3},{3,2},{4,5},{5,4},{6,7},{7,6},{8,9},{9,8},{10,11... | collective-permute-start | bytes 786440 | tf_op jit(solution)/shard_map/ppermute | solution.py:233
  23.4 5.0 %collective-permute-start.10 = (f32[128,256]{1,0:T(8,128)S(1)}, f32[128,256]{1,0:T(8,128)S(1)}, u32[]{:S(2)}, u32[]{:S(2)}) collective-permute-start(f32[128,256]{1,0:T(8,128)S(1)} %get-tuple-element.81), channel_id=1, source_target_pairs={{0,2},{1,17},{2,0},{3,19},{4,6},{5,21},{6,4},{7,23},{8,10},{9,25},... | collective-permute-start | bytes 393224 | tf_op jit(solution)/shard_map/ppermute | solution.py:233
  24.9 5.0 %collective-permute-start.11 = (f32[128,256]{1,0:T(8,128)S(1)}, f32[128,256]{1,0:T(8,128)S(1)}, u32[]{:S(2)}, u32[]{:S(2)}) collective-permute-start(f32[128,256]{1,0:T(8,128)S(1)} %get-tuple-element.81), channel_id=1, source_target_pairs={{0,2},{1,25},{2,0},{3,27},{4,6},{5,29},{6,4},{7,31},{8,10},{9,17},... | collective-permute-start | bytes 393224 | tf_op jit(solution)/shard_map/ppermute | solution.py:233
  25.5 6.0 %collective-permute-start.14 = (f32[128,256]{1,0:T(8,128)S(1)}, f32[128,256]{1,0:T(8,128)S(1)}, u32[]{:S(2)}, u32[]{:S(2)}) collective-permute-start(f32[128,256]{1,0:T(8,128)S(1)} %get-tuple-element.86), channel_id=1, source_target_pairs={{0,2},{1,5},{2,0},{3,7},{4,6},{5,1},{6,4},{7,3},{8,10},{9,13},{10,... | collective-permute-start | bytes 393224 | tf_op jit(solution)/shard_map/ppermute | solution.py:233
  29.9 5.1 %collective-permute-start.12 = (f32[128,256]{1,0:T(8,128)S(1)}, f32[128,256]{1,0:T(8,128)S(1)}, u32[]{:S(2)}, u32[]{:S(2)}) collective-permute-start(f32[128,256]{1,0:T(8,128)S(1)} %add_select_fusion.4), channel_id=1, source_target_pairs={{0,8},{1,5},{2,10},{3,7},{4,12},{5,1},{6,14},{7,3},{8,0},{9,13},{1... | collective-permute-start | bytes 393224 | tf_op jit(solution)/shard_map/ppermute | solution.py:233
  31.5 7.0 %collective-permute-start.15 = (f32[128,256]{1,0:T(8,128)S(1)}, f32[128,256]{1,0:T(8,128)S(1)}, u32[]{:S(2)}, u32[]{:S(2)}) collective-permute-start(f32[128,256]{1,0:T(8,128)S(1)} %add.53.high_ref), channel_id=1, source_target_pairs={{0,1},{1,0},{2,3},{3,2},{4,5},{5,4},{6,7},{7,6},{8,9},{9,8},{10,11... | collective-permute-start | bytes 393224 | tf_op jit(solution)/shard_map/ppermute | solution.py:233
  33.4 5.0 %collective-permute-start.17 = (f32[128,256]{1,0:T(8,128)S(1)}, f32[128,256]{1,0:T(8,128)S(1)}, u32[]{:S(2)}, u32[]{:S(2)}) collective-permute-start(f32[128,256]{1,0:T(8,128)S(1)} %collective-permute-done.14), channel_id=1, source_target_pairs={{0,8},{1,3},{2,10},{3,1},{4,12},{5,7},{6,14},{7,5},{8,0},{9,11},{1... | collective-permute-start | bytes 393224 | tf_op jit(solution)/shard_map/ppermute | solution.py:233
  35.0 5.0 %collective-permute-start.13 = (f32[128,256]{1,0:T(8,128)S(1)}, f32[128,256]{1,0:T(8,128)S(1)}, u32[]{:S(2)}, u32[]{:S(2)}) collective-permute-start(f32[128,256]{1,0:T(8,128)S(1)} %add_select_fusion.1), channel_id=1, source_target_pairs={{0,4},{1,3},{2,6},{3,1},{4,0},{5,7},{6,2},{7,5},{8,12},{9,11},{10,... | collective-permute-start | bytes 393224 | tf_op jit(solution)/shard_map/ppermute | solution.py:233
  38.4 1.9 %collective-permute-start.18 = (f32[128,256]{1,0:T(8,128)S(1)}, f32[128,256]{1,0:T(8,128)S(1)}, u32[]{:S(2)}, u32[]{:S(2)}) collective-permute-start(f32[128,256]{1,0:T(8,128)S(1)} %add_select_fusion.low_ref), channel_id=1, source_target_pairs={{0,1},{1,0},{2,3},{3,2},{4,5},{5,4},{6,7},{7,6},{8,9},{9,8},{10,11... | collective-permute-start | bytes 393224 | tf_op jit(solution)/shard_map/ppermute | solution.py:233
  40.0 1.4 %collective-permute-start.16 = (f32[128,256]{1,0:T(8,128)S(1)}, f32[128,256]{1,0:T(8,128)S(1)}, u32[]{:S(2)}, u32[]{:S(2)}) collective-permute-start(f32[128,256]{1,0:T(8,128)S(1)} %add.59.high_ref), channel_id=1, source_target_pairs={{0,1},{1,0},{2,3},{3,2},{4,5},{5,4},{6,7},{7,6},{8,9},{9,8},{10,11... | collective-permute-start | bytes 393224 | tf_op jit(solution)/shard_map/ppermute | solution.py:233

commit v8 on v7

--- a/solution.py
+++ b/solution.py
@@ -245,17 +245,17 @@
         return high, low
 
     def rounds(high, low, rider_one, rider_two, rider_three, passenger=None):
-        near = swap(high, far1, far4)
+        near = swap(high, far1, far3)
         across = swap(high, far1 | far2, far4)
         near, across, *ridden = beside((near, across), *rider_one())
         high = jnp.where(odd, near + across, high + near)
-        got = swap(high, far3, far2)
+        got = swap(high, far4, far2)
         low, passenger = beside((swap(low, far3, far4),), ridden.pop() if passenger is None else passenger)
         passenger = swap(passenger, 1, 1)
         got, *ridden = beside((got,), *rider_two(*ridden))
         high = jnp.where(odd, high + got, got)
-        low = jnp.where(odd, low + swap(low, far4, far2), low)
-        got = swap(high, far4, far3)
+        low = jnp.where(odd, low + swap(low, far4, far3), low)
+        got = swap(high, far3, far4)
         got, *ridden = beside((got,), *rider_three(low, passenger, *ridden))
         return high + got, low, *ridden
 

time: 42.8 us -> 42.8 us (level)
  starting transfers between devices: 22.3 us -> 19.4 us
  waiting for transfers between devices: 11.8 us -> 14.6 us
    ppermute x19, starting transfers between devices: 22.3 us -> 19.4 us  [swap(): return lax.ppermute(value, AXIS, pairs)]
    ppermute x19, waiting for transfers between devices: 11.8 us -> 14.6 us  [swap(): return lax.ppermute(value, AXIS, pairs)]
  transfers between devices with their start and end apart: 19 -> 19, of which waited for: 11 -> 12; matrix products, arithmetic and copies ran while one was open for 0% -> 0% of each run, Pallas kernels for 11% -> 11%
where the time goes in v8:
time: 42.8 us; the launch traced here: 42.6 us
  starting transfers between devices  19.4 us (45%)
  waiting for transfers between devices  14.6 us (34%)
  Pallas kernels  7.91 us (18%)
    ppermute x19, starting transfers between devices, swap(): return lax.ppermute(value, AXIS, pairs)  19.4 us
    ppermute x19, waiting for transfers between devices, swap(): return lax.ppermute(value, AXIS, pairs)  14.6 us
    pallas_call x10, Pallas kernels, call(): pl.pallas_call(kernel, out_shape=outs, in_specs=[arrays_in] * len(arrays)...  7.91 us
  transfers between devices with their start and end apart: 19, of which 12 were waited for; matrix products, arithmetic and copies ran while one was open for 0% of the time, Pallas kernels for 11%

profile of v8, /device:TPU:0, one launch (start us, length us, event | category | flops | bytes accessed | tf_op | source)
XLA Modules:
  0.0 42.6 jit_solution(18110817149859241846)
XLA Ops:
  0.0 1.6 %shard_map.55 = (f32[2,128,256]{2,1,0:T(8,128)S(1)}, bf16[4,1024,128]{2,1,0:T(8,128)(2,1)S(1)}, bf16[1024,256]{1,0:T(8,128)(2,1)S(1)}) custom-call(bf16[4,1024,128]{2,1,0:T(8,128)(2,1)} %bases_in.1, bf16[1024,256]{1,0:T(8,128)(2,1)} %vec_in.1), custom_call_target="tpu_custom_call" | custom-call | flops 134217728 | bytes 3407872 | tf_op jit(solution)/shard_map/pallas_call | solution.py:25
  2.5 0.8 %collective-permute-done = f32[2,128,256]{2,1,0:T(8,128)S(1)} collective-permute-done((f32[2,128,256]{2,1,0:T(8,128)S(1)}, f32[2,128,256]{2,1,0:T(8,128)S(1)}, u32[]{:S(2)}, u32[]{:S(2)}) %collective-permute-start) | collective-permute-done | bytes 262176 | tf_op jit(solution)/shard_map/ppermute | solution.py:233
  3.3 3.0 %collective-permute-start.1 = (f32[128,256]{1,0:T(8,128)S(1)}, f32[128,256]{1,0:T(8,128)S(1)}, u32[]{:S(2)}, u32[]{:S(2)}) collective-permute-start(f32[128,256]{1,0:T(8,128)S(1)} %get-tuple-element.96), channel_id=1, source_target_pairs={{0,4},{1,17},{2,6},{3,19},{4,0},{5,21},{6,2},{7,23},{8,12},{9,25},... | collective-permute-start | bytes 393224 | tf_op jit(solution)/shard_map/ppermute | solution.py:233
  6.3 1.5 %collective-permute-start.2 = (f32[128,256]{1,0:T(8,128)S(1)}, f32[128,256]{1,0:T(8,128)S(1)}, u32[]{:S(2)}, u32[]{:S(2)}) collective-permute-start(f32[128,256]{1,0:T(8,128)S(1)} %get-tuple-element.96), channel_id=1, source_target_pairs={{0,2},{1,25},{2,0},{3,27},{4,6},{5,29},{6,4},{7,31},{8,10},{9,17},... | collective-permute-start | bytes 393224 | tf_op jit(solution)/shard_map/ppermute | solution.py:233
  8.4 1.0 %shard_map.58 = (f32[512,256]{1,0:T(8,128)S(1)}, f32[512,256]{1,0:T(8,128)S(1)}) custom-call(bf16[4,1024,128]{2,1,0:T(8,128)(2,1)S(1)} %get-tuple-element.49.bases_ref, f32[8,128]{1,0:T(8,128)S(1)} %bitcast.17, bf16[512,1024]{1,0:T(8,128)(2,1)S(1)} %get-tuple-element.70.turned_ref), custom_call_target="tpu_custom_call" | custom-call | flops 536870912 | bytes 3149824 | tf_op jit(solution)/shard_map/pallas_call | solution.py:25
  10.0 1.2 %collective-permute-done.2 = f32[128,256]{1,0:T(8,128)S(1)} collective-permute-done((f32[128,256]{1,0:T(8,128)S(1)}, f32[128,256]{1,0:T(8,128)S(1)}, u32[]{:S(2)}, u32[]{:S(2)}) %collective-permute-start.2) | collective-permute-done | bytes 131104 | tf_op jit(solution)/shard_map/ppermute | solution.py:233
  11.3 1.6 %collective-permute-start.3 = (f32[128,256]{1,0:T(8,128)S(1)}, f32[128,256]{1,0:T(8,128)S(1)}, u32[]{:S(2)}, u32[]{:S(2)}) collective-permute-start(f32[128,256]{1,0:T(8,128)S(1)} %add_select_fusion.5), channel_id=1, source_target_pairs={{0,8},{1,3},{2,10},{3,1},{4,12},{5,7},{6,14},{7,5},{8,0},{9,11},{1... | collective-permute-start | bytes 393224 | tf_op jit(solution)/shard_map/ppermute | solution.py:233
  13.3 1.1 %collective-permute-done.5 = f32[128,256]{1,0:T(8,128)S(1)} collective-permute-done((f32[128,256]{1,0:T(8,128)S(1)}, f32[128,256]{1,0:T(8,128)S(1)}, u32[]{:S(2)}, u32[]{:S(2)}) %collective-permute-start.5) | collective-permute-done | bytes 131104 | tf_op jit(solution)/shard_map/ppermute | solution.py:233
  15.0 1.3 %collective-permute-done.3 = f32[128,256]{1,0:T(8,128)S(1)} collective-permute-done((f32[128,256]{1,0:T(8,128)S(1)}, f32[128,256]{1,0:T(8,128)S(1)}, u32[]{:S(2)}, u32[]{:S(2)}) %collective-permute-start.3) | collective-permute-done | bytes 131104 | tf_op jit(solution)/shard_map/ppermute | solution.py:233
  16.3 1.6 %collective-permute-start.4 = (f32[128,256]{1,0:T(8,128)S(1)}, f32[128,256]{1,0:T(8,128)S(1)}, u32[]{:S(2)}, u32[]{:S(2)}) collective-permute-start(f32[128,256]{1,0:T(8,128)S(1)} %add_select_fusion.3), channel_id=1, source_target_pairs={{0,2},{1,5},{2,0},{3,7},{4,6},{5,1},{6,4},{7,3},{8,10},{9,13},{10,... | collective-permute-start | bytes 393224 | tf_op jit(solution)/shard_map/ppermute | solution.py:233
  17.9 1.5 %collective-permute-done.6 = f32[128,256]{1,0:T(8,128)S(1)} collective-permute-done((f32[128,256]{1,0:T(8,128)S(1)}, f32[128,256]{1,0:T(8,128)S(1)}, u32[]{:S(2)}, u32[]{:S(2)}) %collective-permute-start.6) | collective-permute-done | bytes 131104 | tf_op jit(solution)/shard_map/ppermute | solution.py:233
  20.3 1.1 %collective-permute-done.4 = f32[128,256]{1,0:T(8,128)S(1)} collective-permute-done((f32[128,256]{1,0:T(8,128)S(1)}, f32[128,256]{1,0:T(8,128)S(1)}, u32[]{:S(2)}, u32[]{:S(2)}) %collective-permute-start.4) | collective-permute-done | bytes 131104 | tf_op jit(solution)/shard_map/ppermute | solution.py:233
  21.9 1.5 %collective-permute-done.9 = f32[2,128,256]{2,1,0:T(8,128)S(1)} collective-permute-done((f32[2,128,256]{2,1,0:T(8,128)S(1)}, f32[2,128,256]{2,1,0:T(8,128)S(1)}, u32[]{:S(2)}, u32[]{:S(2)}) %collective-permute-start.9) | collective-permute-done | bytes 262176 | tf_op jit(solution)/shard_map/ppermute | solution.py:233
  23.4 0.9 %collective-permute-start.10 = (f32[128,256]{1,0:T(8,128)S(1)}, f32[128,256]{1,0:T(8,128)S(1)}, u32[]{:S(2)}, u32[]{:S(2)}) collective-permute-start(f32[128,256]{1,0:T(8,128)S(1)} %get-tuple-element.81), channel_id=1, source_target_pairs={{0,4},{1,17},{2,6},{3,19},{4,0},{5,21},{6,2},{7,23},{8,12},{9,25},... | collective-permute-start | bytes 393224 | tf_op jit(solution)/shard_map/ppermute | solution.py:233
  24.3 1.5 %collective-permute-start.11 = (f32[128,256]{1,0:T(8,128)S(1)}, f32[128,256]{1,0:T(8,128)S(1)}, u32[]{:S(2)}, u32[]{:S(2)}) collective-permute-start(f32[128,256]{1,0:T(8,128)S(1)} %get-tuple-element.81), channel_id=1, source_target_pairs={{0,2},{1,25},{2,0},{3,27},{4,6},{5,29},{6,4},{7,31},{8,10},{9,17},... | collective-permute-start | bytes 393224 | tf_op jit(solution)/shard_map/ppermute | solution.py:233
  26.3 2.1 %collective-permute-done.10 = f32[128,256]{1,0:T(8,128)S(1)} collective-permute-done((f32[128,256]{1,0:T(8,128)S(1)}, f32[128,256]{1,0:T(8,128)S(1)}, u32[]{:S(2)}, u32[]{:S(2)}) %collective-permute-start.10) | collective-permute-done | bytes 131104 | tf_op jit(solution)/shard_map/ppermute | solution.py:233
  28.5 0.8 %collective-permute-done.11 = f32[128,256]{1,0:T(8,128)S(1)} collective-permute-done((f32[128,256]{1,0:T(8,128)S(1)}, f32[128,256]{1,0:T(8,128)S(1)}, u32[]{:S(2)}, u32[]{:S(2)}) %collective-permute-start.11) | collective-permute-done | bytes 131104 | tf_op jit(solution)/shard_map/ppermute | solution.py:233
  29.3 1.9 %collective-permute-start.12 = (f32[128,256]{1,0:T(8,128)S(1)}, f32[128,256]{1,0:T(8,128)S(1)}, u32[]{:S(2)}, u32[]{:S(2)}) collective-permute-start(f32[128,256]{1,0:T(8,128)S(1)} %add_select_fusion.4), channel_id=1, source_target_pairs={{0,8},{1,3},{2,10},{3,1},{4,12},{5,7},{6,14},{7,5},{8,0},{9,11},{1... | collective-permute-start | bytes 393224 | tf_op jit(solution)/shard_map/ppermute | solution.py:233
  31.2 2.2 %collective-permute-start.15 = (f32[128,256]{1,0:T(8,128)S(1)}, f32[128,256]{1,0:T(8,128)S(1)}, u32[]{:S(2)}, u32[]{:S(2)}) collective-permute-start(f32[128,256]{1,0:T(8,128)S(1)} %add.53.high_ref), channel_id=1, source_target_pairs={{0,1},{1,0},{2,3},{3,2},{4,5},{5,4},{6,7},{7,6},{8,9},{9,8},{10,11... | collective-permute-start | bytes 393224 | tf_op jit(solution)/shard_map/ppermute | solution.py:233
  33.4 1.5 %collective-permute-start.17 = (f32[128,256]{1,0:T(8,128)S(1)}, f32[128,256]{1,0:T(8,128)S(1)}, u32[]{:S(2)}, u32[]{:S(2)}) collective-permute-start(f32[128,256]{1,0:T(8,128)S(1)} %collective-permute-done.14), channel_id=1, source_target_pairs={{0,4},{1,3},{2,6},{3,1},{4,0},{5,7},{6,2},{7,5},{8,12},{9,11},{10,... | collective-permute-start | bytes 393224 | tf_op jit(solution)/shard_map/ppermute | solution.py:233
  34.9 1.0 %collective-permute-start.13 = (f32[128,256]{1,0:T(8,128)S(1)}, f32[128,256]{1,0:T(8,128)S(1)}, u32[]{:S(2)}, u32[]{:S(2)}) collective-permute-start(f32[128,256]{1,0:T(8,128)S(1)} %add_select_fusion.1), channel_id=1, source_target_pairs={{0,2},{1,5},{2,0},{3,7},{4,6},{5,1},{6,4},{7,3},{8,10},{9,13},{10,... | collective-permute-start | bytes 393224 | tf_op jit(solution)/shard_map/ppermute | solution.py:233
  35.9 2.4 %collective-permute-done.17 = f32[128,256]{1,0:T(8,128)S(1)} collective-permute-done((f32[128,256]{1,0:T(8,128)S(1)}, f32[128,256]{1,0:T(8,128)S(1)}, u32[]{:S(2)}, u32[]{:S(2)}) %collective-permute-start.17) | collective-permute-done | bytes 131104 | tf_op jit(solution)/shard_map/ppermute | solution.py:233
  38.5 1.2 %shard_map.62.part_ref = f32[1024,256]{1,0:T(8,128)S(1)} custom-call(bf16[4,128,128]{2,1,0:T(8,128)(2,1)S(1)} %get-tuple-element.73.oriented_ref, f32[128,256]{1,0:T(8,128)S(1)} %add.53.high_ref, f32[128,256]{1,0:T(8,128)S(1)} %add_select_fusion.2.low_ref, f32[128,256]{1,0:T(8,128)S(1)} %collective-permute-done.15.high_other_ref, ...), custom_call_target="tpu_custom_call" | custom-call | flops 536870912 | bytes 4853760 | tf_op jit(solution)/shard_map/pallas_call | solution.py:25
  41.4 1.2 %shard_map.64 = bf16[1024,256]{1,0:T(8,128)(2,1)} custom-call(bf16[4,128,128]{2,1,0:T(8,128)(2,1)S(1)} %get-tuple-element.73.oriented_ref, f32[128,256]{1,0:T(8,128)S(1)} %collective-permute-done.16.other_ref, bf16[4,1024,128]{2,1,0:T(8,128)(2,1)S(1)} %get-tuple-element.49.bases_ref, f32[1024,256]{1,0:T(8,128)S(1)} %shard_map.63.part_ref), custom_call_target="tpu_custom_call" | custom-call | flops 67108864 | bytes 2883584 | tf_op jit(solution)/shard_map/pallas_call | solution.py:25
  (40 shorter events, 7.0 us)
Async XLA Ops:
  1.6 1.7 %collective-permute-start = (f32[2,128,256]{2,1,0:T(8,128)S(1)}, f32[2,128,256]{2,1,0:T(8,128)S(1)}, u32[]{:S(2)}, u32[]{:S(2)}) collective-permute-start(f32[2,128,256]{2,1,0:T(8,128)S(1)} %get-tuple-element.52), channel_id=1, source_target_pairs={{0,1},{1,0},{2,3},{3,2},{4,5},{5,4},{6,7},{7,6},{8,9},{9,8},{10,11... | collective-permute-start | bytes 786440 | tf_op jit(solution)/shard_map/ppermute | solution.py:233
  2.5 5.3 %copy-start.1 = (bf16[15,128,128]{2,1,0:T(8,128)(2,1)S(1)}, bf16[15,128,128]{2,1,0:T(8,128)(2,1)}, u32[]{:S(2)}) copy-start(bf16[15,128,128]{2,1,0:T(8,128)(2,1)} %couplings_ref.1) | copy-start | bytes 1474564
  3.3 6.7 %collective-permute-start.1 = (f32[128,256]{1,0:T(8,128)S(1)}, f32[128,256]{1,0:T(8,128)S(1)}, u32[]{:S(2)}, u32[]{:S(2)}) collective-permute-start(f32[128,256]{1,0:T(8,128)S(1)} %get-tuple-element.96), channel_id=1, source_target_pairs={{0,4},{1,17},{2,6},{3,19},{4,0},{5,21},{6,2},{7,23},{8,12},{9,25},... | collective-permute-start | bytes 393224 | tf_op jit(solution)/shard_map/ppermute | solution.py:233
  6.3 5.0 %collective-permute-start.2 = (f32[128,256]{1,0:T(8,128)S(1)}, f32[128,256]{1,0:T(8,128)S(1)}, u32[]{:S(2)}, u32[]{:S(2)}) collective-permute-start(f32[128,256]{1,0:T(8,128)S(1)} %get-tuple-element.96), channel_id=1, source_target_pairs={{0,2},{1,25},{2,0},{3,27},{4,6},{5,29},{6,4},{7,31},{8,10},{9,17},... | collective-permute-start | bytes 393224 | tf_op jit(solution)/shard_map/ppermute | solution.py:233
  7.8 0.7 %copy-start.2 = (f32[1024]{0:T(1024)S(1)}, f32[1024]{0:T(1024)}, u32[]{:S(2)}) copy-start(f32[1024]{0:T(1024)} %param.9) | copy-start | bytes 12292
  8.4 4.5 %copy-start = (bf16[1024,512]{1,0:T(8,128)(2,1)S(1)}, bf16[1024,512]{1,0:T(8,128)(2,1)}, u32[]{:S(2)}) copy-start(bf16[1024,512]{1,0:T(8,128)(2,1)} %leaves_ref.3) | copy-start | bytes 3145732
  9.4 5.0 %collective-permute-start.5 = (f32[128,256]{1,0:T(8,128)S(1)}, f32[128,256]{1,0:T(8,128)S(1)}, u32[]{:S(2)}, u32[]{:S(2)}) collective-permute-start(f32[128,256]{1,0:T(8,128)S(1)} %get-tuple-element.95), channel_id=1, source_target_pairs={{0,2},{1,5},{2,0},{3,7},{4,6},{5,1},{6,4},{7,3},{8,10},{9,13},{10,... | collective-permute-start | bytes 393224 | tf_op jit(solution)/shard_map/ppermute | solution.py:233
  11.3 5.0 %collective-permute-start.3 = (f32[128,256]{1,0:T(8,128)S(1)}, f32[128,256]{1,0:T(8,128)S(1)}, u32[]{:S(2)}, u32[]{:S(2)}) collective-permute-start(f32[128,256]{1,0:T(8,128)S(1)} %add_select_fusion.5), channel_id=1, source_target_pairs={{0,8},{1,3},{2,10},{3,1},{4,12},{5,7},{6,14},{7,5},{8,0},{9,11},{1... | collective-permute-start | bytes 393224 | tf_op jit(solution)/shard_map/ppermute | solution.py:233
  14.4 5.0 %collective-permute-start.6 = (f32[128,256]{1,0:T(8,128)S(1)}, f32[128,256]{1,0:T(8,128)S(1)}, u32[]{:S(2)}, u32[]{:S(2)}) collective-permute-start(f32[128,256]{1,0:T(8,128)S(1)} %collective-permute-done.5), channel_id=1, source_target_pairs={{0,4},{1,3},{2,6},{3,1},{4,0},{5,7},{6,2},{7,5},{8,12},{9,11},{10,... | collective-permute-start | bytes 393224 | tf_op jit(solution)/shard_map/ppermute | solution.py:233
  14.9 4.6 %collective-permute-start.7 = (f32[512,256]{1,0:T(8,128)S(1)}, f32[512,256]{1,0:T(8,128)S(1)}, u32[]{:S(2)}, u32[]{:S(2)}) collective-permute-start(f32[512,256]{1,0:T(8,128)S(1)} %get-tuple-element.69), channel_id=1, source_target_pairs={{0,1},{1,0},{2,3},{3,2},{4,5},{5,4},{6,7},{7,6},{8,9},{9,8},{10,11... | collective-permute-start | bytes 1572872 | tf_op jit(solution)/shard_map/ppermute | solution.py:233
  16.3 5.0 %collective-permute-start.4 = (f32[128,256]{1,0:T(8,128)S(1)}, f32[128,256]{1,0:T(8,128)S(1)}, u32[]{:S(2)}, u32[]{:S(2)}) collective-permute-start(f32[128,256]{1,0:T(8,128)S(1)} %add_select_fusion.3), channel_id=1, source_target_pairs={{0,2},{1,5},{2,0},{3,7},{4,6},{5,1},{6,4},{7,3},{8,10},{9,13},{10,... | collective-permute-start | bytes 393224 | tf_op jit(solution)/shard_map/ppermute | solution.py:233
  19.4 1.9 %collective-permute-start.8 = (f32[128,256]{1,0:T(8,128)S(1)}, f32[128,256]{1,0:T(8,128)S(1)}, u32[]{:S(2)}, u32[]{:S(2)}) collective-permute-start(f32[128,256]{1,0:T(8,128)S(1)} %add_select_fusion.2.low_ref), channel_id=1, source_target_pairs={{0,1},{1,0},{2,3},{3,2},{4,5},{5,4},{6,7},{7,6},{8,9},{9,8},{10,11... | collective-permute-start | bytes 393224 | tf_op jit(solution)/shard_map/ppermute | solution.py:233
  21.8 1.6 %collective-permute-start.9 = (f32[2,128,256]{2,1,0:T(8,128)S(1)}, f32[2,128,256]{2,1,0:T(8,128)S(1)}, u32[]{:S(2)}, u32[]{:S(2)}) collective-permute-start(f32[2,128,256]{2,1,0:T(8,128)S(1)} %get-tuple-element.79), channel_id=1, source_target_pairs={{0,1},{1,0},{2,3},{3,2},{4,5},{5,4},{6,7},{7,6},{8,9},{9,8},{10,11... | collective-permute-start | bytes 786440 | tf_op jit(solution)/shard_map/ppermute | solution.py:233
  23.4 5.0 %collective-permute-start.10 = (f32[128,256]{1,0:T(8,128)S(1)}, f32[128,256]{1,0:T(8,128)S(1)}, u32[]{:S(2)}, u32[]{:S(2)}) collective-permute-start(f32[128,256]{1,0:T(8,128)S(1)} %get-tuple-element.81), channel_id=1, source_target_pairs={{0,4},{1,17},{2,6},{3,19},{4,0},{5,21},{6,2},{7,23},{8,12},{9,25},... | collective-permute-start | bytes 393224 | tf_op jit(solution)/shard_map/ppermute | solution.py:233
  24.3 5.0 %collective-permute-start.11 = (f32[128,256]{1,0:T(8,128)S(1)}, f32[128,256]{1,0:T(8,128)S(1)}, u32[]{:S(2)}, u32[]{:S(2)}) collective-permute-start(f32[128,256]{1,0:T(8,128)S(1)} %get-tuple-element.81), channel_id=1, source_target_pairs={{0,2},{1,25},{2,0},{3,27},{4,6},{5,29},{6,4},{7,31},{8,10},{9,17},... | collective-permute-start | bytes 393224 | tf_op jit(solution)/shard_map/ppermute | solution.py:233
  25.8 5.4 %collective-permute-start.14 = (f32[128,256]{1,0:T(8,128)S(1)}, f32[128,256]{1,0:T(8,128)S(1)}, u32[]{:S(2)}, u32[]{:S(2)}) collective-permute-start(f32[128,256]{1,0:T(8,128)S(1)} %get-tuple-element.86), channel_id=1, source_target_pairs={{0,2},{1,5},{2,0},{3,7},{4,6},{5,1},{6,4},{7,3},{8,10},{9,13},{10,... | collective-permute-start | bytes 393224 | tf_op jit(solution)/shard_map/ppermute | solution.py:233
  29.3 5.6 %collective-permute-start.12 = (f32[128,256]{1,0:T(8,128)S(1)}, f32[128,256]{1,0:T(8,128)S(1)}, u32[]{:S(2)}, u32[]{:S(2)}) collective-permute-start(f32[128,256]{1,0:T(8,128)S(1)} %add_select_fusion.4), channel_id=1, source_target_pairs={{0,8},{1,3},{2,10},{3,1},{4,12},{5,7},{6,14},{7,5},{8,0},{9,11},{1... | collective-permute-start | bytes 393224 | tf_op jit(solution)/shard_map/ppermute | solution.py:233
  31.2 7.2 %collective-permute-start.15 = (f32[128,256]{1,0:T(8,128)S(1)}, f32[128,256]{1,0:T(8,128)S(1)}, u32[]{:S(2)}, u32[]{:S(2)}) collective-permute-start(f32[128,256]{1,0:T(8,128)S(1)} %add.53.high_ref), channel_id=1, source_target_pairs={{0,1},{1,0},{2,3},{3,2},{4,5},{5,4},{6,7},{7,6},{8,9},{9,8},{10,11... | collective-permute-start | bytes 393224 | tf_op jit(solution)/shard_map/ppermute | solution.py:233
  33.4 5.0 %collective-permute-start.17 = (f32[128,256]{1,0:T(8,128)S(1)}, f32[128,256]{1,0:T(8,128)S(1)}, u32[]{:S(2)}, u32[]{:S(2)}) collective-permute-start(f32[128,256]{1,0:T(8,128)S(1)} %collective-permute-done.14), channel_id=1, source_target_pairs={{0,4},{1,3},{2,6},{3,1},{4,0},{5,7},{6,2},{7,5},{8,12},{9,11},{10,... | collective-permute-start | bytes 393224 | tf_op jit(solution)/shard_map/ppermute | solution.py:233
  34.9 5.0 %collective-permute-start.13 = (f32[128,256]{1,0:T(8,128)S(1)}, f32[128,256]{1,0:T(8,128)S(1)}, u32[]{:S(2)}, u32[]{:S(2)}) collective-permute-start(f32[128,256]{1,0:T(8,128)S(1)} %add_select_fusion.1), channel_id=1, source_target_pairs={{0,2},{1,5},{2,0},{3,7},{4,6},{5,1},{6,4},{7,3},{8,10},{9,13},{10,... | collective-permute-start | bytes 393224 | tf_op jit(solution)/shard_map/ppermute | solution.py:233
  38.4 1.9 %collective-permute-start.18 = (f32[128,256]{1,0:T(8,128)S(1)}, f32[128,256]{1,0:T(8,128)S(1)}, u32[]{:S(2)}, u32[]{:S(2)}) collective-permute-start(f32[128,256]{1,0:T(8,128)S(1)} %add_select_fusion.low_ref), channel_id=1, source_target_pairs={{0,1},{1,0},{2,3},{3,2},{4,5},{5,4},{6,7},{7,6},{8,9},{9,8},{10,11... | collective-permute-start | bytes 393224 | tf_op jit(solution)/shard_map/ppermute | solution.py:233
  40.0 1.4 %collective-permute-start.16 = (f32[128,256]{1,0:T(8,128)S(1)}, f32[128,256]{1,0:T(8,128)S(1)}, u32[]{:S(2)}, u32[]{:S(2)}) collective-permute-start(f32[128,256]{1,0:T(8,128)S(1)} %add.59.high_ref), channel_id=1, source_target_pairs={{0,1},{1,0},{2,3},{3,2},{4,5},{5,4},{6,7},{7,6},{8,9},{9,8},{10,11... | collective-permute-start | bytes 393224 | tf_op jit(solution)/shard_map/ppermute | solution.py:233

commit v9 on v8

--- a/solution.py
+++ b/solution.py
@@ -53,33 +53,26 @@
     return parity_of() + 2 * slot
 
 
-def first_kernel(bases_in, vec_in, out_ref, bases_ref, vec_ref, sems):
-    rank = bases_in.shape[2]
-
-    def basis_copy(level, sem):
-        return pltpu.make_async_copy(bases_in.at[level], bases_ref.at[level], sem)
-
-    copies = [pltpu.make_async_copy(vec_in, vec_ref, sems.at[0])]
-    copies += [basis_copy(other_level(slot), sems.at[1 + slot]) for slot in range(2)]
-    later = [basis_copy(own_level(slot), sems.at[3 + slot]) for slot in range(2)]
-    for copy in copies + later:
+def first_kernel(bases_in, vec_in, send_high_ref, vec_ref, basis_buf, sems):
+    copies = [
+        pltpu.make_async_copy(vec_in, vec_ref, sems.at[0]),
+        pltpu.make_async_copy(bases_in.at[other_level(0)], basis_buf, sems.at[1]),
+    ]
+    for copy in copies:
         copy.start()
     for copy in copies:
         copy.wait()
-    basis = jnp.concatenate([bases_ref[other_level(slot)] for slot in range(2)], axis=1)
+    send_high_ref[...] = transposed_dot(basis_buf[...], vec_ref[...])
+
+
+def kept_kernel(bases_ref, vec_ref, send_low_ref, high_ref, low_ref):
+    rank = bases_ref.shape[2]
+    order = [other_level(1), own_level(0), own_level(1)]
+    basis = jnp.concatenate([bases_ref[level] for level in order], axis=1)
     proj = transposed_dot(basis, vec_ref[...])
-    out_ref[0] = proj[:rank]
-    out_ref[1] = proj[rank:]
-    for copy in later:
-        copy.wait()
-
-
-def kept_kernel(bases_ref, vec_ref, high_ref, low_ref):
-    rank = bases_ref.shape[2]
-    both = jnp.concatenate([bases_ref[own_level(slot)] for slot in range(2)], axis=1)
-    proj = transposed_dot(both, vec_ref[...])
-    high_ref[...] = proj[:rank]
-    low_ref[...] = proj[rank:]
+    send_low_ref[...] = proj[:rank]
+    high_ref[...] = proj[rank : 2 * rank]
+    low_ref[...] = proj[2 * rank :]
 
 
 def prepare_kernel(couplings_ref, bases_ref, oriented_ref, turned_ref):
@@ -157,13 +150,13 @@
     gram_ref[:, rank:] = rest[:, :rank]
 
 
-def middle_kernel(factors, oriented_ref, high_ref, gram_ref, sums_ref, send_ref, keep_high_ref, keep_low_ref):
+def middle_kernel(factors, oriented_ref, high_ref, gram_ref, sums_ref, send_high_ref, send_low_ref, keep_high_ref, keep_low_ref):
     coeffs = own_coefficients(oriented_ref, 0, high_ref[...], factors)
     delta = jnp.dot(gram_ref[...], jnp.concatenate([coeffs] * 2, axis=0), preferred_element_type=F32)
     proj = sums_ref[...] + delta
     rank = high_ref.shape[0]
-    send_ref[0] = proj[:rank]
-    send_ref[1] = proj[rank : 2 * rank]
+    send_high_ref[...] = proj[:rank]
+    send_low_ref[...] = proj[rank : 2 * rank]
     keep_high_ref[...] = proj[2 * rank : 3 * rank]
     keep_low_ref[...] = proj[3 * rank :]
 
@@ -235,10 +228,9 @@
     def beside(arrays, *riders):
         return lax.optimization_barrier((*arrays, *riders))
 
-    def begin(send, high, low):
-        got = swap(send, 1, 1)
-        high = high + got[0]
-        low = low + got[1]
+    def begin(send_high, send_low, high, low):
+        high = high + swap(send_high, 1, 1)
+        low = low + swap(send_low, 1, 1)
         for bit in range(1, bits - levels):
             high = high + swap(high, 1 << bit, 1 << bit)
             low = low + swap(low, 1 << bit, 1 << bit)
@@ -259,15 +251,15 @@
         got, *ridden = beside((got,), *rider_three(low, passenger, *ridden))
         return high + got, low, *ridden
 
-    send, bases, signal = call(
+    send_high, signal = call(
         first_kernel,
-        [pair_shape, jax.ShapeDtypeStruct(bases.shape, BF16), jax.ShapeDtypeStruct(signal.shape, BF16)],
+        [sums_shape, jax.ShapeDtypeStruct(signal.shape, BF16)],
         [pltpu.with_memory_space_constraint(array, pltpu.HBM) for array in (bases, signal)],
-        2 * mults,
+        mults,
         arrays_in=HBM,
-        scratch=[pltpu.SemaphoreType.DMA((5,))],
-    )
-    kept = call(kept_kernel, [sums_shape] * 2, [bases, signal], 2 * mults)
+        scratch=[pltpu.VMEM((rows_dev, rank), BF16), pltpu.SemaphoreType.DMA((2,))],
+    )
+    kept = call(kept_kernel, [sums_shape] * 3, [bases, signal], 3 * mults)
 
     def first_riders():
         oriented, turned = call(
@@ -299,16 +291,16 @@
         return oriented, part, sums, gram
 
     high, low, oriented, part, sums, gram = rounds(
-        *begin(send, *kept), first_riders, second_riders, third_riders
+        *begin(send_high, *kept), first_riders, second_riders, third_riders
     )
     high, low_other = beside((high, swap(low, 1, 1)))
-    send, *kept = call(
+    kept = call(
         functools.partial(middle_kernel, factors),
-        [pair_shape, sums_shape, sums_shape],
+        [sums_shape] * 4,
         [oriented, high, gram, sums],
         mults,
     )
-    next_high, next_low, high, low = beside(begin(send, *kept), high, low)
+    next_high, next_low, high, low = beside(begin(*kept), high, low)
 
     def second_part(_, high_other):
         return call(

time: 42.8 us -> 42.5 us (level)
  waiting for transfers between devices: 14.6 us -> 13.5 us
  starting transfers between devices: 19.4 us -> 20.2 us
    ppermute x19 -> x21, waiting for transfers between devices: 14.6 us -> 13.5 us  [swap(): return lax.ppermute(value, AXIS, pairs)]
    ppermute x19 -> x21, starting transfers between devices: 19.4 us -> 20.2 us  [swap(): return lax.ppermute(value, AXIS, pairs)]
  transfers between devices with their start and end apart: 19 -> 21, of which waited for: 12 -> 13; matrix products, arithmetic and copies ran while one was open for 0% -> 1% of each run, Pallas kernels for 11% -> 11%
where the time goes in v9:
time: 42.5 us; the launch traced here: 42.3 us
  starting transfers between devices  20.2 us (48%)
  waiting for transfers between devices  13.5 us (32%)
  Pallas kernels  7.87 us (19%)
    ppermute x21, starting transfers between devices, swap(): return lax.ppermute(value, AXIS, pairs)  20.2 us
    ppermute x21, waiting for transfers between devices, swap(): return lax.ppermute(value, AXIS, pairs)  13.5 us
    pallas_call x10, Pallas kernels, call(): pl.pallas_call(kernel, out_shape=outs, in_specs=[arrays_in] * len(arrays)...  7.87 us
  transfers between devices with their start and end apart: 21, of which 13 were waited for; matrix products, arithmetic and copies ran while one was open for 1% of the time, Pallas kernels for 11%

profile of v9, /device:TPU:0, one launch (start us, length us, event | category | flops | bytes accessed | tf_op | source)
XLA Modules:
  0.0 42.3 jit_solution(3630332415229876310)
XLA Ops:
  0.0 1.5 %shard_map.55 = (f32[128,256]{1,0:T(8,128)S(1)}, bf16[1024,256]{1,0:T(8,128)(2,1)S(1)}) custom-call(bf16[4,1024,128]{2,1,0:T(8,128)(2,1)} %bases_ref.11, bf16[1024,256]{1,0:T(8,128)(2,1)} %vec_in.1), custom_call_target="tpu_custom_call" | custom-call | flops 67108864 | bytes 2228224 | tf_op jit(solution)/shard_map/pallas_call | solution.py:25
  3.0 2.9 %collective-permute-start.1 = (f32[128,256]{1,0:T(8,128)S(1)}, f32[128,256]{1,0:T(8,128)S(1)}, u32[]{:S(2)}, u32[]{:S(2)}) collective-permute-start(f32[128,256]{1,0:T(8,128)S(1)} %add.47), channel_id=1, source_target_pairs={{0,4},{1,17},{2,6},{3,19},{4,0},{5,21},{6,2},{7,23},{8,12},{9,25},... | collective-permute-start | bytes 393224 | tf_op jit(solution)/shard_map/ppermute | solution.py:226
  6.0 1.5 %collective-permute-start.2 = (f32[128,256]{1,0:T(8,128)S(1)}, f32[128,256]{1,0:T(8,128)S(1)}, u32[]{:S(2)}, u32[]{:S(2)}) collective-permute-start(f32[128,256]{1,0:T(8,128)S(1)} %add.47), channel_id=1, source_target_pairs={{0,2},{1,25},{2,0},{3,27},{4,6},{5,29},{6,4},{7,31},{8,10},{9,17},... | collective-permute-start | bytes 393224 | tf_op jit(solution)/shard_map/ppermute | solution.py:226
  8.1 1.0 %shard_map.58 = (f32[512,256]{1,0:T(8,128)S(1)}, f32[512,256]{1,0:T(8,128)S(1)}) custom-call(bf16[4,1024,128]{2,1,0:T(8,128)(2,1)S(1)} %copy-done, f32[8,128]{1,0:T(8,128)S(1)} %bitcast.1, bf16[512,1024]{1,0:T(8,128)(2,1)S(1)} %get-tuple-element.71.turned_ref), custom_call_target="tpu_custom_call" | custom-call | flops 536870912 | bytes 3149824 | tf_op jit(solution)/shard_map/pallas_call | solution.py:25
  9.7 1.2 %collective-permute-done.2 = f32[128,256]{1,0:T(8,128)S(1)} collective-permute-done((f32[128,256]{1,0:T(8,128)S(1)}, f32[128,256]{1,0:T(8,128)S(1)}, u32[]{:S(2)}, u32[]{:S(2)}) %collective-permute-start.2) | collective-permute-done | bytes 131104 | tf_op jit(solution)/shard_map/ppermute | solution.py:226
  11.0 1.6 %collective-permute-start.3 = (f32[128,256]{1,0:T(8,128)S(1)}, f32[128,256]{1,0:T(8,128)S(1)}, u32[]{:S(2)}, u32[]{:S(2)}) collective-permute-start(f32[128,256]{1,0:T(8,128)S(1)} %add_select_fusion.5), channel_id=1, source_target_pairs={{0,8},{1,3},{2,10},{3,1},{4,12},{5,7},{6,14},{7,5},{8,0},{9,11},{1... | collective-permute-start | bytes 393224 | tf_op jit(solution)/shard_map/ppermute | solution.py:226
  13.0 1.1 %collective-permute-done.6 = f32[128,256]{1,0:T(8,128)S(1)} collective-permute-done((f32[128,256]{1,0:T(8,128)S(1)}, f32[128,256]{1,0:T(8,128)S(1)}, u32[]{:S(2)}, u32[]{:S(2)}) %collective-permute-start.6) | collective-permute-done | bytes 131104 | tf_op jit(solution)/shard_map/ppermute | solution.py:226
  14.8 1.2 %collective-permute-done.3 = f32[128,256]{1,0:T(8,128)S(1)} collective-permute-done((f32[128,256]{1,0:T(8,128)S(1)}, f32[128,256]{1,0:T(8,128)S(1)}, u32[]{:S(2)}, u32[]{:S(2)}) %collective-permute-start.3) | collective-permute-done | bytes 131104 | tf_op jit(solution)/shard_map/ppermute | solution.py:226
  16.0 1.6 %collective-permute-start.4 = (f32[128,256]{1,0:T(8,128)S(1)}, f32[128,256]{1,0:T(8,128)S(1)}, u32[]{:S(2)}, u32[]{:S(2)}) collective-permute-start(f32[128,256]{1,0:T(8,128)S(1)} %add_select_fusion.3), channel_id=1, source_target_pairs={{0,2},{1,5},{2,0},{3,7},{4,6},{5,1},{6,4},{7,3},{8,10},{9,13},{10,... | collective-permute-start | bytes 393224 | tf_op jit(solution)/shard_map/ppermute | solution.py:226
  17.6 1.6 %collective-permute-done.7 = f32[128,256]{1,0:T(8,128)S(1)} collective-permute-done((f32[128,256]{1,0:T(8,128)S(1)}, f32[128,256]{1,0:T(8,128)S(1)}, u32[]{:S(2)}, u32[]{:S(2)}) %collective-permute-start.7) | collective-permute-done | bytes 131104 | tf_op jit(solution)/shard_map/ppermute | solution.py:226
  19.3 0.8 %shard_map.60 = (f32[512,256]{1,0:T(8,128)S(1)}, bf16[512,256]{1,0:T(8,128)(2,1)S(1)}) custom-call(bf16[4,128,128]{2,1,0:T(8,128)(2,1)S(1)} %get-tuple-element.74.oriented_ref, f32[128,256]{1,0:T(8,128)S(1)} %add_select_fusion.2.low_ref, f32[512,256]{1,0:T(8,128)S(1)} %get-tuple-element.69.keep_ref, f32[512,256]{1,0:T(8,128)S(1)} %collective-permute-done.8.got_ref, ...), custom_call_target="tpu_custom_call" | custom-call | flops 335544320 | bytes 4198400 | tf_op jit(solution)/shard_map/pallas_call | solution.py:25
  20.0 1.0 %collective-permute-done.4 = f32[128,256]{1,0:T(8,128)S(1)} collective-permute-done((f32[128,256]{1,0:T(8,128)S(1)}, f32[128,256]{1,0:T(8,128)S(1)}, u32[]{:S(2)}, u32[]{:S(2)}) %collective-permute-start.4) | collective-permute-done | bytes 131104 | tf_op jit(solution)/shard_map/ppermute | solution.py:226
  22.1 0.8 %collective-permute-done.10 = f32[128,256]{1,0:T(8,128)S(1)} collective-permute-done((f32[128,256]{1,0:T(8,128)S(1)}, f32[128,256]{1,0:T(8,128)S(1)}, u32[]{:S(2)}, u32[]{:S(2)}) %collective-permute-start.10) | collective-permute-done | bytes 131104 | tf_op jit(solution)/shard_map/ppermute | solution.py:226
  23.1 0.8 %collective-permute-start.12 = (f32[128,256]{1,0:T(8,128)S(1)}, f32[128,256]{1,0:T(8,128)S(1)}, u32[]{:S(2)}, u32[]{:S(2)}) collective-permute-start(f32[128,256]{1,0:T(8,128)S(1)} %add.54), channel_id=1, source_target_pairs={{0,4},{1,17},{2,6},{3,19},{4,0},{5,21},{6,2},{7,23},{8,12},{9,25},... | collective-permute-start | bytes 393224 | tf_op jit(solution)/shard_map/ppermute | solution.py:226
  23.9 1.8 %collective-permute-start.13 = (f32[128,256]{1,0:T(8,128)S(1)}, f32[128,256]{1,0:T(8,128)S(1)}, u32[]{:S(2)}, u32[]{:S(2)}) collective-permute-start(f32[128,256]{1,0:T(8,128)S(1)} %add.54), channel_id=1, source_target_pairs={{0,2},{1,25},{2,0},{3,27},{4,6},{5,29},{6,4},{7,31},{8,10},{9,17},... | collective-permute-start | bytes 393224 | tf_op jit(solution)/shard_map/ppermute | solution.py:226
  25.9 2.2 %collective-permute-done.12 = f32[128,256]{1,0:T(8,128)S(1)} collective-permute-done((f32[128,256]{1,0:T(8,128)S(1)}, f32[128,256]{1,0:T(8,128)S(1)}, u32[]{:S(2)}, u32[]{:S(2)}) %collective-permute-start.12) | collective-permute-done | bytes 131104 | tf_op jit(solution)/shard_map/ppermute | solution.py:226
  28.1 0.7 %collective-permute-done.13 = f32[128,256]{1,0:T(8,128)S(1)} collective-permute-done((f32[128,256]{1,0:T(8,128)S(1)}, f32[128,256]{1,0:T(8,128)S(1)}, u32[]{:S(2)}, u32[]{:S(2)}) %collective-permute-start.13) | collective-permute-done | bytes 131104 | tf_op jit(solution)/shard_map/ppermute | solution.py:226
  28.9 2.2 %collective-permute-start.14 = (f32[128,256]{1,0:T(8,128)S(1)}, f32[128,256]{1,0:T(8,128)S(1)}, u32[]{:S(2)}, u32[]{:S(2)}) collective-permute-start(f32[128,256]{1,0:T(8,128)S(1)} %add_select_fusion.4), channel_id=1, source_target_pairs={{0,8},{1,3},{2,10},{3,1},{4,12},{5,7},{6,14},{7,5},{8,0},{9,11},{1... | collective-permute-start | bytes 393224 | tf_op jit(solution)/shard_map/ppermute | solution.py:226
  31.1 2.0 %collective-permute-start.17 = (f32[128,256]{1,0:T(8,128)S(1)}, f32[128,256]{1,0:T(8,128)S(1)}, u32[]{:S(2)}, u32[]{:S(2)}) collective-permute-start(f32[128,256]{1,0:T(8,128)S(1)} %add.53.high_ref), channel_id=1, source_target_pairs={{0,1},{1,0},{2,3},{3,2},{4,5},{5,4},{6,7},{7,6},{8,9},{9,8},{10,11... | collective-permute-start | bytes 393224 | tf_op jit(solution)/shard_map/ppermute | solution.py:226
  33.1 1.5 %collective-permute-start.19 = (f32[128,256]{1,0:T(8,128)S(1)}, f32[128,256]{1,0:T(8,128)S(1)}, u32[]{:S(2)}, u32[]{:S(2)}) collective-permute-start(f32[128,256]{1,0:T(8,128)S(1)} %collective-permute-done.16), channel_id=1, source_target_pairs={{0,4},{1,3},{2,6},{3,1},{4,0},{5,7},{6,2},{7,5},{8,12},{9,11},{10,... | collective-permute-start | bytes 393224 | tf_op jit(solution)/shard_map/ppermute | solution.py:226
  34.7 1.1 %collective-permute-start.15 = (f32[128,256]{1,0:T(8,128)S(1)}, f32[128,256]{1,0:T(8,128)S(1)}, u32[]{:S(2)}, u32[]{:S(2)}) collective-permute-start(f32[128,256]{1,0:T(8,128)S(1)} %add_select_fusion.1), channel_id=1, source_target_pairs={{0,2},{1,5},{2,0},{3,7},{4,6},{5,1},{6,4},{7,3},{8,10},{9,13},{10,... | collective-permute-start | bytes 393224 | tf_op jit(solution)/shard_map/ppermute | solution.py:226
  35.8 2.3 %collective-permute-done.19 = f32[128,256]{1,0:T(8,128)S(1)} collective-permute-done((f32[128,256]{1,0:T(8,128)S(1)}, f32[128,256]{1,0:T(8,128)S(1)}, u32[]{:S(2)}, u32[]{:S(2)}) %collective-permute-start.19) | collective-permute-done | bytes 131104 | tf_op jit(solution)/shard_map/ppermute | solution.py:226
  38.2 1.2 %shard_map.62.part_ref = f32[1024,256]{1,0:T(8,128)S(1)} custom-call(bf16[4,128,128]{2,1,0:T(8,128)(2,1)S(1)} %get-tuple-element.74.oriented_ref, f32[128,256]{1,0:T(8,128)S(1)} %add.53.high_ref, f32[128,256]{1,0:T(8,128)S(1)} %add_select_fusion.2.low_ref, f32[128,256]{1,0:T(8,128)S(1)} %collective-permute-done.17.high_other_ref, ...), custom_call_target="tpu_custom_call" | custom-call | flops 536870912 | bytes 4853760 | tf_op jit(solution)/shard_map/pallas_call | solution.py:25
  41.1 1.2 %shard_map.64 = bf16[1024,256]{1,0:T(8,128)(2,1)} custom-call(bf16[4,128,128]{2,1,0:T(8,128)(2,1)S(1)} %get-tuple-element.74.oriented_ref, f32[128,256]{1,0:T(8,128)S(1)} %collective-permute-done.18.other_ref, bf16[4,1024,128]{2,1,0:T(8,128)(2,1)S(1)} %copy-done, f32[1024,256]{1,0:T(8,128)S(1)} %shard_map.63.part_ref), custom_call_target="tpu_custom_call" | custom-call | flops 67108864 | bytes 2883584 | tf_op jit(solution)/shard_map/pallas_call | solution.py:25
  (48 shorter events, 7.2 us)
Async XLA Ops:
  0.0 2.0 %copy-start = (bf16[4,1024,128]{2,1,0:T(8,128)(2,1)S(1)}, bf16[4,1024,128]{2,1,0:T(8,128)(2,1)}, u32[]{:S(2)}) copy-start(bf16[4,1024,128]{2,1,0:T(8,128)(2,1)} %bases_ref.11) | copy-start | bytes 3145732
  1.5 1.5 %collective-permute-start = (f32[128,256]{1,0:T(8,128)S(1)}, f32[128,256]{1,0:T(8,128)S(1)}, u32[]{:S(2)}, u32[]{:S(2)}) collective-permute-start(f32[128,256]{1,0:T(8,128)S(1)} %get-tuple-element.52), channel_id=1, source_target_pairs={{0,1},{1,0},{2,3},{3,2},{4,5},{5,4},{6,7},{7,6},{8,9},{9,8},{10,11... | collective-permute-start | bytes 393224 | tf_op jit(solution)/shard_map/ppermute | solution.py:226
  2.0 5.4 %copy-start.2 = (bf16[15,128,128]{2,1,0:T(8,128)(2,1)S(1)}, bf16[15,128,128]{2,1,0:T(8,128)(2,1)}, u32[]{:S(2)}) copy-start(bf16[15,128,128]{2,1,0:T(8,128)(2,1)} %couplings_ref.1) | copy-start | bytes 1474564
  2.5 6.7 %collective-permute-start.5 = (f32[128,256]{1,0:T(8,128)S(1)}, f32[128,256]{1,0:T(8,128)S(1)}, u32[]{:S(2)}, u32[]{:S(2)}) collective-permute-start(f32[128,256]{1,0:T(8,128)S(1)} %get-tuple-element.66), channel_id=1, source_target_pairs={{0,1},{1,0},{2,3},{3,2},{4,5},{5,4},{6,7},{7,6},{8,9},{9,8},{10,11... | collective-permute-start | bytes 393224 | tf_op jit(solution)/shard_map/ppermute | solution.py:226
  3.0 6.7 %collective-permute-start.1 = (f32[128,256]{1,0:T(8,128)S(1)}, f32[128,256]{1,0:T(8,128)S(1)}, u32[]{:S(2)}, u32[]{:S(2)}) collective-permute-start(f32[128,256]{1,0:T(8,128)S(1)} %add.47), channel_id=1, source_target_pairs={{0,4},{1,17},{2,6},{3,19},{4,0},{5,21},{6,2},{7,23},{8,12},{9,25},... | collective-permute-start | bytes 393224 | tf_op jit(solution)/shard_map/ppermute | solution.py:226
  6.0 5.0 %collective-permute-start.2 = (f32[128,256]{1,0:T(8,128)S(1)}, f32[128,256]{1,0:T(8,128)S(1)}, u32[]{:S(2)}, u32[]{:S(2)}) collective-permute-start(f32[128,256]{1,0:T(8,128)S(1)} %add.47), channel_id=1, source_target_pairs={{0,2},{1,25},{2,0},{3,27},{4,6},{5,29},{6,4},{7,31},{8,10},{9,17},... | collective-permute-start | bytes 393224 | tf_op jit(solution)/shard_map/ppermute | solution.py:226
  8.1 4.5 %copy-start.1 = (bf16[1024,512]{1,0:T(8,128)(2,1)S(1)}, bf16[1024,512]{1,0:T(8,128)(2,1)}, u32[]{:S(2)}) copy-start(bf16[1024,512]{1,0:T(8,128)(2,1)} %leaves_ref.3) | copy-start | bytes 3145732
  9.1 5.0 %collective-permute-start.6 = (f32[128,256]{1,0:T(8,128)S(1)}, f32[128,256]{1,0:T(8,128)S(1)}, u32[]{:S(2)}, u32[]{:S(2)}) collective-permute-start(f32[128,256]{1,0:T(8,128)S(1)} %add.51), channel_id=1, source_target_pairs={{0,2},{1,5},{2,0},{3,7},{4,6},{5,1},{6,4},{7,3},{8,10},{9,13},{10,... | collective-permute-start | bytes 393224 | tf_op jit(solution)/shard_map/ppermute | solution.py:226
  11.0 5.0 %collective-permute-start.3 = (f32[128,256]{1,0:T(8,128)S(1)}, f32[128,256]{1,0:T(8,128)S(1)}, u32[]{:S(2)}, u32[]{:S(2)}) collective-permute-start(f32[128,256]{1,0:T(8,128)S(1)} %add_select_fusion.5), channel_id=1, source_target_pairs={{0,8},{1,3},{2,10},{3,1},{4,12},{5,7},{6,14},{7,5},{8,0},{9,11},{1... | collective-permute-start | bytes 393224 | tf_op jit(solution)/shard_map/ppermute | solution.py:226
  14.2 5.0 %collective-permute-start.7 = (f32[128,256]{1,0:T(8,128)S(1)}, f32[128,256]{1,0:T(8,128)S(1)}, u32[]{:S(2)}, u32[]{:S(2)}) collective-permute-start(f32[128,256]{1,0:T(8,128)S(1)} %collective-permute-done.6), channel_id=1, source_target_pairs={{0,4},{1,3},{2,6},{3,1},{4,0},{5,7},{6,2},{7,5},{8,12},{9,11},{10,... | collective-permute-start | bytes 393224 | tf_op jit(solution)/shard_map/ppermute | solution.py:226
  14.7 4.6 %collective-permute-start.8 = (f32[512,256]{1,0:T(8,128)S(1)}, f32[512,256]{1,0:T(8,128)S(1)}, u32[]{:S(2)}, u32[]{:S(2)}) collective-permute-start(f32[512,256]{1,0:T(8,128)S(1)} %get-tuple-element.70), channel_id=1, source_target_pairs={{0,1},{1,0},{2,3},{3,2},{4,5},{5,4},{6,7},{7,6},{8,9},{9,8},{10,11... | collective-permute-start | bytes 1572872 | tf_op jit(solution)/shard_map/ppermute | solution.py:226
  16.0 5.0 %collective-permute-start.4 = (f32[128,256]{1,0:T(8,128)S(1)}, f32[128,256]{1,0:T(8,128)S(1)}, u32[]{:S(2)}, u32[]{:S(2)}) collective-permute-start(f32[128,256]{1,0:T(8,128)S(1)} %add_select_fusion.3), channel_id=1, source_target_pairs={{0,2},{1,5},{2,0},{3,7},{4,6},{5,1},{6,4},{7,3},{8,10},{9,13},{10,... | collective-permute-start | bytes 393224 | tf_op jit(solution)/shard_map/ppermute | solution.py:226
  19.2 1.9 %collective-permute-start.9 = (f32[128,256]{1,0:T(8,128)S(1)}, f32[128,256]{1,0:T(8,128)S(1)}, u32[]{:S(2)}, u32[]{:S(2)}) collective-permute-start(f32[128,256]{1,0:T(8,128)S(1)} %add_select_fusion.2.low_ref), channel_id=1, source_target_pairs={{0,1},{1,0},{2,3},{3,2},{4,5},{5,4},{6,7},{7,6},{8,9},{9,8},{10,11... | collective-permute-start | bytes 393224 | tf_op jit(solution)/shard_map/ppermute | solution.py:226
  21.5 1.4 %collective-permute-start.10 = (f32[128,256]{1,0:T(8,128)S(1)}, f32[128,256]{1,0:T(8,128)S(1)}, u32[]{:S(2)}, u32[]{:S(2)}) collective-permute-start(f32[128,256]{1,0:T(8,128)S(1)} %get-tuple-element.80), channel_id=1, source_target_pairs={{0,1},{1,0},{2,3},{3,2},{4,5},{5,4},{6,7},{7,6},{8,9},{9,8},{10,11... | collective-permute-start | bytes 393224 | tf_op jit(solution)/shard_map/ppermute | solution.py:226
  21.6 1.5 %collective-permute-start.11 = (f32[128,256]{1,0:T(8,128)S(1)}, f32[128,256]{1,0:T(8,128)S(1)}, u32[]{:S(2)}, u32[]{:S(2)}) collective-permute-start(f32[128,256]{1,0:T(8,128)S(1)} %get-tuple-element.82), channel_id=1, source_target_pairs={{0,1},{1,0},{2,3},{3,2},{4,5},{5,4},{6,7},{7,6},{8,9},{9,8},{10,11... | collective-permute-start | bytes 393224 | tf_op jit(solution)/shard_map/ppermute | solution.py:226
  23.1 5.0 %collective-permute-start.12 = (f32[128,256]{1,0:T(8,128)S(1)}, f32[128,256]{1,0:T(8,128)S(1)}, u32[]{:S(2)}, u32[]{:S(2)}) collective-permute-start(f32[128,256]{1,0:T(8,128)S(1)} %add.54), channel_id=1, source_target_pairs={{0,4},{1,17},{2,6},{3,19},{4,0},{5,21},{6,2},{7,23},{8,12},{9,25},... | collective-permute-start | bytes 393224 | tf_op jit(solution)/shard_map/ppermute | solution.py:226
  23.9 5.0 %collective-permute-start.13 = (f32[128,256]{1,0:T(8,128)S(1)}, f32[128,256]{1,0:T(8,128)S(1)}, u32[]{:S(2)}, u32[]{:S(2)}) collective-permute-start(f32[128,256]{1,0:T(8,128)S(1)} %add.54), channel_id=1, source_target_pairs={{0,2},{1,25},{2,0},{3,27},{4,6},{5,29},{6,4},{7,31},{8,10},{9,17},... | collective-permute-start | bytes 393224 | tf_op jit(solution)/shard_map/ppermute | solution.py:226
  25.7 5.4 %collective-permute-start.16 = (f32[128,256]{1,0:T(8,128)S(1)}, f32[128,256]{1,0:T(8,128)S(1)}, u32[]{:S(2)}, u32[]{:S(2)}) collective-permute-start(f32[128,256]{1,0:T(8,128)S(1)} %add.55), channel_id=1, source_target_pairs={{0,2},{1,5},{2,0},{3,7},{4,6},{5,1},{6,4},{7,3},{8,10},{9,13},{10,... | collective-permute-start | bytes 393224 | tf_op jit(solution)/shard_map/ppermute | solution.py:226
  28.9 5.7 %collective-permute-start.14 = (f32[128,256]{1,0:T(8,128)S(1)}, f32[128,256]{1,0:T(8,128)S(1)}, u32[]{:S(2)}, u32[]{:S(2)}) collective-permute-start(f32[128,256]{1,0:T(8,128)S(1)} %add_select_fusion.4), channel_id=1, source_target_pairs={{0,8},{1,3},{2,10},{3,1},{4,12},{5,7},{6,14},{7,5},{8,0},{9,11},{1... | collective-permute-start | bytes 393224 | tf_op jit(solution)/shard_map/ppermute | solution.py:226
  31.1 7.0 %collective-permute-start.17 = (f32[128,256]{1,0:T(8,128)S(1)}, f32[128,256]{1,0:T(8,128)S(1)}, u32[]{:S(2)}, u32[]{:S(2)}) collective-permute-start(f32[128,256]{1,0:T(8,128)S(1)} %add.53.high_ref), channel_id=1, source_target_pairs={{0,1},{1,0},{2,3},{3,2},{4,5},{5,4},{6,7},{7,6},{8,9},{9,8},{10,11... | collective-permute-start | bytes 393224 | tf_op jit(solution)/shard_map/ppermute | solution.py:226
  33.1 5.0 %collective-permute-start.19 = (f32[128,256]{1,0:T(8,128)S(1)}, f32[128,256]{1,0:T(8,128)S(1)}, u32[]{:S(2)}, u32[]{:S(2)}) collective-permute-start(f32[128,256]{1,0:T(8,128)S(1)} %collective-permute-done.16), channel_id=1, source_target_pairs={{0,4},{1,3},{2,6},{3,1},{4,0},{5,7},{6,2},{7,5},{8,12},{9,11},{10,... | collective-permute-start | bytes 393224 | tf_op jit(solution)/shard_map/ppermute | solution.py:226
  34.7 5.0 %collective-permute-start.15 = (f32[128,256]{1,0:T(8,128)S(1)}, f32[128,256]{1,0:T(8,128)S(1)}, u32[]{:S(2)}, u32[]{:S(2)}) collective-permute-start(f32[128,256]{1,0:T(8,128)S(1)} %add_select_fusion.1), channel_id=1, source_target_pairs={{0,2},{1,5},{2,0},{3,7},{4,6},{5,1},{6,4},{7,3},{8,10},{9,13},{10,... | collective-permute-start | bytes 393224 | tf_op jit(solution)/shard_map/ppermute | solution.py:226
  38.1 1.9 %collective-permute-start.20 = (f32[128,256]{1,0:T(8,128)S(1)}, f32[128,256]{1,0:T(8,128)S(1)}, u32[]{:S(2)}, u32[]{:S(2)}) collective-permute-start(f32[128,256]{1,0:T(8,128)S(1)} %add_select_fusion.low_ref), channel_id=1, source_target_pairs={{0,1},{1,0},{2,3},{3,2},{4,5},{5,4},{6,7},{7,6},{8,9},{9,8},{10,11... | collective-permute-start | bytes 393224 | tf_op jit(solution)/shard_map/ppermute | solution.py:226
  39.7 1.4 %collective-permute-start.18 = (f32[128,256]{1,0:T(8,128)S(1)}, f32[128,256]{1,0:T(8,128)S(1)}, u32[]{:S(2)}, u32[]{:S(2)}) collective-permute-start(f32[128,256]{1,0:T(8,128)S(1)} %add.59.high_ref), channel_id=1, source_target_pairs={{0,1},{1,0},{2,3},{3,2},{4,5},{5,4},{6,7},{7,6},{8,9},{9,8},{10,11... | collective-permute-start | bytes 393224 | tf_op jit(solution)/shard_map/ppermute | solution.py:226
  (1 other events, 0.7 us)

commit v10 on v9

--- a/solution.py
+++ b/solution.py
@@ -242,9 +242,9 @@
         near, across, *ridden = beside((near, across), *rider_one())
         high = jnp.where(odd, near + across, high + near)
         got = swap(high, far4, far2)
-        low, passenger = beside((swap(low, far3, far4),), ridden.pop() if passenger is None else passenger)
+        passenger = ridden.pop() if passenger is None else passenger
+        low, passenger, *ridden = beside((swap(low, far3, far4),), passenger, *rider_two(*ridden))
         passenger = swap(passenger, 1, 1)
-        got, *ridden = beside((got,), *rider_two(*ridden))
         high = jnp.where(odd, high + got, got)
         low = jnp.where(odd, low + swap(low, far4, far3), low)
         got = swap(high, far3, far4)

time: 42.5 us -> 42.5 us (level)
  no operation moved by 1% of the time
where the time goes in v10:
time: 42.5 us; the launch traced here: 42.3 us
  starting transfers between devices  20.2 us (48%)
  waiting for transfers between devices  13.5 us (32%)
  Pallas kernels  7.87 us (19%)
    ppermute x21, starting transfers between devices, swap(): return lax.ppermute(value, AXIS, pairs)  20.2 us
    ppermute x21, waiting for transfers between devices, swap(): return lax.ppermute(value, AXIS, pairs)  13.5 us
    pallas_call x10, Pallas kernels, call(): pl.pallas_call(kernel, out_shape=outs, in_specs=[arrays_in] * len(arrays)...  7.87 us
  transfers between devices with their start and end apart: 21, of which 13 were waited for; matrix products, arithmetic and copies ran while one was open for 1% of the time, Pallas kernels for 11%

profile of v10, /device:TPU:0, one launch (start us, length us, event | category | flops | bytes accessed | tf_op | source)
XLA Modules:
  0.0 42.3 jit_solution(3630332415229876310)
XLA Ops:
  0.0 1.5 %shard_map.55 = (f32[128,256]{1,0:T(8,128)S(1)}, bf16[1024,256]{1,0:T(8,128)(2,1)S(1)}) custom-call(bf16[4,1024,128]{2,1,0:T(8,128)(2,1)} %bases_ref.11, bf16[1024,256]{1,0:T(8,128)(2,1)} %vec_in.1), custom_call_target="tpu_custom_call" | custom-call | flops 67108864 | bytes 2228224 | tf_op jit(solution)/shard_map/pallas_call | solution.py:25
  3.0 2.9 %collective-permute-start.1 = (f32[128,256]{1,0:T(8,128)S(1)}, f32[128,256]{1,0:T(8,128)S(1)}, u32[]{:S(2)}, u32[]{:S(2)}) collective-permute-start(f32[128,256]{1,0:T(8,128)S(1)} %add.47), channel_id=1, source_target_pairs={{0,4},{1,17},{2,6},{3,19},{4,0},{5,21},{6,2},{7,23},{8,12},{9,25},... | collective-permute-start | bytes 393224 | tf_op jit(solution)/shard_map/ppermute | solution.py:226
  6.0 1.5 %collective-permute-start.2 = (f32[128,256]{1,0:T(8,128)S(1)}, f32[128,256]{1,0:T(8,128)S(1)}, u32[]{:S(2)}, u32[]{:S(2)}) collective-permute-start(f32[128,256]{1,0:T(8,128)S(1)} %add.47), channel_id=1, source_target_pairs={{0,2},{1,25},{2,0},{3,27},{4,6},{5,29},{6,4},{7,31},{8,10},{9,17},... | collective-permute-start | bytes 393224 | tf_op jit(solution)/shard_map/ppermute | solution.py:226
  8.1 1.0 %shard_map.58 = (f32[512,256]{1,0:T(8,128)S(1)}, f32[512,256]{1,0:T(8,128)S(1)}) custom-call(bf16[4,1024,128]{2,1,0:T(8,128)(2,1)S(1)} %copy-done, f32[8,128]{1,0:T(8,128)S(1)} %bitcast.1, bf16[512,1024]{1,0:T(8,128)(2,1)S(1)} %get-tuple-element.69.turned_ref), custom_call_target="tpu_custom_call" | custom-call | flops 536870912 | bytes 3149824 | tf_op jit(solution)/shard_map/pallas_call | solution.py:25
  9.7 1.2 %collective-permute-done.2 = f32[128,256]{1,0:T(8,128)S(1)} collective-permute-done((f32[128,256]{1,0:T(8,128)S(1)}, f32[128,256]{1,0:T(8,128)S(1)}, u32[]{:S(2)}, u32[]{:S(2)}) %collective-permute-start.2) | collective-permute-done | bytes 131104 | tf_op jit(solution)/shard_map/ppermute | solution.py:226
  11.0 1.6 %collective-permute-start.3 = (f32[128,256]{1,0:T(8,128)S(1)}, f32[128,256]{1,0:T(8,128)S(1)}, u32[]{:S(2)}, u32[]{:S(2)}) collective-permute-start(f32[128,256]{1,0:T(8,128)S(1)} %add_select_fusion.5), channel_id=1, source_target_pairs={{0,8},{1,3},{2,10},{3,1},{4,12},{5,7},{6,14},{7,5},{8,0},{9,11},{1... | collective-permute-start | bytes 393224 | tf_op jit(solution)/shard_map/ppermute | solution.py:226
  13.0 1.1 %collective-permute-done.6 = f32[128,256]{1,0:T(8,128)S(1)} collective-permute-done((f32[128,256]{1,0:T(8,128)S(1)}, f32[128,256]{1,0:T(8,128)S(1)}, u32[]{:S(2)}, u32[]{:S(2)}) %collective-permute-start.6) | collective-permute-done | bytes 131104 | tf_op jit(solution)/shard_map/ppermute | solution.py:226
  14.8 1.2 %collective-permute-done.3 = f32[128,256]{1,0:T(8,128)S(1)} collective-permute-done((f32[128,256]{1,0:T(8,128)S(1)}, f32[128,256]{1,0:T(8,128)S(1)}, u32[]{:S(2)}, u32[]{:S(2)}) %collective-permute-start.3) | collective-permute-done | bytes 131104 | tf_op jit(solution)/shard_map/ppermute | solution.py:226
  16.0 1.6 %collective-permute-start.4 = (f32[128,256]{1,0:T(8,128)S(1)}, f32[128,256]{1,0:T(8,128)S(1)}, u32[]{:S(2)}, u32[]{:S(2)}) collective-permute-start(f32[128,256]{1,0:T(8,128)S(1)} %add_select_fusion.3), channel_id=1, source_target_pairs={{0,2},{1,5},{2,0},{3,7},{4,6},{5,1},{6,4},{7,3},{8,10},{9,13},{10,... | collective-permute-start | bytes 393224 | tf_op jit(solution)/shard_map/ppermute | solution.py:226
  17.6 1.6 %collective-permute-done.7 = f32[128,256]{1,0:T(8,128)S(1)} collective-permute-done((f32[128,256]{1,0:T(8,128)S(1)}, f32[128,256]{1,0:T(8,128)S(1)}, u32[]{:S(2)}, u32[]{:S(2)}) %collective-permute-start.7) | collective-permute-done | bytes 131104 | tf_op jit(solution)/shard_map/ppermute | solution.py:226
  19.3 0.8 %shard_map.60 = (f32[512,256]{1,0:T(8,128)S(1)}, bf16[512,256]{1,0:T(8,128)(2,1)S(1)}) custom-call(bf16[4,128,128]{2,1,0:T(8,128)(2,1)S(1)} %get-tuple-element.72.oriented_ref, f32[128,256]{1,0:T(8,128)S(1)} %add_select_fusion.2.low_ref, f32[512,256]{1,0:T(8,128)S(1)} %get-tuple-element.67.keep_ref, f32[512,256]{1,0:T(8,128)S(1)} %collective-permute-done.8.got_ref, ...), custom_call_target="tpu_custom_call" | custom-call | flops 335544320 | bytes 4198400 | tf_op jit(solution)/shard_map/pallas_call | solution.py:25
  20.0 1.0 %collective-permute-done.4 = f32[128,256]{1,0:T(8,128)S(1)} collective-permute-done((f32[128,256]{1,0:T(8,128)S(1)}, f32[128,256]{1,0:T(8,128)S(1)}, u32[]{:S(2)}, u32[]{:S(2)}) %collective-permute-start.4) | collective-permute-done | bytes 131104 | tf_op jit(solution)/shard_map/ppermute | solution.py:226
  22.1 0.8 %collective-permute-done.10 = f32[128,256]{1,0:T(8,128)S(1)} collective-permute-done((f32[128,256]{1,0:T(8,128)S(1)}, f32[128,256]{1,0:T(8,128)S(1)}, u32[]{:S(2)}, u32[]{:S(2)}) %collective-permute-start.10) | collective-permute-done | bytes 131104 | tf_op jit(solution)/shard_map/ppermute | solution.py:226
  23.1 0.8 %collective-permute-start.12 = (f32[128,256]{1,0:T(8,128)S(1)}, f32[128,256]{1,0:T(8,128)S(1)}, u32[]{:S(2)}, u32[]{:S(2)}) collective-permute-start(f32[128,256]{1,0:T(8,128)S(1)} %add.54), channel_id=1, source_target_pairs={{0,4},{1,17},{2,6},{3,19},{4,0},{5,21},{6,2},{7,23},{8,12},{9,25},... | collective-permute-start | bytes 393224 | tf_op jit(solution)/shard_map/ppermute | solution.py:226
  23.9 1.8 %collective-permute-start.13 = (f32[128,256]{1,0:T(8,128)S(1)}, f32[128,256]{1,0:T(8,128)S(1)}, u32[]{:S(2)}, u32[]{:S(2)}) collective-permute-start(f32[128,256]{1,0:T(8,128)S(1)} %add.54), channel_id=1, source_target_pairs={{0,2},{1,25},{2,0},{3,27},{4,6},{5,29},{6,4},{7,31},{8,10},{9,17},... | collective-permute-start | bytes 393224 | tf_op jit(solution)/shard_map/ppermute | solution.py:226
  25.9 2.2 %collective-permute-done.12 = f32[128,256]{1,0:T(8,128)S(1)} collective-permute-done((f32[128,256]{1,0:T(8,128)S(1)}, f32[128,256]{1,0:T(8,128)S(1)}, u32[]{:S(2)}, u32[]{:S(2)}) %collective-permute-start.12) | collective-permute-done | bytes 131104 | tf_op jit(solution)/shard_map/ppermute | solution.py:226
  28.1 0.7 %collective-permute-done.13 = f32[128,256]{1,0:T(8,128)S(1)} collective-permute-done((f32[128,256]{1,0:T(8,128)S(1)}, f32[128,256]{1,0:T(8,128)S(1)}, u32[]{:S(2)}, u32[]{:S(2)}) %collective-permute-start.13) | collective-permute-done | bytes 131104 | tf_op jit(solution)/shard_map/ppermute | solution.py:226
  28.9 2.2 %collective-permute-start.14 = (f32[128,256]{1,0:T(8,128)S(1)}, f32[128,256]{1,0:T(8,128)S(1)}, u32[]{:S(2)}, u32[]{:S(2)}) collective-permute-start(f32[128,256]{1,0:T(8,128)S(1)} %add_select_fusion.4), channel_id=1, source_target_pairs={{0,8},{1,3},{2,10},{3,1},{4,12},{5,7},{6,14},{7,5},{8,0},{9,11},{1... | collective-permute-start | bytes 393224 | tf_op jit(solution)/shard_map/ppermute | solution.py:226
  31.1 2.0 %collective-permute-start.17 = (f32[128,256]{1,0:T(8,128)S(1)}, f32[128,256]{1,0:T(8,128)S(1)}, u32[]{:S(2)}, u32[]{:S(2)}) collective-permute-start(f32[128,256]{1,0:T(8,128)S(1)} %add.53.high_ref), channel_id=1, source_target_pairs={{0,1},{1,0},{2,3},{3,2},{4,5},{5,4},{6,7},{7,6},{8,9},{9,8},{10,11... | collective-permute-start | bytes 393224 | tf_op jit(solution)/shard_map/ppermute | solution.py:226
  33.1 1.5 %collective-permute-start.19 = (f32[128,256]{1,0:T(8,128)S(1)}, f32[128,256]{1,0:T(8,128)S(1)}, u32[]{:S(2)}, u32[]{:S(2)}) collective-permute-start(f32[128,256]{1,0:T(8,128)S(1)} %collective-permute-done.16), channel_id=1, source_target_pairs={{0,4},{1,3},{2,6},{3,1},{4,0},{5,7},{6,2},{7,5},{8,12},{9,11},{10,... | collective-permute-start | bytes 393224 | tf_op jit(solution)/shard_map/ppermute | solution.py:226
  34.7 1.1 %collective-permute-start.15 = (f32[128,256]{1,0:T(8,128)S(1)}, f32[128,256]{1,0:T(8,128)S(1)}, u32[]{:S(2)}, u32[]{:S(2)}) collective-permute-start(f32[128,256]{1,0:T(8,128)S(1)} %add_select_fusion.1), channel_id=1, source_target_pairs={{0,2},{1,5},{2,0},{3,7},{4,6},{5,1},{6,4},{7,3},{8,10},{9,13},{10,... | collective-permute-start | bytes 393224 | tf_op jit(solution)/shard_map/ppermute | solution.py:226
  35.8 2.3 %collective-permute-done.19 = f32[128,256]{1,0:T(8,128)S(1)} collective-permute-done((f32[128,256]{1,0:T(8,128)S(1)}, f32[128,256]{1,0:T(8,128)S(1)}, u32[]{:S(2)}, u32[]{:S(2)}) %collective-permute-start.19) | collective-permute-done | bytes 131104 | tf_op jit(solution)/shard_map/ppermute | solution.py:226
  38.2 1.2 %shard_map.62.part_ref = f32[1024,256]{1,0:T(8,128)S(1)} custom-call(bf16[4,128,128]{2,1,0:T(8,128)(2,1)S(1)} %get-tuple-element.72.oriented_ref, f32[128,256]{1,0:T(8,128)S(1)} %add.53.high_ref, f32[128,256]{1,0:T(8,128)S(1)} %add_select_fusion.2.low_ref, f32[128,256]{1,0:T(8,128)S(1)} %collective-permute-done.17.high_other_ref, ...), custom_call_target="tpu_custom_call" | custom-call | flops 536870912 | bytes 4853760 | tf_op jit(solution)/shard_map/pallas_call | solution.py:25
  41.1 1.2 %shard_map.64 = bf16[1024,256]{1,0:T(8,128)(2,1)} custom-call(bf16[4,128,128]{2,1,0:T(8,128)(2,1)S(1)} %get-tuple-element.72.oriented_ref, f32[128,256]{1,0:T(8,128)S(1)} %collective-permute-done.18.other_ref, bf16[4,1024,128]{2,1,0:T(8,128)(2,1)S(1)} %copy-done, f32[1024,256]{1,0:T(8,128)S(1)} %shard_map.63.part_ref), custom_call_target="tpu_custom_call" | custom-call | flops 67108864 | bytes 2883584 | tf_op jit(solution)/shard_map/pallas_call | solution.py:25
  (48 shorter events, 7.2 us)
Async XLA Ops:
  0.0 2.0 %copy-start = (bf16[4,1024,128]{2,1,0:T(8,128)(2,1)S(1)}, bf16[4,1024,128]{2,1,0:T(8,128)(2,1)}, u32[]{:S(2)}) copy-start(bf16[4,1024,128]{2,1,0:T(8,128)(2,1)} %bases_ref.11) | copy-start | bytes 3145732
  1.5 1.5 %collective-permute-start = (f32[128,256]{1,0:T(8,128)S(1)}, f32[128,256]{1,0:T(8,128)S(1)}, u32[]{:S(2)}, u32[]{:S(2)}) collective-permute-start(f32[128,256]{1,0:T(8,128)S(1)} %get-tuple-element.51), channel_id=1, source_target_pairs={{0,1},{1,0},{2,3},{3,2},{4,5},{5,4},{6,7},{7,6},{8,9},{9,8},{10,11... | collective-permute-start | bytes 393224 | tf_op jit(solution)/shard_map/ppermute | solution.py:226
  2.0 5.4 %copy-start.2 = (bf16[15,128,128]{2,1,0:T(8,128)(2,1)S(1)}, bf16[15,128,128]{2,1,0:T(8,128)(2,1)}, u32[]{:S(2)}) copy-start(bf16[15,128,128]{2,1,0:T(8,128)(2,1)} %couplings_ref.1) | copy-start | bytes 1474564
  2.5 6.7 %collective-permute-start.5 = (f32[128,256]{1,0:T(8,128)S(1)}, f32[128,256]{1,0:T(8,128)S(1)}, u32[]{:S(2)}, u32[]{:S(2)}) collective-permute-start(f32[128,256]{1,0:T(8,128)S(1)} %get-tuple-element.59), channel_id=1, source_target_pairs={{0,1},{1,0},{2,3},{3,2},{4,5},{5,4},{6,7},{7,6},{8,9},{9,8},{10,11... | collective-permute-start | bytes 393224 | tf_op jit(solution)/shard_map/ppermute | solution.py:226
  3.0 6.7 %collective-permute-start.1 = (f32[128,256]{1,0:T(8,128)S(1)}, f32[128,256]{1,0:T(8,128)S(1)}, u32[]{:S(2)}, u32[]{:S(2)}) collective-permute-start(f32[128,256]{1,0:T(8,128)S(1)} %add.47), channel_id=1, source_target_pairs={{0,4},{1,17},{2,6},{3,19},{4,0},{5,21},{6,2},{7,23},{8,12},{9,25},... | collective-permute-start | bytes 393224 | tf_op jit(solution)/shard_map/ppermute | solution.py:226
  6.0 5.0 %collective-permute-start.2 = (f32[128,256]{1,0:T(8,128)S(1)}, f32[128,256]{1,0:T(8,128)S(1)}, u32[]{:S(2)}, u32[]{:S(2)}) collective-permute-start(f32[128,256]{1,0:T(8,128)S(1)} %add.47), channel_id=1, source_target_pairs={{0,2},{1,25},{2,0},{3,27},{4,6},{5,29},{6,4},{7,31},{8,10},{9,17},... | collective-permute-start | bytes 393224 | tf_op jit(solution)/shard_map/ppermute | solution.py:226
  8.1 4.5 %copy-start.1 = (bf16[1024,512]{1,0:T(8,128)(2,1)S(1)}, bf16[1024,512]{1,0:T(8,128)(2,1)}, u32[]{:S(2)}) copy-start(bf16[1024,512]{1,0:T(8,128)(2,1)} %leaves_ref.3) | copy-start | bytes 3145732
  9.1 5.0 %collective-permute-start.6 = (f32[128,256]{1,0:T(8,128)S(1)}, f32[128,256]{1,0:T(8,128)S(1)}, u32[]{:S(2)}, u32[]{:S(2)}) collective-permute-start(f32[128,256]{1,0:T(8,128)S(1)} %add.51), channel_id=1, source_target_pairs={{0,2},{1,5},{2,0},{3,7},{4,6},{5,1},{6,4},{7,3},{8,10},{9,13},{10,... | collective-permute-start | bytes 393224 | tf_op jit(solution)/shard_map/ppermute | solution.py:226
  11.0 5.0 %collective-permute-start.3 = (f32[128,256]{1,0:T(8,128)S(1)}, f32[128,256]{1,0:T(8,128)S(1)}, u32[]{:S(2)}, u32[]{:S(2)}) collective-permute-start(f32[128,256]{1,0:T(8,128)S(1)} %add_select_fusion.5), channel_id=1, source_target_pairs={{0,8},{1,3},{2,10},{3,1},{4,12},{5,7},{6,14},{7,5},{8,0},{9,11},{1... | collective-permute-start | bytes 393224 | tf_op jit(solution)/shard_map/ppermute | solution.py:226
  14.2 5.0 %collective-permute-start.7 = (f32[128,256]{1,0:T(8,128)S(1)}, f32[128,256]{1,0:T(8,128)S(1)}, u32[]{:S(2)}, u32[]{:S(2)}) collective-permute-start(f32[128,256]{1,0:T(8,128)S(1)} %collective-permute-done.6), channel_id=1, source_target_pairs={{0,4},{1,3},{2,6},{3,1},{4,0},{5,7},{6,2},{7,5},{8,12},{9,11},{10,... | collective-permute-start | bytes 393224 | tf_op jit(solution)/shard_map/ppermute | solution.py:226
  14.7 4.6 %collective-permute-start.8 = (f32[512,256]{1,0:T(8,128)S(1)}, f32[512,256]{1,0:T(8,128)S(1)}, u32[]{:S(2)}, u32[]{:S(2)}) collective-permute-start(f32[512,256]{1,0:T(8,128)S(1)} %get-tuple-element.68), channel_id=1, source_target_pairs={{0,1},{1,0},{2,3},{3,2},{4,5},{5,4},{6,7},{7,6},{8,9},{9,8},{10,11... | collective-permute-start | bytes 1572872 | tf_op jit(solution)/shard_map/ppermute | solution.py:226
  16.0 5.0 %collective-permute-start.4 = (f32[128,256]{1,0:T(8,128)S(1)}, f32[128,256]{1,0:T(8,128)S(1)}, u32[]{:S(2)}, u32[]{:S(2)}) collective-permute-start(f32[128,256]{1,0:T(8,128)S(1)} %add_select_fusion.3), channel_id=1, source_target_pairs={{0,2},{1,5},{2,0},{3,7},{4,6},{5,1},{6,4},{7,3},{8,10},{9,13},{10,... | collective-permute-start | bytes 393224 | tf_op jit(solution)/shard_map/ppermute | solution.py:226
  19.2 1.9 %collective-permute-start.9 = (f32[128,256]{1,0:T(8,128)S(1)}, f32[128,256]{1,0:T(8,128)S(1)}, u32[]{:S(2)}, u32[]{:S(2)}) collective-permute-start(f32[128,256]{1,0:T(8,128)S(1)} %add_select_fusion.2.low_ref), channel_id=1, source_target_pairs={{0,1},{1,0},{2,3},{3,2},{4,5},{5,4},{6,7},{7,6},{8,9},{9,8},{10,11... | collective-permute-start | bytes 393224 | tf_op jit(solution)/shard_map/ppermute | solution.py:226
  21.5 1.4 %collective-permute-start.10 = (f32[128,256]{1,0:T(8,128)S(1)}, f32[128,256]{1,0:T(8,128)S(1)}, u32[]{:S(2)}, u32[]{:S(2)}) collective-permute-start(f32[128,256]{1,0:T(8,128)S(1)} %get-tuple-element.78), channel_id=1, source_target_pairs={{0,1},{1,0},{2,3},{3,2},{4,5},{5,4},{6,7},{7,6},{8,9},{9,8},{10,11... | collective-permute-start | bytes 393224 | tf_op jit(solution)/shard_map/ppermute | solution.py:226
  21.6 1.5 %collective-permute-start.11 = (f32[128,256]{1,0:T(8,128)S(1)}, f32[128,256]{1,0:T(8,128)S(1)}, u32[]{:S(2)}, u32[]{:S(2)}) collective-permute-start(f32[128,256]{1,0:T(8,128)S(1)} %get-tuple-element.80), channel_id=1, source_target_pairs={{0,1},{1,0},{2,3},{3,2},{4,5},{5,4},{6,7},{7,6},{8,9},{9,8},{10,11... | collective-permute-start | bytes 393224 | tf_op jit(solution)/shard_map/ppermute | solution.py:226
  23.1 5.0 %collective-permute-start.12 = (f32[128,256]{1,0:T(8,128)S(1)}, f32[128,256]{1,0:T(8,128)S(1)}, u32[]{:S(2)}, u32[]{:S(2)}) collective-permute-start(f32[128,256]{1,0:T(8,128)S(1)} %add.54), channel_id=1, source_target_pairs={{0,4},{1,17},{2,6},{3,19},{4,0},{5,21},{6,2},{7,23},{8,12},{9,25},... | collective-permute-start | bytes 393224 | tf_op jit(solution)/shard_map/ppermute | solution.py:226
  23.9 5.0 %collective-permute-start.13 = (f32[128,256]{1,0:T(8,128)S(1)}, f32[128,256]{1,0:T(8,128)S(1)}, u32[]{:S(2)}, u32[]{:S(2)}) collective-permute-start(f32[128,256]{1,0:T(8,128)S(1)} %add.54), channel_id=1, source_target_pairs={{0,2},{1,25},{2,0},{3,27},{4,6},{5,29},{6,4},{7,31},{8,10},{9,17},... | collective-permute-start | bytes 393224 | tf_op jit(solution)/shard_map/ppermute | solution.py:226
  25.7 5.4 %collective-permute-start.16 = (f32[128,256]{1,0:T(8,128)S(1)}, f32[128,256]{1,0:T(8,128)S(1)}, u32[]{:S(2)}, u32[]{:S(2)}) collective-permute-start(f32[128,256]{1,0:T(8,128)S(1)} %add.55), channel_id=1, source_target_pairs={{0,2},{1,5},{2,0},{3,7},{4,6},{5,1},{6,4},{7,3},{8,10},{9,13},{10,... | collective-permute-start | bytes 393224 | tf_op jit(solution)/shard_map/ppermute | solution.py:226
  28.9 5.7 %collective-permute-start.14 = (f32[128,256]{1,0:T(8,128)S(1)}, f32[128,256]{1,0:T(8,128)S(1)}, u32[]{:S(2)}, u32[]{:S(2)}) collective-permute-start(f32[128,256]{1,0:T(8,128)S(1)} %add_select_fusion.4), channel_id=1, source_target_pairs={{0,8},{1,3},{2,10},{3,1},{4,12},{5,7},{6,14},{7,5},{8,0},{9,11},{1... | collective-permute-start | bytes 393224 | tf_op jit(solution)/shard_map/ppermute | solution.py:226
  31.1 7.0 %collective-permute-start.17 = (f32[128,256]{1,0:T(8,128)S(1)}, f32[128,256]{1,0:T(8,128)S(1)}, u32[]{:S(2)}, u32[]{:S(2)}) collective-permute-start(f32[128,256]{1,0:T(8,128)S(1)} %add.53.high_ref), channel_id=1, source_target_pairs={{0,1},{1,0},{2,3},{3,2},{4,5},{5,4},{6,7},{7,6},{8,9},{9,8},{10,11... | collective-permute-start | bytes 393224 | tf_op jit(solution)/shard_map/ppermute | solution.py:226
  33.1 5.0 %collective-permute-start.19 = (f32[128,256]{1,0:T(8,128)S(1)}, f32[128,256]{1,0:T(8,128)S(1)}, u32[]{:S(2)}, u32[]{:S(2)}) collective-permute-start(f32[128,256]{1,0:T(8,128)S(1)} %collective-permute-done.16), channel_id=1, source_target_pairs={{0,4},{1,3},{2,6},{3,1},{4,0},{5,7},{6,2},{7,5},{8,12},{9,11},{10,... | collective-permute-start | bytes 393224 | tf_op jit(solution)/shard_map/ppermute | solution.py:226
  34.7 5.0 %collective-permute-start.15 = (f32[128,256]{1,0:T(8,128)S(1)}, f32[128,256]{1,0:T(8,128)S(1)}, u32[]{:S(2)}, u32[]{:S(2)}) collective-permute-start(f32[128,256]{1,0:T(8,128)S(1)} %add_select_fusion.1), channel_id=1, source_target_pairs={{0,2},{1,5},{2,0},{3,7},{4,6},{5,1},{6,4},{7,3},{8,10},{9,13},{10,... | collective-permute-start | bytes 393224 | tf_op jit(solution)/shard_map/ppermute | solution.py:226
  38.1 1.9 %collective-permute-start.20 = (f32[128,256]{1,0:T(8,128)S(1)}, f32[128,256]{1,0:T(8,128)S(1)}, u32[]{:S(2)}, u32[]{:S(2)}) collective-permute-start(f32[128,256]{1,0:T(8,128)S(1)} %add_select_fusion.low_ref), channel_id=1, source_target_pairs={{0,1},{1,0},{2,3},{3,2},{4,5},{5,4},{6,7},{7,6},{8,9},{9,8},{10,11... | collective-permute-start | bytes 393224 | tf_op jit(solution)/shard_map/ppermute | solution.py:226
  39.7 1.4 %collective-permute-start.18 = (f32[128,256]{1,0:T(8,128)S(1)}, f32[128,256]{1,0:T(8,128)S(1)}, u32[]{:S(2)}, u32[]{:S(2)}) collective-permute-start(f32[128,256]{1,0:T(8,128)S(1)} %add.59.high_ref), channel_id=1, source_target_pairs={{0,1},{1,0},{2,3},{3,2},{4,5},{5,4},{6,7},{7,6},{8,9},{9,8},{10,11... | collective-permute-start | bytes 393224 | tf_op jit(solution)/shard_map/ppermute | solution.py:226
  (1 other events, 0.7 us)

commit v11 on v9

--- a/solution.py
+++ b/solution.py
@@ -150,13 +150,13 @@
     gram_ref[:, rank:] = rest[:, :rank]
 
 
-def middle_kernel(factors, oriented_ref, high_ref, gram_ref, sums_ref, send_high_ref, send_low_ref, keep_high_ref, keep_low_ref):
+def middle_kernel(factors, oriented_ref, high_ref, gram_ref, sums_ref, send_ref, keep_high_ref, keep_low_ref):
     coeffs = own_coefficients(oriented_ref, 0, high_ref[...], factors)
     delta = jnp.dot(gram_ref[...], jnp.concatenate([coeffs] * 2, axis=0), preferred_element_type=F32)
     proj = sums_ref[...] + delta
     rank = high_ref.shape[0]
-    send_high_ref[...] = proj[:rank]
-    send_low_ref[...] = proj[rank : 2 * rank]
+    send_ref[0] = proj[:rank]
+    send_ref[1] = proj[rank : 2 * rank]
     keep_high_ref[...] = proj[2 * rank : 3 * rank]
     keep_low_ref[...] = proj[3 * rank :]
 
@@ -228,9 +228,9 @@
     def beside(arrays, *riders):
         return lax.optimization_barrier((*arrays, *riders))
 
-    def begin(send_high, send_low, high, low):
-        high = high + swap(send_high, 1, 1)
-        low = low + swap(send_low, 1, 1)
+    def begin(got_high, got_low, high, low):
+        high = high + got_high
+        low = low + got_low
         for bit in range(1, bits - levels):
             high = high + swap(high, 1 << bit, 1 << bit)
             low = low + swap(low, 1 << bit, 1 << bit)
@@ -259,7 +259,7 @@
         arrays_in=HBM,
         scratch=[pltpu.VMEM((rows_dev, rank), BF16), pltpu.SemaphoreType.DMA((2,))],
     )
-    kept = call(kept_kernel, [sums_shape] * 3, [bases, signal], 3 * mults)
+    send_low, *kept = call(kept_kernel, [sums_shape] * 3, [bases, signal], 3 * mults)
 
     def first_riders():
         oriented, turned = call(
@@ -291,16 +291,16 @@
         return oriented, part, sums, gram
 
     high, low, oriented, part, sums, gram = rounds(
-        *begin(send_high, *kept), first_riders, second_riders, third_riders
+        *begin(swap(send_high, 1, 1), swap(send_low, 1, 1), *kept), first_riders, second_riders, third_riders
     )
     high, low_other = beside((high, swap(low, 1, 1)))
-    kept = call(
+    send, *kept = call(
         functools.partial(middle_kernel, factors),
-        [sums_shape] * 4,
+        [pair_shape, sums_shape, sums_shape],
         [oriented, high, gram, sums],
         mults,
     )
-    next_high, next_low, high, low = beside(begin(*kept), high, low)
+    next_high, next_low, high, low = beside(begin(*swap(send, 1, 1), *kept), high, low)
 
     def second_part(_, high_other):
         return call(

time: 42.5 us -> 42.5 us (level)
  starting transfers between devices: 20.2 us -> 19.5 us
  waiting for transfers between devices: 13.5 us -> 14.2 us
    ppermute x21 -> x20, waiting for transfers between devices: 13.5 us -> 14.2 us  [swap(): return lax.ppermute(value, AXIS, pairs)]
    ppermute x21 -> x20, starting transfers between devices: 20.2 us -> 19.5 us  [swap(): return lax.ppermute(value, AXIS, pairs)]
  transfers between devices with their start and end apart: 21 -> 20, of which waited for: 13 -> 12; matrix products, arithmetic and copies ran while one was open for 1% -> 0% of each run, Pallas kernels for 11% -> 11%
where the time goes in v11:
time: 42.5 us; the launch traced here: 42.3 us
  starting transfers between devices  19.5 us (46%)
  waiting for transfers between devices  14.2 us (33%)
  Pallas kernels  7.88 us (19%)
    ppermute x20, starting transfers between devices, swap(): return lax.ppermute(value, AXIS, pairs)  19.5 us
    ppermute x20, waiting for transfers between devices, swap(): return lax.ppermute(value, AXIS, pairs)  14.2 us
    pallas_call x10, Pallas kernels, call(): pl.pallas_call(kernel, out_shape=outs, in_specs=[arrays_in] * len(arrays)...  7.88 us
  transfers between devices with their start and end apart: 20, of which 12 were waited for; matrix products, arithmetic and copies ran while one was open for 0% of the time, Pallas kernels for 11%

profile of v11, /device:TPU:0, one launch (start us, length us, event | category | flops | bytes accessed | tf_op | source)
XLA Modules:
  0.0 42.3 jit_solution(3798304142328224103)
XLA Ops:
  0.0 1.5 %shard_map.55 = (f32[128,256]{1,0:T(8,128)S(1)}, bf16[1024,256]{1,0:T(8,128)(2,1)S(1)}) custom-call(bf16[4,1024,128]{2,1,0:T(8,128)(2,1)} %bases_ref.11, bf16[1024,256]{1,0:T(8,128)(2,1)} %vec_in.1), custom_call_target="tpu_custom_call" | custom-call | flops 67108864 | bytes 2228224 | tf_op jit(solution)/shard_map/pallas_call | solution.py:25
  3.0 2.9 %collective-permute-start.1 = (f32[128,256]{1,0:T(8,128)S(1)}, f32[128,256]{1,0:T(8,128)S(1)}, u32[]{:S(2)}, u32[]{:S(2)}) collective-permute-start(f32[128,256]{1,0:T(8,128)S(1)} %add.47), channel_id=1, source_target_pairs={{0,4},{1,17},{2,6},{3,19},{4,0},{5,21},{6,2},{7,23},{8,12},{9,25},... | collective-permute-start | bytes 393224 | tf_op jit(solution)/shard_map/ppermute | solution.py:226
  6.0 1.5 %collective-permute-start.2 = (f32[128,256]{1,0:T(8,128)S(1)}, f32[128,256]{1,0:T(8,128)S(1)}, u32[]{:S(2)}, u32[]{:S(2)}) collective-permute-start(f32[128,256]{1,0:T(8,128)S(1)} %add.47), channel_id=1, source_target_pairs={{0,2},{1,25},{2,0},{3,27},{4,6},{5,29},{6,4},{7,31},{8,10},{9,17},... | collective-permute-start | bytes 393224 | tf_op jit(solution)/shard_map/ppermute | solution.py:226
  8.1 1.0 %shard_map.58 = (f32[512,256]{1,0:T(8,128)S(1)}, f32[512,256]{1,0:T(8,128)S(1)}) custom-call(bf16[4,1024,128]{2,1,0:T(8,128)(2,1)S(1)} %copy-done, f32[8,128]{1,0:T(8,128)S(1)} %bitcast.9, bf16[512,1024]{1,0:T(8,128)(2,1)S(1)} %get-tuple-element.70.turned_ref), custom_call_target="tpu_custom_call" | custom-call | flops 536870912 | bytes 3149824 | tf_op jit(solution)/shard_map/pallas_call | solution.py:25
  9.7 1.2 %collective-permute-done.2 = f32[128,256]{1,0:T(8,128)S(1)} collective-permute-done((f32[128,256]{1,0:T(8,128)S(1)}, f32[128,256]{1,0:T(8,128)S(1)}, u32[]{:S(2)}, u32[]{:S(2)}) %collective-permute-start.2) | collective-permute-done | bytes 131104 | tf_op jit(solution)/shard_map/ppermute | solution.py:226
  11.0 1.6 %collective-permute-start.3 = (f32[128,256]{1,0:T(8,128)S(1)}, f32[128,256]{1,0:T(8,128)S(1)}, u32[]{:S(2)}, u32[]{:S(2)}) collective-permute-start(f32[128,256]{1,0:T(8,128)S(1)} %add_select_fusion.5), channel_id=1, source_target_pairs={{0,8},{1,3},{2,10},{3,1},{4,12},{5,7},{6,14},{7,5},{8,0},{9,11},{1... | collective-permute-start | bytes 393224 | tf_op jit(solution)/shard_map/ppermute | solution.py:226
  13.0 1.1 %collective-permute-done.6 = f32[128,256]{1,0:T(8,128)S(1)} collective-permute-done((f32[128,256]{1,0:T(8,128)S(1)}, f32[128,256]{1,0:T(8,128)S(1)}, u32[]{:S(2)}, u32[]{:S(2)}) %collective-permute-start.6) | collective-permute-done | bytes 131104 | tf_op jit(solution)/shard_map/ppermute | solution.py:226
  14.8 1.2 %collective-permute-done.3 = f32[128,256]{1,0:T(8,128)S(1)} collective-permute-done((f32[128,256]{1,0:T(8,128)S(1)}, f32[128,256]{1,0:T(8,128)S(1)}, u32[]{:S(2)}, u32[]{:S(2)}) %collective-permute-start.3) | collective-permute-done | bytes 131104 | tf_op jit(solution)/shard_map/ppermute | solution.py:226
  16.0 1.6 %collective-permute-start.4 = (f32[128,256]{1,0:T(8,128)S(1)}, f32[128,256]{1,0:T(8,128)S(1)}, u32[]{:S(2)}, u32[]{:S(2)}) collective-permute-start(f32[128,256]{1,0:T(8,128)S(1)} %add_select_fusion.3), channel_id=1, source_target_pairs={{0,2},{1,5},{2,0},{3,7},{4,6},{5,1},{6,4},{7,3},{8,10},{9,13},{10,... | collective-permute-start | bytes 393224 | tf_op jit(solution)/shard_map/ppermute | solution.py:226
  17.6 1.6 %collective-permute-done.7 = f32[128,256]{1,0:T(8,128)S(1)} collective-permute-done((f32[128,256]{1,0:T(8,128)S(1)}, f32[128,256]{1,0:T(8,128)S(1)}, u32[]{:S(2)}, u32[]{:S(2)}) %collective-permute-start.7) | collective-permute-done | bytes 131104 | tf_op jit(solution)/shard_map/ppermute | solution.py:226
  19.3 0.8 %shard_map.60 = (f32[512,256]{1,0:T(8,128)S(1)}, bf16[512,256]{1,0:T(8,128)(2,1)S(1)}) custom-call(bf16[4,128,128]{2,1,0:T(8,128)(2,1)S(1)} %get-tuple-element.73.oriented_ref, f32[128,256]{1,0:T(8,128)S(1)} %add_select_fusion.2.low_ref, f32[512,256]{1,0:T(8,128)S(1)} %get-tuple-element.68.keep_ref, f32[512,256]{1,0:T(8,128)S(1)} %collective-permute-done.8.got_ref, ...), custom_call_target="tpu_custom_call" | custom-call | flops 335544320 | bytes 4198400 | tf_op jit(solution)/shard_map/pallas_call | solution.py:25
  20.0 1.0 %collective-permute-done.4 = f32[128,256]{1,0:T(8,128)S(1)} collective-permute-done((f32[128,256]{1,0:T(8,128)S(1)}, f32[128,256]{1,0:T(8,128)S(1)}, u32[]{:S(2)}, u32[]{:S(2)}) %collective-permute-start.4) | collective-permute-done | bytes 131104 | tf_op jit(solution)/shard_map/ppermute | solution.py:226
  21.6 1.5 %collective-permute-done.10 = f32[2,128,256]{2,1,0:T(8,128)S(1)} collective-permute-done((f32[2,128,256]{2,1,0:T(8,128)S(1)}, f32[2,128,256]{2,1,0:T(8,128)S(1)}, u32[]{:S(2)}, u32[]{:S(2)}) %collective-permute-start.10) | collective-permute-done | bytes 262176 | tf_op jit(solution)/shard_map/ppermute | solution.py:226
  23.1 0.7 %collective-permute-start.11 = (f32[128,256]{1,0:T(8,128)S(1)}, f32[128,256]{1,0:T(8,128)S(1)}, u32[]{:S(2)}, u32[]{:S(2)}) collective-permute-start(f32[128,256]{1,0:T(8,128)S(1)} %get-tuple-element.81), channel_id=1, source_target_pairs={{0,4},{1,17},{2,6},{3,19},{4,0},{5,21},{6,2},{7,23},{8,12},{9,25},... | collective-permute-start | bytes 393224 | tf_op jit(solution)/shard_map/ppermute | solution.py:226
  23.8 1.7 %collective-permute-start.12 = (f32[128,256]{1,0:T(8,128)S(1)}, f32[128,256]{1,0:T(8,128)S(1)}, u32[]{:S(2)}, u32[]{:S(2)}) collective-permute-start(f32[128,256]{1,0:T(8,128)S(1)} %get-tuple-element.81), channel_id=1, source_target_pairs={{0,2},{1,25},{2,0},{3,27},{4,6},{5,29},{6,4},{7,31},{8,10},{9,17},... | collective-permute-start | bytes 393224 | tf_op jit(solution)/shard_map/ppermute | solution.py:226
  25.8 2.3 %collective-permute-done.11 = f32[128,256]{1,0:T(8,128)S(1)} collective-permute-done((f32[128,256]{1,0:T(8,128)S(1)}, f32[128,256]{1,0:T(8,128)S(1)}, u32[]{:S(2)}, u32[]{:S(2)}) %collective-permute-start.11) | collective-permute-done | bytes 131104 | tf_op jit(solution)/shard_map/ppermute | solution.py:226
  28.8 2.2 %collective-permute-start.13 = (f32[128,256]{1,0:T(8,128)S(1)}, f32[128,256]{1,0:T(8,128)S(1)}, u32[]{:S(2)}, u32[]{:S(2)}) collective-permute-start(f32[128,256]{1,0:T(8,128)S(1)} %add_select_fusion.4), channel_id=1, source_target_pairs={{0,8},{1,3},{2,10},{3,1},{4,12},{5,7},{6,14},{7,5},{8,0},{9,11},{1... | collective-permute-start | bytes 393224 | tf_op jit(solution)/shard_map/ppermute | solution.py:226
  31.0 2.2 %collective-permute-start.16 = (f32[128,256]{1,0:T(8,128)S(1)}, f32[128,256]{1,0:T(8,128)S(1)}, u32[]{:S(2)}, u32[]{:S(2)}) collective-permute-start(f32[128,256]{1,0:T(8,128)S(1)} %add.53.high_ref), channel_id=1, source_target_pairs={{0,1},{1,0},{2,3},{3,2},{4,5},{5,4},{6,7},{7,6},{8,9},{9,8},{10,11... | collective-permute-start | bytes 393224 | tf_op jit(solution)/shard_map/ppermute | solution.py:226
  33.1 1.5 %collective-permute-start.18 = (f32[128,256]{1,0:T(8,128)S(1)}, f32[128,256]{1,0:T(8,128)S(1)}, u32[]{:S(2)}, u32[]{:S(2)}) collective-permute-start(f32[128,256]{1,0:T(8,128)S(1)} %collective-permute-done.15), channel_id=1, source_target_pairs={{0,4},{1,3},{2,6},{3,1},{4,0},{5,7},{6,2},{7,5},{8,12},{9,11},{10,... | collective-permute-start | bytes 393224 | tf_op jit(solution)/shard_map/ppermute | solution.py:226
  34.7 1.0 %collective-permute-start.14 = (f32[128,256]{1,0:T(8,128)S(1)}, f32[128,256]{1,0:T(8,128)S(1)}, u32[]{:S(2)}, u32[]{:S(2)}) collective-permute-start(f32[128,256]{1,0:T(8,128)S(1)} %add_select_fusion.1), channel_id=1, source_target_pairs={{0,2},{1,5},{2,0},{3,7},{4,6},{5,1},{6,4},{7,3},{8,10},{9,13},{10,... | collective-permute-start | bytes 393224 | tf_op jit(solution)/shard_map/ppermute | solution.py:226
  35.6 2.5 %collective-permute-done.18 = f32[128,256]{1,0:T(8,128)S(1)} collective-permute-done((f32[128,256]{1,0:T(8,128)S(1)}, f32[128,256]{1,0:T(8,128)S(1)}, u32[]{:S(2)}, u32[]{:S(2)}) %collective-permute-start.18) | collective-permute-done | bytes 131104 | tf_op jit(solution)/shard_map/ppermute | solution.py:226
  38.2 1.2 %shard_map.62.part_ref = f32[1024,256]{1,0:T(8,128)S(1)} custom-call(bf16[4,128,128]{2,1,0:T(8,128)(2,1)S(1)} %get-tuple-element.73.oriented_ref, f32[128,256]{1,0:T(8,128)S(1)} %add.53.high_ref, f32[128,256]{1,0:T(8,128)S(1)} %add_select_fusion.2.low_ref, f32[128,256]{1,0:T(8,128)S(1)} %collective-permute-done.16.high_other_ref, ...), custom_call_target="tpu_custom_call" | custom-call | flops 536870912 | bytes 4853760 | tf_op jit(solution)/shard_map/pallas_call | solution.py:25
  40.0 0.6 %shard_map.63.part_ref = f32[1024,256]{1,0:T(8,128)S(1)} custom-call(bf16[4,128,128]{2,1,0:T(8,128)(2,1)S(1)} %get-tuple-element.73.oriented_ref, f32[128,256]{1,0:T(8,128)S(1)} %add.59.high_ref, f32[128,256]{1,0:T(8,128)S(1)} %add_select_fusion.low_ref, f32[128,256]{1,0:T(8,128)S(1)} %collective-permute-done.19.other_ref, ...), custom_call_target="tpu_custom_call" | custom-call | flops 201326592 | bytes 3670016 | tf_op jit(solution)/shard_map/pallas_call | solution.py:25
  41.1 1.2 %shard_map.64 = bf16[1024,256]{1,0:T(8,128)(2,1)} custom-call(bf16[4,128,128]{2,1,0:T(8,128)(2,1)S(1)} %get-tuple-element.73.oriented_ref, f32[128,256]{1,0:T(8,128)S(1)} %collective-permute-done.17.other_ref, bf16[4,1024,128]{2,1,0:T(8,128)(2,1)S(1)} %copy-done, f32[1024,256]{1,0:T(8,128)S(1)} %shard_map.63.part_ref), custom_call_target="tpu_custom_call" | custom-call | flops 67108864 | bytes 2883584 | tf_op jit(solution)/shard_map/pallas_call | solution.py:25
  (45 shorter events, 6.6 us)
Async XLA Ops:
  0.0 2.0 %copy-start = (bf16[4,1024,128]{2,1,0:T(8,128)(2,1)S(1)}, bf16[4,1024,128]{2,1,0:T(8,128)(2,1)}, u32[]{:S(2)}) copy-start(bf16[4,1024,128]{2,1,0:T(8,128)(2,1)} %bases_ref.11) | copy-start | bytes 3145732
  1.5 1.5 %collective-permute-start = (f32[128,256]{1,0:T(8,128)S(1)}, f32[128,256]{1,0:T(8,128)S(1)}, u32[]{:S(2)}, u32[]{:S(2)}) collective-permute-start(f32[128,256]{1,0:T(8,128)S(1)} %get-tuple-element.51), channel_id=1, source_target_pairs={{0,1},{1,0},{2,3},{3,2},{4,5},{5,4},{6,7},{7,6},{8,9},{9,8},{10,11... | collective-permute-start | bytes 393224 | tf_op jit(solution)/shard_map/ppermute | solution.py:226
  2.0 5.4 %copy-start.2 = (bf16[15,128,128]{2,1,0:T(8,128)(2,1)S(1)}, bf16[15,128,128]{2,1,0:T(8,128)(2,1)}, u32[]{:S(2)}) copy-start(bf16[15,128,128]{2,1,0:T(8,128)(2,1)} %couplings_ref.1) | copy-start | bytes 1474564
  2.5 6.7 %collective-permute-start.5 = (f32[128,256]{1,0:T(8,128)S(1)}, f32[128,256]{1,0:T(8,128)S(1)}, u32[]{:S(2)}, u32[]{:S(2)}) collective-permute-start(f32[128,256]{1,0:T(8,128)S(1)} %get-tuple-element.65), channel_id=1, source_target_pairs={{0,1},{1,0},{2,3},{3,2},{4,5},{5,4},{6,7},{7,6},{8,9},{9,8},{10,11... | collective-permute-start | bytes 393224 | tf_op jit(solution)/shard_map/ppermute | solution.py:226
  3.0 6.7 %collective-permute-start.1 = (f32[128,256]{1,0:T(8,128)S(1)}, f32[128,256]{1,0:T(8,128)S(1)}, u32[]{:S(2)}, u32[]{:S(2)}) collective-permute-start(f32[128,256]{1,0:T(8,128)S(1)} %add.47), channel_id=1, source_target_pairs={{0,4},{1,17},{2,6},{3,19},{4,0},{5,21},{6,2},{7,23},{8,12},{9,25},... | collective-permute-start | bytes 393224 | tf_op jit(solution)/shard_map/ppermute | solution.py:226
  6.0 5.0 %collective-permute-start.2 = (f32[128,256]{1,0:T(8,128)S(1)}, f32[128,256]{1,0:T(8,128)S(1)}, u32[]{:S(2)}, u32[]{:S(2)}) collective-permute-start(f32[128,256]{1,0:T(8,128)S(1)} %add.47), channel_id=1, source_target_pairs={{0,2},{1,25},{2,0},{3,27},{4,6},{5,29},{6,4},{7,31},{8,10},{9,17},... | collective-permute-start | bytes 393224 | tf_op jit(solution)/shard_map/ppermute | solution.py:226
  7.5 0.7 %copy-start.3 = (f32[1024]{0:T(1024)S(1)}, f32[1024]{0:T(1024)}, u32[]{:S(2)}) copy-start(f32[1024]{0:T(1024)} %param.9) | copy-start | bytes 12292
  8.1 4.5 %copy-start.1 = (bf16[1024,512]{1,0:T(8,128)(2,1)S(1)}, bf16[1024,512]{1,0:T(8,128)(2,1)}, u32[]{:S(2)}) copy-start(bf16[1024,512]{1,0:T(8,128)(2,1)} %leaves_ref.3) | copy-start | bytes 3145732
  9.1 5.0 %collective-permute-start.6 = (f32[128,256]{1,0:T(8,128)S(1)}, f32[128,256]{1,0:T(8,128)S(1)}, u32[]{:S(2)}, u32[]{:S(2)}) collective-permute-start(f32[128,256]{1,0:T(8,128)S(1)} %add.51), channel_id=1, source_target_pairs={{0,2},{1,5},{2,0},{3,7},{4,6},{5,1},{6,4},{7,3},{8,10},{9,13},{10,... | collective-permute-start | bytes 393224 | tf_op jit(solution)/shard_map/ppermute | solution.py:226
  11.0 5.0 %collective-permute-start.3 = (f32[128,256]{1,0:T(8,128)S(1)}, f32[128,256]{1,0:T(8,128)S(1)}, u32[]{:S(2)}, u32[]{:S(2)}) collective-permute-start(f32[128,256]{1,0:T(8,128)S(1)} %add_select_fusion.5), channel_id=1, source_target_pairs={{0,8},{1,3},{2,10},{3,1},{4,12},{5,7},{6,14},{7,5},{8,0},{9,11},{1... | collective-permute-start | bytes 393224 | tf_op jit(solution)/shard_map/ppermute | solution.py:226
  14.2 5.0 %collective-permute-start.7 = (f32[128,256]{1,0:T(8,128)S(1)}, f32[128,256]{1,0:T(8,128)S(1)}, u32[]{:S(2)}, u32[]{:S(2)}) collective-permute-start(f32[128,256]{1,0:T(8,128)S(1)} %collective-permute-done.6), channel_id=1, source_target_pairs={{0,4},{1,3},{2,6},{3,1},{4,0},{5,7},{6,2},{7,5},{8,12},{9,11},{10,... | collective-permute-start | bytes 393224 | tf_op jit(solution)/shard_map/ppermute | solution.py:226
  14.7 4.6 %collective-permute-start.8 = (f32[512,256]{1,0:T(8,128)S(1)}, f32[512,256]{1,0:T(8,128)S(1)}, u32[]{:S(2)}, u32[]{:S(2)}) collective-permute-start(f32[512,256]{1,0:T(8,128)S(1)} %get-tuple-element.69), channel_id=1, source_target_pairs={{0,1},{1,0},{2,3},{3,2},{4,5},{5,4},{6,7},{7,6},{8,9},{9,8},{10,11... | collective-permute-start | bytes 1572872 | tf_op jit(solution)/shard_map/ppermute | solution.py:226
  16.0 5.0 %collective-permute-start.4 = (f32[128,256]{1,0:T(8,128)S(1)}, f32[128,256]{1,0:T(8,128)S(1)}, u32[]{:S(2)}, u32[]{:S(2)}) collective-permute-start(f32[128,256]{1,0:T(8,128)S(1)} %add_select_fusion.3), channel_id=1, source_target_pairs={{0,2},{1,5},{2,0},{3,7},{4,6},{5,1},{6,4},{7,3},{8,10},{9,13},{10,... | collective-permute-start | bytes 393224 | tf_op jit(solution)/shard_map/ppermute | solution.py:226
  19.2 1.9 %collective-permute-start.9 = (f32[128,256]{1,0:T(8,128)S(1)}, f32[128,256]{1,0:T(8,128)S(1)}, u32[]{:S(2)}, u32[]{:S(2)}) collective-permute-start(f32[128,256]{1,0:T(8,128)S(1)} %add_select_fusion.2.low_ref), channel_id=1, source_target_pairs={{0,1},{1,0},{2,3},{3,2},{4,5},{5,4},{6,7},{7,6},{8,9},{9,8},{10,11... | collective-permute-start | bytes 393224 | tf_op jit(solution)/shard_map/ppermute | solution.py:226
  21.5 1.6 %collective-permute-start.10 = (f32[2,128,256]{2,1,0:T(8,128)S(1)}, f32[2,128,256]{2,1,0:T(8,128)S(1)}, u32[]{:S(2)}, u32[]{:S(2)}) collective-permute-start(f32[2,128,256]{2,1,0:T(8,128)S(1)} %get-tuple-element.79), channel_id=1, source_target_pairs={{0,1},{1,0},{2,3},{3,2},{4,5},{5,4},{6,7},{7,6},{8,9},{9,8},{10,11... | collective-permute-start | bytes 786440 | tf_op jit(solution)/shard_map/ppermute | solution.py:226
  23.1 5.0 %collective-permute-start.11 = (f32[128,256]{1,0:T(8,128)S(1)}, f32[128,256]{1,0:T(8,128)S(1)}, u32[]{:S(2)}, u32[]{:S(2)}) collective-permute-start(f32[128,256]{1,0:T(8,128)S(1)} %get-tuple-element.81), channel_id=1, source_target_pairs={{0,4},{1,17},{2,6},{3,19},{4,0},{5,21},{6,2},{7,23},{8,12},{9,25},... | collective-permute-start | bytes 393224 | tf_op jit(solution)/shard_map/ppermute | solution.py:226
  23.8 5.0 %collective-permute-start.12 = (f32[128,256]{1,0:T(8,128)S(1)}, f32[128,256]{1,0:T(8,128)S(1)}, u32[]{:S(2)}, u32[]{:S(2)}) collective-permute-start(f32[128,256]{1,0:T(8,128)S(1)} %get-tuple-element.81), channel_id=1, source_target_pairs={{0,2},{1,25},{2,0},{3,27},{4,6},{5,29},{6,4},{7,31},{8,10},{9,17},... | collective-permute-start | bytes 393224 | tf_op jit(solution)/shard_map/ppermute | solution.py:226
  25.5 5.4 %collective-permute-start.15 = (f32[128,256]{1,0:T(8,128)S(1)}, f32[128,256]{1,0:T(8,128)S(1)}, u32[]{:S(2)}, u32[]{:S(2)}) collective-permute-start(f32[128,256]{1,0:T(8,128)S(1)} %get-tuple-element.86), channel_id=1, source_target_pairs={{0,2},{1,5},{2,0},{3,7},{4,6},{5,1},{6,4},{7,3},{8,10},{9,13},{10,... | collective-permute-start | bytes 393224 | tf_op jit(solution)/shard_map/ppermute | solution.py:226
  28.8 5.9 %collective-permute-start.13 = (f32[128,256]{1,0:T(8,128)S(1)}, f32[128,256]{1,0:T(8,128)S(1)}, u32[]{:S(2)}, u32[]{:S(2)}) collective-permute-start(f32[128,256]{1,0:T(8,128)S(1)} %add_select_fusion.4), channel_id=1, source_target_pairs={{0,8},{1,3},{2,10},{3,1},{4,12},{5,7},{6,14},{7,5},{8,0},{9,11},{1... | collective-permute-start | bytes 393224 | tf_op jit(solution)/shard_map/ppermute | solution.py:226
  31.0 7.2 %collective-permute-start.16 = (f32[128,256]{1,0:T(8,128)S(1)}, f32[128,256]{1,0:T(8,128)S(1)}, u32[]{:S(2)}, u32[]{:S(2)}) collective-permute-start(f32[128,256]{1,0:T(8,128)S(1)} %add.53.high_ref), channel_id=1, source_target_pairs={{0,1},{1,0},{2,3},{3,2},{4,5},{5,4},{6,7},{7,6},{8,9},{9,8},{10,11... | collective-permute-start | bytes 393224 | tf_op jit(solution)/shard_map/ppermute | solution.py:226
  33.1 5.0 %collective-permute-start.18 = (f32[128,256]{1,0:T(8,128)S(1)}, f32[128,256]{1,0:T(8,128)S(1)}, u32[]{:S(2)}, u32[]{:S(2)}) collective-permute-start(f32[128,256]{1,0:T(8,128)S(1)} %collective-permute-done.15), channel_id=1, source_target_pairs={{0,4},{1,3},{2,6},{3,1},{4,0},{5,7},{6,2},{7,5},{8,12},{9,11},{10,... | collective-permute-start | bytes 393224 | tf_op jit(solution)/shard_map/ppermute | solution.py:226
  34.7 5.0 %collective-permute-start.14 = (f32[128,256]{1,0:T(8,128)S(1)}, f32[128,256]{1,0:T(8,128)S(1)}, u32[]{:S(2)}, u32[]{:S(2)}) collective-permute-start(f32[128,256]{1,0:T(8,128)S(1)} %add_select_fusion.1), channel_id=1, source_target_pairs={{0,2},{1,5},{2,0},{3,7},{4,6},{5,1},{6,4},{7,3},{8,10},{9,13},{10,... | collective-permute-start | bytes 393224 | tf_op jit(solution)/shard_map/ppermute | solution.py:226
  38.1 1.9 %collective-permute-start.19 = (f32[128,256]{1,0:T(8,128)S(1)}, f32[128,256]{1,0:T(8,128)S(1)}, u32[]{:S(2)}, u32[]{:S(2)}) collective-permute-start(f32[128,256]{1,0:T(8,128)S(1)} %add_select_fusion.low_ref), channel_id=1, source_target_pairs={{0,1},{1,0},{2,3},{3,2},{4,5},{5,4},{6,7},{7,6},{8,9},{9,8},{10,11... | collective-permute-start | bytes 393224 | tf_op jit(solution)/shard_map/ppermute | solution.py:226
  39.7 1.4 %collective-permute-start.17 = (f32[128,256]{1,0:T(8,128)S(1)}, f32[128,256]{1,0:T(8,128)S(1)}, u32[]{:S(2)}, u32[]{:S(2)}) collective-permute-start(f32[128,256]{1,0:T(8,128)S(1)} %add.59.high_ref), channel_id=1, source_target_pairs={{0,1},{1,0},{2,3},{3,2},{4,5},{5,4},{6,7},{7,6},{8,9},{9,8},{10,11... | collective-permute-start | bytes 393224 | tf_op jit(solution)/shard_map/ppermute | solution.py:226
